TPU v7x, 512 devices: a whole 4x4x16 slice. The times are simulated.
512 devices in a mesh: blk: 64 (over y_lo, z, core), along: 8 (over x, y_hi).
Axes of the slice: x: 4, y: 4 (y_hi: 2, y_lo: 2; y = y_hi * 2 + y_lo), z: 16, core: 2. Of those that a mesh axis runs over, the one named last changes fastest.
Arguments:
- values: float32 [3, 64, 192, 256], P(None, 'blk', 'along'), may hold values from -6 to 6
- offsets: float32 [3, 64, 192, 256], P(None, 'blk', 'along'), may hold values from 0 to 1
- stiffness: float32 [64, 192, 256], P('blk', 'along'), may hold values from 0.5 to 2
- leaf_basis: float32 [64, 192, 64, 256], P('blk', 'along'), may hold values from -0.375 to 0.375
- transfer: float32 [64, 192, 64, 64], P('blk', 'along'), may hold values from -0.15625 to 0.15625
- slab_transfer_matrices: float32 [64, 8, 64, 64], P('blk', 'along'), may hold values from -0.25 to 0.25
- leaf_coupling_matrices: float32 [64, 30, 64, 64], P('blk'), may hold values from -0.375 to 0.375
- leaf_admissible_mask: int32 [64, 30], P('blk'), may hold values 0 or 1
- top_coupling: float32 [64, 64, 64, 64], P('blk'), may hold values from -0.75 to 0.75
- top_admissible: int32 [64, 64], P('blk'), may hold values 0 or 1
Outputs:
- product: float32 [3, 64, 192, 256], P(None, 'blk', 'along')
All inputs are finite; a program needn't handle non-finite values. No bound on the sum of `leaf_admissible_mask` or of `top_admissible` on one device may be relied on, other than what follows from the above.
Results may differ from a plain program's by a relative error of at most 0.0001.
Values sent between devices are 32-bit elements; how exact they have to be, the bound alone decides.
No kernel may reach another device: no remote copies, remote signals or barrier semaphores. Data moves between devices by JAX's collectives and lax.ppermute only.
A program may use at most 64 MiB of HBM per device.

v0:
```python
import jax
import jax.numpy as jnp
from jax import lax
from jax.sharding import PartitionSpec as P

REACH = 6


SHARPNESS = 2.0
KERNEL_SCALE = 0.125
HIGHEST_ACCURACY = lax.Precision.HIGHEST


def with_halo(cells, sides, width, closed):
    for axis, dim in sides:
        count = lax.axis_size(axis)
        ends = count if closed else count - 1
        head = lax.slice_in_dim(cells, 0, width, axis=dim)
        tail = lax.slice_in_dim(cells, cells.shape[dim] - width, cells.shape[dim], axis=dim)
        cells = jnp.concatenate(
            [
                lax.ppermute(tail, axis, [(i, (i + 1) % count) for i in range(ends)]),
                cells,
                lax.ppermute(head, axis, [((i + 1) % count, i) for i in range(ends)]),
            ],
            axis=dim,
        )
    return cells


def passed_along(x, axis, by):
    count = lax.axis_size(axis)
    return lax.ppermute(x, axis, [(i, (i + by) % count) for i in range(count)])


def from_everyone(x, axis):
    count = lax.axis_size(axis)
    return lax.all_to_all(jnp.broadcast_to(x[None], (count, *x.shape)), axis, 0, 0, tiled=True)


def taken_together(x, axis):
    return from_everyone(x, axis).sum(axis=0)


def in_order(tiles, dim):
    tiles = jnp.moveaxis(tiles, 0, dim)
    shape = tiles.shape
    return tiles.reshape(*shape[:dim], shape[dim] * shape[dim + 1], *shape[dim + 2 :])


def gathered_copies(x, axis, dim):
    tiles = from_everyone(x, axis)
    return in_order(tiles, dim)


def near_field(padded):
    leaves = padded.shape[2] - 2
    center = padded[:, 1:2, 1 : 1 + leaves]
    result = jnp.zeros((3, 1, leaves, padded.shape[3]), jnp.float32)
    for around in (-1, 0, 1):
        for along_step in (-1, 0, 1):
            source = padded[:, 1 + around : 2 + around, 1 + along_step : 1 + along_step + leaves]
            gap_around = around + source[0][..., None, :] - center[0][..., :, None]
            gap_along = along_step + source[1][..., None, :] - center[1][..., :, None]
            gap_radial = source[2][..., None, :] - center[2][..., :, None]
            squared = gap_around * gap_around + gap_along * gap_along + gap_radial * gap_radial
            kernel = (
                KERNEL_SCALE
                * center[3][..., :, None]
                * source[3][..., None, :]
                * jnp.exp(-SHARPNESS * squared)
            )
            result = result + jnp.einsum(
                "alij,ralj->rali", kernel, source[4:], precision=HIGHEST_ACCURACY
            )
    return result


def slot_number(around, along_step, reach):
    block = around - 2 if around > 0 else reach - 1 + (-around - 2)
    return 3 * block + along_step + 1


def add_sector(total, held, around, leaf_coupling_matrices, leaf_admissible_mask):
    leaves = total.shape[2]
    for along_step in (-1, 0, 1):
        slot = slot_number(around, along_step, REACH)
        partner = held[:, :, 1 + along_step : 1 + along_step + leaves]
        coupling = (
            leaf_coupling_matrices[:, slot]
            * leaf_admissible_mask[:, slot].astype(jnp.float32)[:, None, None]
        )
        total = total + jnp.einsum("skq,rslq->rslk", coupling, partner, precision=HIGHEST_ACCURACY)
    return total


def body(
    values,
    offsets,
    stiffness,
    leaf_basis,
    transfer,
    slab_transfer_matrices,
    leaf_coupling_matrices,
    leaf_admissible_mask,
    top_coupling,
    top_admissible,
):
    stacked = jnp.concatenate([offsets, stiffness[None], values], 0)
    padded = with_halo(stacked, (("blk", 1), ("along", 2)), 1, True)
    at_start = lax.axis_index("along") == 0
    at_finish = lax.axis_index("along") == lax.axis_size("along") - 1
    lower_rim = jnp.where(at_start, 0.0, padded[:, :, :1])
    upper_rim = jnp.where(at_finish, 0.0, padded[:, :, -1:])
    padded = jnp.concatenate([lower_rim, padded[:, :, 1:-1], upper_rim], 2)
    near = near_field(padded)
    coefs = jnp.einsum("slki,rsli->rslk", leaf_basis, values, precision=HIGHEST_ACCURACY)
    rimmed = with_halo(coefs, (("along", 2),), 1, False)
    far_leaf = jnp.zeros(coefs.shape, jnp.float32)
    sectors = lax.axis_size("blk")
    lower_window = rimmed
    upper_window = rimmed
    breadth = 1
    while breadth <= REACH:
        lower_came = passed_along(lower_window, "blk", breadth)
        upper_came = passed_along(upper_window, "blk", -breadth)
        lower_window = jnp.concatenate([lower_window, lower_came], 1)
        upper_window = jnp.concatenate([upper_window, upper_came], 1)
        breadth = 2 * breadth
    for distance in range(2, REACH + 1):
        far_leaf = add_sector(
            far_leaf,
            lower_window[:, distance : distance + 1],
            -distance,
            leaf_coupling_matrices,
            leaf_admissible_mask,
        )
        far_leaf = add_sector(
            far_leaf,
            upper_window[:, distance : distance + 1],
            distance,
            leaf_coupling_matrices,
            leaf_admissible_mask,
        )
    slab_coefficient_rows = jnp.einsum(
        "slqk,rslq->rsk", transfer, coefs, precision=HIGHEST_ACCURACY
    )
    shared_portion = jnp.einsum(
        "oxz,eox->eoz",
        slab_transfer_matrices[:, 0],
        slab_coefficient_rows,
        precision=HIGHEST_ACCURACY,
    )
    sector_coefs = taken_together(shared_portion, "along")
    every_sector = gathered_copies(sector_coefs, "blk", 1)
    sector = lax.axis_index("blk")
    others = jnp.arange(sectors, dtype=jnp.int32)
    apart = (others - sector) % sectors
    distant = jnp.logical_and(apart > REACH, apart < sectors - REACH).astype(jnp.float32)
    allowed = top_admissible[0].astype(jnp.float32) * distant
    sector_local_coefs = jnp.einsum(
        "stkq,rtq->rsk",
        top_coupling * allowed[None, :, None, None],
        every_sector,
        precision=HIGHEST_ACCURACY,
    )
    slab_local_coefs = jnp.einsum(
        "baz,lbz->lba", slab_transfer_matrices[:, 0], sector_local_coefs, precision=HIGHEST_ACCURACY
    )
    leaf_down = jnp.einsum("slqk,rsk->rslq", transfer, slab_local_coefs, precision=HIGHEST_ACCURACY)
    leaf_local = far_leaf + leaf_down
    return near + jnp.einsum("slki,rslk->rsli", leaf_basis, leaf_local, precision=HIGHEST_ACCURACY)


def solution(mesh):
    return jax.shard_map(
        body,
        mesh=mesh,
        in_specs=(
            P(None, "blk", "along", None),
            P(None, "blk", "along", None),
            P("blk", "along", None),
            P("blk", "along", None, None),
            P("blk", "along", None, None),
            P("blk", "along", None, None),
            P("blk", None, None, None),
            P("blk", None),
            P("blk", None, None, None),
            P("blk", None),
        ),
        out_specs=P(None, "blk", "along", None),
        check_vma=False,
    )
```

profile of v0, /device:TPU:1, one launch (start us, length us, event | category | flops | bytes accessed | tf_op | source)
XLA Modules:
  0.0 229.0 jit_solution(18158832542448089966)
XLA Ops:
  0.1 1.1 copy.139
  1.1 0.8 broadcast_in_dim.12
  1.9 0.9 copy.138
  3.6 8.8 %collective-permute-start.1 = (f32[7,1,24,256]{3,0,2,1:T(8,128)}, f32[7,1,24,256]{3,0,2,1:T(8,128)S(1)}, u32[]{:S(2)}, u32[]{:S(2)}) collective-permute-start(f32[7,1,24,256]{3,0,2,1:T(8,128)} %pad_maximum_fusion.4), channel_id=1, source_target_pairs={{8,0},{16,8},{24,16},{32,24},{40,32},{48,40},{56,48},{64,56},{72,6... | collective-permute-start | bytes 516104 | tf_op jit(solution)/shard_map/ppermute | solution.py:24
  12.3 1.9 collective-permute-start
  14.3 2.3 fusion.203
  16.5 1.3 collective-permute-start.5
  17.8 5.5 %collective-permute-start.4 = (f32[3,1,1,64]{3,0,2,1:T(4,128)S(1)}, f32[3,1,1,64]{3,0,2,1:T(4,128)S(1)}, u32[]{:S(2)}, u32[]{:S(2)}) collective-permute-start(f32[3,1,1,64]{3,0,2,1:T(4,128)S(1)} %get-tuple-element.78), channel_id=1, source_target_pairs={{0,1},{1,2},{2,3},{3,4},{4,5},{5,6},{6,7},{8,9},{9,10},{10,11},{11... | collective-permute-start | bytes 2312 | tf_op jit(solution)/shard_map/ppermute | solution.py:22
  25.8 3.7 %all-to-all-start = ((f32[8,1,192]{2,1,0:T(1,128)}), f32[8,1,192]{2,1,0:T(1,128)S(1)}, u32[]{:S(2)}, u32[]{:S(2)}) async-start(f32[8,1,192]{2,1,0:T(1,128)} %reshape.1052), calls=%async_computation | async-start | bytes 16384 | tf_op jit(solution)/shard_map/all_to_all | solution.py:38
  31.4 3.2 %collective-permute-start.6 = (f32[3,1,26,64]{3,0,2,1:T(4,128)S(1)}, f32[3,1,26,64]{3,0,2,1:T(4,128)S(1)}, u32[]{:S(2)}, u32[]{:S(2)}) collective-permute-start(f32[3,1,26,64]{3,0,2,1:T(4,128)S(1)} %pad_maximum_fusion.8), channel_id=1, source_target_pairs={{0,8},{8,16},{16,24},{24,32},{32,40},{40,48},{48,56},{56,64},{64,7... | collective-permute-start | bytes 59912 | tf_op jit(solution)/shard_map/ppermute | solution.py:33
  34.7 9.6 %collective-permute-start.8 = (f32[3,1,26,64]{3,0,2,1:T(4,128)S(1)}, f32[3,1,26,64]{3,0,2,1:T(4,128)S(1)}, u32[]{:S(2)}, u32[]{:S(2)}) collective-permute-start(f32[3,1,26,64]{3,0,2,1:T(4,128)S(1)} %pad_maximum_fusion.8), channel_id=1, source_target_pairs={{0,504},{8,0},{16,8},{24,16},{32,24},{40,32},{48,40},{56,48},{64,5... | collective-permute-start | bytes 59912 | tf_op jit(solution)/shard_map/ppermute | solution.py:33
  44.3 0.7 fusion.472
  45.8 1.9 collective-permute-start.7
  47.8 10.1 %collective-permute-start.9 = (f32[3,2,26,64]{3,0,2,1:T(4,128)}, f32[3,2,26,64]{3,0,2,1:T(4,128)S(1)}, u32[]{:S(2)}, u32[]{:S(2)}) collective-permute-start(f32[3,2,26,64]{3,0,2,1:T(4,128)} %get-tuple-element.77), channel_id=1, source_target_pairs={{0,496},{8,504},{16,0},{24,8},{32,16},{40,24},{48,32},{56,40},{64,... | collective-permute-start | bytes 119816 | tf_op jit(solution)/shard_map/ppermute | solution.py:33
  78.1 0.9 reduce.3
  78.9 0.8 reshape.1054
  79.7 5.4 %all-to-all-start.1 = ((f32[64,1,192]{2,1,0:T(1,128)}), f32[64,1,192]{2,1,0:T(1,128)S(1)}, u32[]{:S(2)}, u32[]{:S(2)}) async-start(f32[64,1,192]{2,1,0:T(1,128)} %reshape.1054), calls=%async_computation.1 | async-start | bytes 131072 | tf_op jit(solution)/shard_map/all_to_all | solution.py:38
  85.1 1.0 pad_maximum_fusion.1
  86.2 6.6 %collective-permute-start.11 = (f32[3,4,26,64]{3,0,2,1:T(4,128)S(1)}, f32[3,4,26,64]{3,0,2,1:T(4,128)S(1)}, u32[]{:S(2)}, u32[]{:S(2)}) collective-permute-start(f32[3,4,26,64]{3,0,2,1:T(4,128)S(1)} %get-tuple-element.75), channel_id=1, source_target_pairs={{0,480},{8,488},{16,496},{24,504},{32,0},{40,8},{48,16},{56,24},{6... | collective-permute-start | bytes 239624 | tf_op jit(solution)/shard_map/ppermute | solution.py:33
  92.8 1.9 collective-permute-start.10
  94.7 1.0 fusion.315
  95.7 1.0 fusion.317
  96.7 1.0 fusion.319
  98.4 0.8 fusion.327
  99.2 0.8 fusion.329
  100.0 0.8 fusion.331
  100.9 0.8 fusion.333
  101.7 0.8 fusion.335
  102.6 0.8 fusion.279
  103.4 0.8 fusion.281
  104.2 0.8 fusion.283
  105.1 1.8 collective-permute-done.10
  106.9 0.8 fusion.285
  107.8 0.8 fusion.287
  108.6 0.8 fusion.289
  109.4 0.8 fusion.291
  110.2 0.8 fusion.293
  111.1 0.8 fusion.295
  111.9 0.8 fusion.297
  112.7 0.8 fusion.299
  113.5 0.8 fusion.301
  114.4 0.8 fusion.303
  115.2 0.8 fusion.305
  116.0 0.8 fusion.307
  116.8 0.8 fusion.309
  117.7 0.8 fusion.311
  118.5 7.9 %collective-permute-start.3 = (f32[7,3,1,256]{3,0,2,1:T(8,128)S(1)}, f32[7,3,1,256]{3,0,2,1:T(8,128)S(1)}, u32[]{:S(2)}, u32[]{:S(2)}) collective-permute-start(f32[7,3,1,256]{3,0,2,1:T(8,128)S(1)} %get-tuple-element.32), channel_id=1, source_target_pairs={{1,0},{2,1},{3,2},{4,3},{5,4},{6,5},{7,6},{0,7},{9,8},{10,9},{11,1... | collective-permute-start | bytes 64520 | tf_op jit(solution)/shard_map/ppermute | solution.py:24
  126.4 0.8 fusion.313
  127.2 2.1 collective-permute-start.2
  129.6 5.8 %collective-permute-done.2 = f32[7,3,1,256]{3,0,2,1:T(8,128)S(1)} collective-permute-done((f32[7,3,1,256]{3,0,2,1:T(8,128)S(1)}, f32[7,3,1,256]{3,0,2,1:T(8,128)S(1)}, u32[]{:S(2)}, u32[]{:S(2)}) %collective-permute-start.2) | collective-permute-done | bytes 21536 | tf_op jit(solution)/shard_map/ppermute | solution.py:22
  136.8 9.0 %fusion = f32[24,3,256]{2,1,0:T(4,128)S(1)} fusion(f32[24,256]{1,0:T(8,128)S(1)} %get-tuple-element.110, f32[24,256]{1,0:T(8,128)S(1)} %get-tuple-element.111, f32[24,256]{1,0:T(8,128)S(1)} %get-tuple-element.112, f32[24,256]{1,0:T(8,128)S(1)} %get-tuple-element.113, f32[24,256]{1,0:T(8,128)S(1)} %copy-done.28, f32[24,256]{1,0:T(8,128)S(1)} %copy-done.29, ...), kind=kOutput, calls=%fused_computation | convolution fusion | flops 73924608 | bytes 368640 | tf_op jit(solution)/shard_map/alij,ralj->rali/dot_general | solution.py:73
  145.8 9.1 %fusion.39 = f32[24,3,256]{2,1,0:T(4,128)S(1)} fusion(f32[24,256]{1,0:T(8,128)S(1)} %get-tuple-element.122, f32[24,256]{1,0:T(8,128)S(1)} %get-tuple-element.123, f32[24,256]{1,0:T(8,128)S(1)} %get-tuple-element.124, f32[24,256]{1,0:T(8,128)S(1)} %get-tuple-element.125, f32[24,256]{1,0:T(8,128)S(1)} %copy-done.28, f32[24,256]{1,0:T(8,128)S(1)} %copy-done.29, ...), kind=kOutput, calls=%fused_computation.39 | convolution fusion | flops 73924608 | bytes 368640 | tf_op jit(solution)/shard_map/alij,ralj->rali/dot_general | solution.py:73
  154.9 9.1 %fusion.26 = f32[24,3,256]{2,1,0:T(4,128)S(1)} fusion(f32[24,256]{1,0:T(8,128)S(1)} %get-tuple-element.114, f32[24,256]{1,0:T(8,128)S(1)} %get-tuple-element.115, f32[24,256]{1,0:T(8,128)S(1)} %get-tuple-element.118, f32[24,256]{1,0:T(8,128)S(1)} %get-tuple-element.119, f32[24,256]{1,0:T(8,128)S(1)} %copy-done.28, f32[24,256]{1,0:T(8,128)S(1)} %copy-done.29, ...), kind=kOutput, calls=%fused_computation.26 | convolution fusion | flops 73924608 | bytes 368640 | tf_op jit(solution)/shard_map/alij,ralj->rali/dot_general | solution.py:73
  164.0 9.1 %fusion.65 = f32[24,3,256]{2,1,0:T(4,128)S(1)} fusion(f32[24,256]{1,0:T(8,128)S(1)} %get-tuple-element.126, f32[24,256]{1,0:T(8,128)S(1)} %get-tuple-element.127, f32[24,256]{1,0:T(8,128)S(1)} %get-tuple-element.130, f32[24,256]{1,0:T(8,128)S(1)} %get-tuple-element.131, f32[24,256]{1,0:T(8,128)S(1)} %copy-done.28, f32[24,256]{1,0:T(8,128)S(1)} %copy-done.29, ...), kind=kOutput, calls=%fused_computation.65 | convolution fusion | flops 73924608 | bytes 368640 | tf_op jit(solution)/shard_map/alij,ralj->rali/dot_general | solution.py:73
  173.0 9.1 %fusion.78 = f32[24,3,256]{2,1,0:T(4,128)S(1)} fusion(f32[24,256]{1,0:T(8,128)S(1)} %get-tuple-element.134, f32[24,256]{1,0:T(8,128)S(1)} %get-tuple-element.135, f32[24,256]{1,0:T(8,128)S(1)} %get-tuple-element.136, f32[24,256]{1,0:T(8,128)S(1)} %get-tuple-element.137, f32[24,256]{1,0:T(8,128)S(1)} %copy-done.28, f32[24,256]{1,0:T(8,128)S(1)} %copy-done.29, ...), kind=kOutput, calls=%fused_computation.78 | convolution fusion | flops 73924608 | bytes 368640 | tf_op jit(solution)/shard_map/alij,ralj->rali/dot_general | solution.py:73
  182.1 9.1 %fusion.104 = f32[24,3,256]{2,1,0:T(4,128)S(1)} fusion(f32[24,256]{1,0:T(8,128)S(1)} %copy-done.28, f32[24,256]{1,0:T(8,128)S(1)} %get-tuple-element.133, f32[24,256]{1,0:T(8,128)S(1)} %copy-done.29, f32[24,256]{1,0:T(8,128)S(1)} %get-tuple-element.129, f32[24,256]{1,0:T(8,128)S(1)} %copy-done.27, f32[24,256]{1,0:T(8,128)S(1)} %get-tuple-element.121, ...), kind=kOutput, calls=%fused_computation.104 | convolution fusion | flops 73924608 | bytes 368640 | tf_op jit(solution)/shard_map/alij,ralj->rali/dot_general | solution.py:73
  191.2 9.1 %fusion.229 = f32[24,3,256]{2,1,0:T(4,128)S(1)} fusion(f32[24,3,256]{2,1,0:T(4,128)S(1)} %fusion.65, f32[24,3,256]{2,1,0:T(4,128)S(1)} %fusion.78, f32[24,3,256]{2,1,0:T(4,128)S(1)} %fusion.104, f32[24,256]{1,0:T(8,128)S(1)} %get-tuple-element.116, f32[24,256]{1,0:T(8,128)S(1)} %get-tuple-element.120, f32[24,256]{1,0:T(8,128)S(1)} %get-tuple-element.128, ...), kind=kOutput, calls=%fused_computation.213 | convolution fusion | flops 73979904 | bytes 663552 | tf_op jit(solution)/shard_map/alij,ralj->rali/dot_general | solution.py:73
  200.3 9.4 %fusion.220 = f32[24,3,256]{2,1,0:T(4,128)S(1)} fusion(f32[24,3,256]{2,1,0:T(4,128)S(1)} %fusion.26, f32[24,3,256]{2,1,0:T(4,128)S(1)} %fusion.39, f32[24,3,256]{2,1,0:T(4,128)S(1)} %fusion.229, f32[24,256]{1,0:T(8,128)S(1)} %copy-done.28, f32[24,256]{1,0:T(8,128)S(1)} %copy-done.29, f32[24,256]{1,0:T(8,128)S(1)} %copy-done.27, ...), kind=kOutput, calls=%fused_computation.210 | convolution fusion | flops 73979904 | bytes 491520 | tf_op jit(solution)/shard_map/alij,ralj->rali/dot_general | solution.py:73
  209.7 9.7 %fusion.235 = f32[24,3,256]{2,1,0:T(4,128)} fusion(f32[24,3,256]{2,1,0:T(4,128)S(1)} %fusion, f32[24,3,256]{2,1,0:T(4,128)S(1)} %fusion.220, f32[24,256]{1,0:T(8,128)S(1)} %get-tuple-element.138, f32[24,256]{1,0:T(8,128)S(1)} %get-tuple-element.139, f32[24,256]{1,0:T(8,128)S(1)} %get-tuple-element.140, f32[24,256]{1,0:T(8,128)S(1)} %get-tuple-element.141, ...), kind=kOutput, calls=%fused_computation.215 | convolution fusion | flops 73961472 | bytes 565248 | tf_op jit(solution)/shard_map/alij,ralj->rali/dot_general | solution.py:73
  219.6 0.9 reduce.4
  220.6 3.4 %fusion.267 = f32[3,64]{1,0:T(4,128)S(1)} fusion(f32[1,64,64,64]{3,2,1,0:T(8,128)} %param.18, f32[64]{0:T(128)S(1)} %copy-done.32, f32[3,64,64]{2,1,0:T(8,128)S(1)} %bitcast.400), kind=kOutput, calls=%fused_computation.246 | convolution fusion | flops 9699328 | bytes 1098752 | tf_op jit(solution)/shard_map/stkq,rtq->rsk/dot_general | solution.py:161
  224.1 1.9 fusion.271
  226.3 1.2 fusion.266
  227.5 0.9 fusion.208
  (137 shorter events, 10.7 us)
Async XLA Ops:
  0.0 14.3 %copy-start = (f32[1,24,64,256]{3,2,1,0:T(8,128)S(1)}, f32[1,24,64,256]{3,2,1,0:T(8,128)}, u32[]{:S(2)}) copy-start(f32[1,24,64,256]{3,2,1,0:T(8,128)} %param.13) | copy-start | bytes 4718596
  0.0 30.2 %copy-start.25 = (f32[1,24,256]{2,1,0:T(8,128)S(1)}, f32[1,24,256]{2,1,0:T(8,128)}, u32[]{:S(2)}) copy-start(f32[1,24,256]{2,1,0:T(8,128)} %param.12) | copy-start | bytes 73732
  0.0 29.5 %copy-start.5 = (f32[3,1,24,256]{3,2,1,0:T(8,128)S(1)}, f32[3,1,24,256]{3,2,1,0:T(8,128)}, u32[]{:S(2)}) copy-start(f32[3,1,24,256]{3,2,1,0:T(8,128)} %param.11) | copy-start | bytes 221188
  0.0 23.3 %copy-start.1 = (f32[1,24,64,64]{3,2,1,0:T(8,128)S(1)}, f32[1,24,64,64]{3,2,1,0:T(8,128)}, u32[]{:S(2)}) copy-start(f32[1,24,64,64]{3,2,1,0:T(8,128)} %param.14) | copy-start | bytes 1179652
  0.0 23.8 %copy-start.23 = (f32[1,1,64,64]{3,2,1,0:T(8,128)S(1)}, f32[1,1,64,64]{3,2,1,0:T(8,128)}, u32[]{:S(2)}) copy-start(f32[1,1,64,64]{3,2,1,0:T(8,128)} %param.15) | copy-start | bytes 49156
  0.0 30.8 %copy-start.33 = (s32[1,64]{1,0:T(1,128)S(1)}, s32[1,64]{1,0:T(1,128)}, u32[]{:S(2)}) copy-start(s32[1,64]{1,0:T(1,128)} %param.19) | copy-start | bytes 772
  0.0 44.2 %copy-start.3 = (s32[1,30]{1,0:T(1,128)S(1)}, s32[1,30]{1,0:T(1,128)}, u32[]{:S(2)}) copy-start(s32[1,30]{1,0:T(1,128)} %param.17) | copy-start | bytes 364
  3.6 114.9 %collective-permute-start.1 = (f32[7,1,24,256]{3,0,2,1:T(8,128)}, f32[7,1,24,256]{3,0,2,1:T(8,128)S(1)}, u32[]{:S(2)}, u32[]{:S(2)}) collective-permute-start(f32[7,1,24,256]{3,0,2,1:T(8,128)} %pad_maximum_fusion.4), channel_id=1, source_target_pairs={{8,0},{16,8},{24,16},{32,24},{40,32},{48,40},{56,48},{64,56},{72,6... | collective-permute-start | bytes 516104 | tf_op jit(solution)/shard_map/ppermute | solution.py:24
  12.3 106.1 %collective-permute-start = (f32[7,1,24,256]{3,0,2,1:T(8,128)}, f32[7,1,24,256]{3,0,2,1:T(8,128)S(1)}, u32[]{:S(2)}, u32[]{:S(2)}) collective-permute-start(f32[7,1,24,256]{3,0,2,1:T(8,128)} %pad_maximum_fusion.4), channel_id=1, source_target_pairs={{0,8},{8,16},{16,24},{24,32},{32,40},{40,48},{48,56},{56,64},{64,7... | collective-permute-start | bytes 516104 | tf_op jit(solution)/shard_map/ppermute | solution.py:22
  16.5 14.8 %collective-permute-start.5 = (f32[3,1,1,64]{3,0,2,1:T(4,128)S(1)}, f32[3,1,1,64]{3,0,2,1:T(4,128)S(1)}, u32[]{:S(2)}, u32[]{:S(2)}) collective-permute-start(f32[3,1,1,64]{3,0,2,1:T(4,128)S(1)} %get-tuple-element.79), channel_id=1, source_target_pairs={{1,0},{2,1},{3,2},{4,3},{5,4},{6,5},{7,6},{9,8},{10,9},{11,10},{12... | collective-permute-start | bytes 2312 | tf_op jit(solution)/shard_map/ppermute | solution.py:24
  17.8 13.6 %collective-permute-start.4 = (f32[3,1,1,64]{3,0,2,1:T(4,128)S(1)}, f32[3,1,1,64]{3,0,2,1:T(4,128)S(1)}, u32[]{:S(2)}, u32[]{:S(2)}) collective-permute-start(f32[3,1,1,64]{3,0,2,1:T(4,128)S(1)} %get-tuple-element.78), channel_id=1, source_target_pairs={{0,1},{1,2},{2,3},{3,4},{4,5},{5,6},{6,7},{8,9},{9,10},{10,11},{11... | collective-permute-start | bytes 2312 | tf_op jit(solution)/shard_map/ppermute | solution.py:22
  25.8 51.5 %all-to-all-start = ((f32[8,1,192]{2,1,0:T(1,128)}), f32[8,1,192]{2,1,0:T(1,128)S(1)}, u32[]{:S(2)}, u32[]{:S(2)}) async-start(f32[8,1,192]{2,1,0:T(1,128)} %reshape.1052), calls=%async_computation | async-start | bytes 16384 | tf_op jit(solution)/shard_map/all_to_all | solution.py:38
  31.4 16.4 %copy-start.31 = (f32[3,1,1,64]{3,0,2,1:T(4,128)}, f32[3,1,1,64]{3,0,2,1:T(4,128)S(1)}, u32[]{:S(2)}) copy-start(f32[3,1,1,64]{3,0,2,1:T(4,128)S(1)} %collective-permute-done.4) | copy-start | bytes 2308
  31.4 13.6 %collective-permute-start.6 = (f32[3,1,26,64]{3,0,2,1:T(4,128)S(1)}, f32[3,1,26,64]{3,0,2,1:T(4,128)S(1)}, u32[]{:S(2)}, u32[]{:S(2)}) collective-permute-start(f32[3,1,26,64]{3,0,2,1:T(4,128)S(1)} %pad_maximum_fusion.8), channel_id=1, source_target_pairs={{0,8},{8,16},{16,24},{24,32},{32,40},{40,48},{48,56},{56,64},{64,7... | collective-permute-start | bytes 59912 | tf_op jit(solution)/shard_map/ppermute | solution.py:33
  34.7 10.4 %collective-permute-start.8 = (f32[3,1,26,64]{3,0,2,1:T(4,128)S(1)}, f32[3,1,26,64]{3,0,2,1:T(4,128)S(1)}, u32[]{:S(2)}, u32[]{:S(2)}) collective-permute-start(f32[3,1,26,64]{3,0,2,1:T(4,128)S(1)} %pad_maximum_fusion.8), channel_id=1, source_target_pairs={{0,504},{8,0},{16,8},{24,16},{32,24},{40,32},{48,40},{56,48},{64,5... | collective-permute-start | bytes 59912 | tf_op jit(solution)/shard_map/ppermute | solution.py:33
  45.1 0.7 copy-start.6
  45.8 39.3 %collective-permute-start.7 = (f32[3,2,26,64]{3,0,2,1:T(4,128)}, f32[3,2,26,64]{3,0,2,1:T(4,128)S(1)}, u32[]{:S(2)}, u32[]{:S(2)}) collective-permute-start(f32[3,2,26,64]{3,0,2,1:T(4,128)} %get-tuple-element.76), channel_id=1, source_target_pairs={{0,16},{8,24},{16,32},{24,40},{32,48},{40,56},{48,64},{56,72},{64,... | collective-permute-start | bytes 119816 | tf_op jit(solution)/shard_map/ppermute | solution.py:33
  47.8 37.4 %collective-permute-start.9 = (f32[3,2,26,64]{3,0,2,1:T(4,128)}, f32[3,2,26,64]{3,0,2,1:T(4,128)S(1)}, u32[]{:S(2)}, u32[]{:S(2)}) collective-permute-start(f32[3,2,26,64]{3,0,2,1:T(4,128)} %get-tuple-element.77), channel_id=1, source_target_pairs={{0,496},{8,504},{16,0},{24,8},{32,16},{40,24},{48,32},{56,40},{64,... | collective-permute-start | bytes 119816 | tf_op jit(solution)/shard_map/ppermute | solution.py:33
  79.7 139.9 %all-to-all-start.1 = ((f32[64,1,192]{2,1,0:T(1,128)}), f32[64,1,192]{2,1,0:T(1,128)S(1)}, u32[]{:S(2)}, u32[]{:S(2)}) async-start(f32[64,1,192]{2,1,0:T(1,128)} %reshape.1054), calls=%async_computation.1 | async-start | bytes 131072 | tf_op jit(solution)/shard_map/all_to_all | solution.py:38
  85.1 12.6 %copy-start.2 = (f32[1,30,64,64]{3,2,1,0:T(8,128)S(1)}, f32[1,30,64,64]{3,2,1,0:T(8,128)}, u32[]{:S(2)}) copy-start(f32[1,30,64,64]{3,2,1,0:T(8,128)} %param.16) | copy-start | bytes 1474564
  86.2 16.4 %collective-permute-start.11 = (f32[3,4,26,64]{3,0,2,1:T(4,128)S(1)}, f32[3,4,26,64]{3,0,2,1:T(4,128)S(1)}, u32[]{:S(2)}, u32[]{:S(2)}) collective-permute-start(f32[3,4,26,64]{3,0,2,1:T(4,128)S(1)} %get-tuple-element.75), channel_id=1, source_target_pairs={{0,480},{8,488},{16,496},{24,504},{32,0},{40,8},{48,16},{56,24},{6... | collective-permute-start | bytes 239624 | tf_op jit(solution)/shard_map/ppermute | solution.py:33
  92.8 14.1 %collective-permute-start.10 = (f32[3,4,26,64]{3,0,2,1:T(4,128)S(1)}, f32[3,4,26,64]{3,0,2,1:T(4,128)S(1)}, u32[]{:S(2)}, u32[]{:S(2)}) collective-permute-start(f32[3,4,26,64]{3,0,2,1:T(4,128)S(1)} %get-tuple-element.74), channel_id=1, source_target_pairs={{0,32},{8,40},{16,48},{24,56},{32,64},{40,72},{48,80},{56,88},{64,... | collective-permute-start | bytes 239624 | tf_op jit(solution)/shard_map/ppermute | solution.py:33
  118.5 10.8 %collective-permute-start.3 = (f32[7,3,1,256]{3,0,2,1:T(8,128)S(1)}, f32[7,3,1,256]{3,0,2,1:T(8,128)S(1)}, u32[]{:S(2)}, u32[]{:S(2)}) collective-permute-start(f32[7,3,1,256]{3,0,2,1:T(8,128)S(1)} %get-tuple-element.32), channel_id=1, source_target_pairs={{1,0},{2,1},{3,2},{4,3},{5,4},{6,5},{7,6},{0,7},{9,8},{10,9},{11,1... | collective-permute-start | bytes 64520 | tf_op jit(solution)/shard_map/ppermute | solution.py:24
  127.2 8.2 %collective-permute-start.2 = (f32[7,3,1,256]{3,0,2,1:T(8,128)S(1)}, f32[7,3,1,256]{3,0,2,1:T(8,128)S(1)}, u32[]{:S(2)}, u32[]{:S(2)}) collective-permute-start(f32[7,3,1,256]{3,0,2,1:T(8,128)S(1)} %get-tuple-element.31), channel_id=1, source_target_pairs={{0,1},{1,2},{2,3},{3,4},{4,5},{5,6},{6,7},{7,0},{8,9},{9,10},{10,1... | collective-permute-start | bytes 64520 | tf_op jit(solution)/shard_map/ppermute | solution.py:22
  136.0 0.7 copy-start.27
  136.0 0.7 copy-start.28
  136.0 0.8 copy-start.29
  136.0 0.8 copy-start.30
  191.1 9.1 %copy-start.4 = (f32[3,1,24,256]{3,2,1,0:T(8,128)S(1)}, f32[3,1,24,256]{3,2,1,0:T(8,128)}, u32[]{:S(2)}) copy-start(f32[3,1,24,256]{3,2,1,0:T(8,128)} %param.10) | copy-start | bytes 221188
  191.1 9.1 %copy-start.26 = (f32[1,24,256]{2,1,0:T(8,128)S(1)}, f32[1,24,256]{2,1,0:T(8,128)}, u32[]{:S(2)}) copy-start(f32[1,24,256]{2,1,0:T(8,128)} %param.12) | copy-start | bytes 73732
  209.7 10.8 %copy-start.32 = (f32[64]{0:T(128)S(1)}, f32[64]{0:T(128)}, u32[]{:S(2)}) copy-start(f32[64]{0:T(128)} %and_select_fusion) | copy-start | bytes 772
  219.4 6.7 %copy-start.7 = (f32[3,24,64]{2,1,0:T(8,128)S(1)}, f32[3,24,64]{2,1,0:T(8,128)}, u32[]{:S(2)}) copy-start(f32[3,24,64]{2,1,0:T(8,128)} %fusion.327) | copy-start | bytes 55300
  219.4 6.7 %copy-start.8 = (f32[3,24,64]{2,1,0:T(8,128)S(1)}, f32[3,24,64]{2,1,0:T(8,128)}, u32[]{:S(2)}) copy-start(f32[3,24,64]{2,1,0:T(8,128)} %fusion.329) | copy-start | bytes 55300
  219.4 6.7 %copy-start.9 = (f32[3,24,64]{2,1,0:T(8,128)S(1)}, f32[3,24,64]{2,1,0:T(8,128)}, u32[]{:S(2)}) copy-start(f32[3,24,64]{2,1,0:T(8,128)} %fusion.331) | copy-start | bytes 55300
  219.4 6.7 %copy-start.10 = (f32[3,24,64]{2,1,0:T(8,128)S(1)}, f32[3,24,64]{2,1,0:T(8,128)}, u32[]{:S(2)}) copy-start(f32[3,24,64]{2,1,0:T(8,128)} %fusion.333) | copy-start | bytes 55300
  219.4 6.7 %copy-start.11 = (f32[3,24,64]{2,1,0:T(8,128)S(1)}, f32[3,24,64]{2,1,0:T(8,128)}, u32[]{:S(2)}) copy-start(f32[3,24,64]{2,1,0:T(8,128)} %fusion.335) | copy-start | bytes 55300
  219.5 6.7 %copy-start.12 = (f32[3,24,64]{2,1,0:T(8,128)S(1)}, f32[3,24,64]{2,1,0:T(8,128)}, u32[]{:S(2)}) copy-start(f32[3,24,64]{2,1,0:T(8,128)} %fusion.279) | copy-start | bytes 55300
  219.5 6.7 %copy-start.13 = (f32[3,24,64]{2,1,0:T(8,128)S(1)}, f32[3,24,64]{2,1,0:T(8,128)}, u32[]{:S(2)}) copy-start(f32[3,24,64]{2,1,0:T(8,128)} %fusion.281) | copy-start | bytes 55300
  219.5 6.7 %copy-start.14 = (f32[3,24,64]{2,1,0:T(8,128)S(1)}, f32[3,24,64]{2,1,0:T(8,128)}, u32[]{:S(2)}) copy-start(f32[3,24,64]{2,1,0:T(8,128)} %fusion.283) | copy-start | bytes 55300
  219.5 6.7 %copy-start.15 = (f32[3,24,64]{2,1,0:T(8,128)S(1)}, f32[3,24,64]{2,1,0:T(8,128)}, u32[]{:S(2)}) copy-start(f32[3,24,64]{2,1,0:T(8,128)} %fusion.285) | copy-start | bytes 55300
  219.5 6.7 %copy-start.16 = (f32[3,24,64]{2,1,0:T(8,128)S(1)}, f32[3,24,64]{2,1,0:T(8,128)}, u32[]{:S(2)}) copy-start(f32[3,24,64]{2,1,0:T(8,128)} %fusion.287) | copy-start | bytes 55300
  219.5 6.7 %copy-start.17 = (f32[3,24,64]{2,1,0:T(8,128)S(1)}, f32[3,24,64]{2,1,0:T(8,128)}, u32[]{:S(2)}) copy-start(f32[3,24,64]{2,1,0:T(8,128)} %fusion.289) | copy-start | bytes 55300
  219.5 6.7 %copy-start.18 = (f32[3,24,64]{2,1,0:T(8,128)S(1)}, f32[3,24,64]{2,1,0:T(8,128)}, u32[]{:S(2)}) copy-start(f32[3,24,64]{2,1,0:T(8,128)} %fusion.291) | copy-start | bytes 55300
  219.5 6.7 %copy-start.19 = (f32[3,24,64]{2,1,0:T(8,128)S(1)}, f32[3,24,64]{2,1,0:T(8,128)}, u32[]{:S(2)}) copy-start(f32[3,24,64]{2,1,0:T(8,128)} %fusion.293) | copy-start | bytes 55300
  219.5 6.7 %copy-start.20 = (f32[3,24,64]{2,1,0:T(8,128)S(1)}, f32[3,24,64]{2,1,0:T(8,128)}, u32[]{:S(2)}) copy-start(f32[3,24,64]{2,1,0:T(8,128)} %fusion.295) | copy-start | bytes 55300
  219.5 6.7 %copy-start.21 = (f32[3,24,64]{2,1,0:T(8,128)S(1)}, f32[3,24,64]{2,1,0:T(8,128)}, u32[]{:S(2)}) copy-start(f32[3,24,64]{2,1,0:T(8,128)} %fusion.297) | copy-start | bytes 55300
  219.6 6.7 %copy-start.22 = (f32[3,24,64]{2,1,0:T(8,128)S(1)}, f32[3,24,64]{2,1,0:T(8,128)}, u32[]{:S(2)}) copy-start(f32[3,24,64]{2,1,0:T(8,128)} %fusion.299) | copy-start | bytes 55300
  220.6 6.9 %copy-start.24 = (f32[24,3,256]{2,1,0:T(4,128)S(1)}, f32[24,3,256]{2,1,0:T(4,128)}, u32[]{:S(2)}) copy-start(f32[24,3,256]{2,1,0:T(4,128)} %fusion.235) | copy-start | bytes 221188
where the time goes:
time: 232 us; the launch traced here: 229 us
  matrix products  116 us (50%)
  starting transfers between devices  69.9 us (30%)
  between operations  19.5 us (8%)
  local copies, waits for them, and re-layouts  8.29 us (4%)
  other arithmetic  7.84 us (3%)
  waiting for transfers between devices  7.76 us (3%)
    dot_general x9, matrix products, near_field(): jnp.einsum('alij,ralj->rali', kernel, source[4:], precision=HIGHEST_ACCUR...  82.6 us
    ppermute x6, starting transfers between devices, passed_along(): return lax.ppermute(x, axis, [(i, (i + by) % count) for i in range(count)])  33.4 us
    dot_general x30, matrix products, add_sector(): jnp.einsum('skq,rslq->rslk', coupling, partner, precision=HIGHEST_ACCURACY)  23.7 us
    ppermute x3, starting transfers between devices, with_halo(): lax.ppermute(head, axis, [((i + 1) % count, i) for i in range(ends)])  17.9 us
    ppermute x3, starting transfers between devices, with_halo(): lax.ppermute(tail, axis, [(i, (i + 1) % count) for i in range(ends)])  9.5 us
    all_to_all x2, starting transfers between devices, from_everyone(): lax.all_to_all(jnp.broadcast_to(x[None], (count, *x.shape)), axis, 0, 0,...  9.16 us
    ppermute x3, waiting for transfers between devices, with_halo(): lax.ppermute(tail, axis, [(i, (i + 1) % count) for i in range(ends)])  5.82 us
  transfers between devices with their start and end apart: 14, of which 3 were waited for; matrix products, arithmetic and copies ran while one was open for 52% of the time, Pallas kernels for 0%

commit v1 on v0

v1 whole, which is shorter than its diff:
```python
import functools
import math

import jax
import jax.numpy as jnp
from jax import lax
from jax.experimental import pallas as pl
from jax.experimental.pallas import tpu as pltpu
from jax.sharding import PartitionSpec as P

REACH = 6
LEAF = 256
RANK = 64
RHS = 3
LD = 24
TALL = LD + 2
ROWS = 32
SHARPNESS = 2.0
KERNEL_SCALE = 0.125
LOG2E = math.log2(math.e)
F32 = jnp.float32
BF16 = jnp.bfloat16
EXACT = lax.Precision.HIGHEST
VMEM = pl.BlockSpec(memory_space=pltpu.VMEM)
SMEM = pl.BlockSpec(memory_space=pltpu.SMEM)
BY_LAST = (((1,), (1,)), ((), ()))
MIB = 2**20


def call(kernel, outs, ins, scratch=(), flops=0, vmem=48):
    return pl.pallas_call(
        kernel,
        out_shape=outs,
        in_specs=ins,
        out_specs=jax.tree.map(lambda _: VMEM, outs),
        scratch_shapes=list(scratch),
        compiler_params=pltpu.CompilerParams(vmem_limit_bytes=vmem * MIB),
        cost_estimate=pl.CostEstimate(flops=flops, bytes_accessed=1 << 20, transcendentals=0),
    )


def shaped(*shape):
    return jax.ShapeDtypeStruct(shape, F32)


def halves(x):
    high = x.astype(BF16).astype(F32)
    return high, x - high


def upward_kernel(at_ref, values_ref, offsets_ref, stiffness_ref, basis_ref, transfer_ref, slab_ref, wire_ref, slots_ref):
    lane = lax.broadcasted_iota(jnp.int32, (RANK, 128), 1)

    def leaf(l, carry):
        sums, columns = carry
        row = pl.ds(l, 1)
        new_sums = []
        for r in range(3):
            wire_ref[l, r : r + 1, :] = offsets_ref[r, row, :] - 0.5
            wire_ref[l, 4 + r : 5 + r, :] = values_ref[r, row, :]
        wire_ref[l, 3:4, :] = stiffness_ref[row, :]
        basis = basis_ref[l]
        transfer = transfer_ref[l]
        for r in range(3):
            column = jnp.sum(basis * values_ref[r, row, :], axis=1, keepdims=True)
            new_sums.append(sums[r] + transfer * column)
            columns = jnp.where(lane == r * ROWS + l, column, columns)
        return tuple(new_sums), columns

    nothing = jnp.zeros((RANK, RANK), F32)
    sums, columns = lax.fori_loop(
        0, LD, leaf, ((nothing,) * 3, jnp.zeros((RANK, 128), F32)), unroll=4
    )
    rows = jnp.transpose(columns, (1, 0))
    coefs = jnp.concatenate(
        [rows[:LD], rows[ROWS : ROWS + LD], rows[2 * ROWS : 2 * ROWS + LD], jnp.zeros((LD, RANK), F32)], 1
    )
    for l in range(LD):
        wire_ref[l, 7:8, :] = coefs[l : l + 1]
    slab_rows = jnp.concatenate(
        [jnp.sum(s, axis=0, keepdims=True) for s in sums] + [jnp.zeros((5, RANK), F32)], 0
    )
    share = jnp.dot(slab_rows, slab_ref[...], precision=EXACT, preferred_element_type=F32)
    share = jnp.concatenate([share, jnp.zeros((8, 128 - RANK), F32)], 1)
    here = at_ref[0]
    for j in range(8):
        slots_ref[j, :, :LEAF] = jnp.where(j < here, wire_ref[0], wire_ref[LD - 1])
        slots_ref[j, :, LEAF:] = share


def joined_kernel(at_ref, came_ref, wire_ref, tall_ref, whole_ref):
    here = at_ref[0]
    total = came_ref[0, :, LEAF:]
    for j in range(1, 8):
        total = total + came_ref[j, :, LEAF:]
    packed = jnp.concatenate(
        [
            jnp.concatenate([total[0:1, :RANK], total[1:2, :RANK]], 1),
            jnp.concatenate([total[2:3, :RANK], jnp.zeros((1, RANK), F32)], 1),
        ],
        0,
    )
    whole_ref[...] = jnp.broadcast_to(packed[None], whole_ref.shape)
    lower = came_ref[jnp.maximum(here - 1, 0), :, :LEAF]
    upper = came_ref[jnp.minimum(here + 1, 7), :, :LEAF]
    tall_ref[0] = jnp.where(here > 0, lower, 0.0)
    tall_ref[1 : LD + 1] = wire_ref[...]
    tall_ref[LD + 1] = jnp.where(here < 7, upper, 0.0)


def source_side(leaf, around, steps, slot, points_ref, loads_ref):
    high, low = halves(leaf)
    points_ref[slot] = jnp.transpose(jnp.concatenate([high, low, low, high], 0), (1, 0)).astype(BF16)
    c0, c1, c2 = leaf[0:1], leaf[1:2], leaf[2:3]
    flat = (c0 + around) * (c0 + around) + c2 * c2
    for step in steps:
        weight = jnp.exp2((-SHARPNESS * LOG2E) * (flat + (c1 + step) * (c1 + step))) * leaf[3:4]
        loads_ref[slot, step + 1] = jnp.concatenate(halves(leaf * weight), 0).astype(BF16)


def target_points(leaf):
    row = lax.broadcasted_iota(jnp.int32, leaf.shape, 0)
    high, low = halves(jnp.where(row < 3, leaf * (2 * SHARPNESS * LOG2E), 0.0))
    return jnp.concatenate([high, low, high, low], 0).astype(BF16)


def pair_kernel(target, points_ref, slot, pairs_ref, place):
    power = jnp.dot(points_ref[slot], target, preferred_element_type=F32)
    pair = jnp.exp2(power)
    high = pair.astype(BF16)
    pairs_ref[place, 0] = high
    pairs_ref[place, 1] = (pair - high.astype(F32)).astype(BF16)


def pair_sum(leaf, loads_ref, slot, pairs_ref, place, around, step):
    c0, c1, c2 = leaf[0:1], leaf[1:2], leaf[2:3]
    loads = loads_ref[slot, step + 1]
    rows = jnp.dot(loads, pairs_ref[place, 0], preferred_element_type=F32) + jnp.dot(
        loads, pairs_ref[place, 1], preferred_element_type=F32
    )
    power = (2 * SHARPNESS * LOG2E) * (around * c0 + step * c1) - (SHARPNESS * LOG2E) * (c0 * c0 + c1 * c1 + c2 * c2)
    weight = jnp.exp2(power) * (KERNEL_SCALE * leaf[3:4])
    return weight * (rows[:8] + rows[8:])


def near_own_kernel(wire_ref, near_ref, points_ref, loads_ref, pairs_ref):
    points_ref[0] = jnp.zeros((LEAF, 32), BF16)
    points_ref[LD + 1] = jnp.zeros((LEAF, 32), BF16)
    loads_ref[0] = jnp.zeros((3, 16, LEAF), BF16)
    loads_ref[LD + 1] = jnp.zeros((3, 16, LEAF), BF16)

    def prepare(l, _):
        source_side(wire_ref[l], 0, (-1, 0, 1), l + 1, points_ref, loads_ref)
        return 0

    lax.fori_loop(0, LD, prepare, 0, unroll=12)

    def leaf(l, _):
        here = wire_ref[l]
        target = target_points(here)
        for step in (-1, 0, 1):
            pair_kernel(target, points_ref, l + 1 + step, pairs_ref, step + 1)
        total = jnp.zeros((8, LEAF), F32)
        for step in (-1, 0, 1):
            total = total + pair_sum(here, loads_ref, l + 1 + step, pairs_ref, step + 1, 0, step)
        near_ref[l] = total
        return 0

    lax.fori_loop(0, LD, leaf, 0)


def near_cross_kernel(tall_ref, lower_ref, upper_ref, near_ref, points_ref, loads_ref, pairs_ref):
    for around, came_ref, base in ((-1, lower_ref, 0), (1, upper_ref, TALL)):

        def prepare(l, _, around=around, came_ref=came_ref, base=base):
            source_side(came_ref[l], around, (-1, 0, 1), base + l, points_ref, loads_ref)
            return 0

        lax.fori_loop(0, TALL, prepare, 0, unroll=13)
    source_side(tall_ref[0], 0, (-1,), 2 * TALL, points_ref, loads_ref)
    source_side(tall_ref[LD + 1], 0, (1,), 2 * TALL + 1, points_ref, loads_ref)

    def leaf(l, _):
        here = tall_ref[l + 1]
        target = target_points(here)
        sides = [(around, base, step) for around, base in ((-1, 0), (1, TALL)) for step in (-1, 0, 1)]
        for place, (around, base, step) in enumerate(sides):
            pair_kernel(target, points_ref, base + l + 1 + step, pairs_ref, place)
        total = jnp.zeros((8, LEAF), F32)
        for place, (around, base, step) in enumerate(sides):
            total = total + pair_sum(here, loads_ref, base + l + 1 + step, pairs_ref, place, around, step)
        near_ref[l] = total
        return 0

    lax.fori_loop(0, LD, leaf, 0)
    for l, slot, step in ((0, 2 * TALL, -1), (LD - 1, 2 * TALL + 1, 1)):
        here = tall_ref[l + 1]
        pair_kernel(target_points(here), points_ref, slot, pairs_ref, 0)
        near_ref[l] += pair_sum(here, loads_ref, slot, pairs_ref, 0, 0, step)


def near_scratch(leaves, places):
    return [
        pltpu.VMEM((leaves, LEAF, 32), BF16),
        pltpu.VMEM((leaves, 3, 16, LEAF), BF16),
        pltpu.VMEM((places, 2, LEAF, LEAF), BF16),
    ]


def window_kernel(lower_ref, tall_ref, upper_ref, window_ref, head_ref, tail_ref):
    for i, came_ref in enumerate((lower_ref, tall_ref, upper_ref)):
        rows = jnp.concatenate(
            [came_ref[l, 7:8, :] for l in range(TALL)] + [jnp.zeros((ROWS - TALL, LEAF), F32)], 0
        )
        window_ref[i] = rows
        if i < 2:
            head_ref[i] = rows
        if i > 0:
            tail_ref[i - 1] = rows


def far_kernel(mask_ref, below_ref, above_ref, far_below_ref, far_above_ref, coupling_ref, basis_ref, own_ref, cross_ref, part_ref):
    held = {-4 + i: below_ref[i] for i in range(3)}
    held |= {2 + i: above_ref[i] for i in range(3)}
    held |= {-6 + i: far_below_ref[i] for i in range(2)}
    held |= {5 + i: far_above_ref[i] for i in range(2)}
    total = jnp.zeros((3 * ROWS, 3 * RANK), F32)
    for q in range(2 * (REACH - 1)):
        around = q + 2 if q < REACH - 1 else 3 - q
        rows = held[around]
        stacked = jnp.concatenate([rows[:, r * RANK : (r + 1) * RANK] for r in range(3)], 0)
        coupling = jnp.concatenate(
            [coupling_ref[3 * q + b] * mask_ref[0, 3 * q + b].astype(F32) for b in range(3)], 0
        )
        total = total + lax.dot_general(stacked, coupling, BY_LAST, precision=EXACT, preferred_element_type=F32)
    far = []
    for r in range(3):
        block = total[r * ROWS : (r + 1) * ROWS]
        far.append(
            block[0:LD, :RANK] + block[1 : LD + 1, RANK : 2 * RANK] + block[2 : LD + 2, 2 * RANK :]
        )
        far.append(jnp.zeros((ROWS - LD, RANK), F32))
    columns = jnp.transpose(jnp.concatenate(far, 0), (1, 0))
    for l in range(LD):
        basis = basis_ref[l]
        for r in range(3):
            at = r * ROWS + l
            down = jnp.sum(basis * columns[:, at : at + 1], axis=0, keepdims=True)
            part_ref[r, l : l + 1, :] = down + own_ref[l, 4 + r : 5 + r, :] + cross_ref[l, 4 + r : 5 + r, :]


def downward_kernel(at_ref, admissible_ref, every_ref, top_ref, slab_ref, transfer_ref, basis_ref, part_ref, out_ref):
    here = at_ref[1]
    sectors = top_ref.shape[0]

    def couple(t, sums):
        apart = lax.rem(t - here + sectors, sectors)
        distant = jnp.logical_and(apart > REACH, apart < sectors - REACH)
        allowed = jnp.where(distant, admissible_ref[0, t], 0).astype(F32)
        coupling = top_ref[t]
        both = every_ref[t] * allowed
        rows = (both[0:1, :RANK], both[0:1, RANK:], both[1:2, :RANK])
        return tuple(s + coupling * row for s, row in zip(sums, rows))

    nothing = jnp.zeros((RANK, RANK), F32)
    sums = lax.fori_loop(0, sectors, couple, (nothing,) * 3, unroll=8)
    lane = lax.broadcasted_iota(jnp.int32, (RANK, 128), 1)
    columns = jnp.zeros((RANK, 128), F32)
    for r in range(3):
        columns = jnp.where(lane == r, jnp.sum(sums[r], axis=1, keepdims=True), columns)
    local = jnp.transpose(columns, (1, 0))[:8]
    slab = lax.dot_general(local, slab_ref[...], BY_LAST, precision=EXACT, preferred_element_type=F32)

    def leaf(l, _):
        basis = basis_ref[l]
        transfer = transfer_ref[l]
        for r in range(3):
            column = jnp.sum(transfer * slab[r : r + 1], axis=1, keepdims=True)
            down = jnp.sum(basis * column, axis=0, keepdims=True)
            out_ref[r, pl.ds(l, 1), :] = part_ref[r, pl.ds(l, 1), :] + down
        return 0

    lax.fori_loop(0, LD, leaf, 0, unroll=4)


def passed_along(x, axis, by):
    count = lax.axis_size(axis)
    return lax.ppermute(x, axis, [(i, (i + by) % count) for i in range(count)])


def body(
    values,
    offsets,
    stiffness,
    leaf_basis,
    transfer,
    slab_transfer_matrices,
    leaf_coupling_matrices,
    leaf_admissible_mask,
    top_coupling,
    top_admissible,
):
    at = jnp.stack([lax.axis_index("along"), lax.axis_index("blk")]).astype(jnp.int32)
    sectors = lax.axis_size("blk")
    values = values[:, 0]
    offsets = offsets[:, 0]
    basis = leaf_basis[0]
    transfer = transfer[0]
    slab = slab_transfer_matrices[0, 0]

    wire, slots = call(
        upward_kernel, (shaped(LD, 8, LEAF), shaped(8, 8, LEAF + 128)), [SMEM] + [VMEM] * 6, flops=10**9
    )(at, values, offsets, stiffness[0], basis, transfer, slab)
    came = lax.all_to_all(slots, "along", 0, 0, tiled=True)
    own = call(
        near_own_kernel, shaped(LD, 8, LEAF), [VMEM], near_scratch(TALL, 3), flops=9 * 10**9
    )(wire)
    tall, whole = call(
        joined_kernel, (shaped(TALL, 8, LEAF), shaped(sectors, 2, 128)), [SMEM, VMEM, VMEM], flops=10**8
    )(at, came, wire)
    lower = passed_along(tall, "blk", 1)
    upper = passed_along(tall, "blk", -1)
    every = lax.all_to_all(whole, "blk", 0, 0, tiled=True)
    window, head, tail = call(
        window_kernel,
        (shaped(3, ROWS, LEAF), shaped(2, ROWS, LEAF), shaped(2, ROWS, LEAF)),
        [VMEM] * 3,
        flops=10**8,
    )(lower, tall, upper)
    below = passed_along(window, "blk", 3)
    above = passed_along(window, "blk", -3)
    far_below = passed_along(head, "blk", 5)
    far_above = passed_along(tail, "blk", -5)
    cross = call(
        near_cross_kernel, shaped(LD, 8, LEAF), [VMEM] * 3, near_scratch(2 * TALL + 2, 6), flops=18 * 10**9
    )(tall, lower, upper)
    part = call(far_kernel, shaped(RHS, LD, LEAF), [SMEM] + [VMEM] * 8, flops=2 * 10**9)(
        leaf_admissible_mask, below, above, far_below, far_above, leaf_coupling_matrices[0], basis, own, cross
    )
    out = call(downward_kernel, shaped(RHS, LD, LEAF), [SMEM] * 2 + [VMEM] * 6, flops=2 * 10**9)(
        at, top_admissible, every, top_coupling[0], slab, transfer, basis, part
    )
    return out[:, None]


def solution(mesh):
    return jax.shard_map(
        body,
        mesh=mesh,
        in_specs=(
            P(None, "blk", "along", None),
            P(None, "blk", "along", None),
            P("blk", "along", None),
            P("blk", "along", None, None),
            P("blk", "along", None, None),
            P("blk", "along", None, None),
            P("blk", None, None, None),
            P("blk", None),
            P("blk", None, None, None),
            P("blk", None),
        ),
        out_specs=P(None, "blk", "along", None),
        check_vma=False,
    )
```

time: 232 us -> 101 us (0.44)
  matrix products: 116 us -> 0 us
  Pallas kernels: 0 us -> 38.3 us
  starting transfers between devices: 69.9 us -> 39 us
  between operations: 19.5 us -> 0.24 us
  blocking collectives: 0 us -> 13.9 us
  other arithmetic: 7.84 us -> 0.07 us
  waiting for transfers between devices: 7.76 us -> 0.03 us
    dot_general x46 -> x0, matrix products: 116 us -> none  [the longest x9 82.6 us: near_field(): jnp.einsum('alij,ralj->rali', kernel, source[4:], precision=HIGHEST_ACCUR...]
    pallas_call x0 -> x7, Pallas kernels: none -> 38.3 us  [the longest x1 16.6 us: body(): call(near_cross_kernel, shaped(LD, 8, LEAF), [VMEM] * 3, near_scratch(2 *...]
    ppermute x6 -> x0, starting transfers between devices: 27.4 us -> none  [the longest x3 17.9 us: with_halo(): lax.ppermute(head, axis, [((i + 1) % count, i) for i in range(ends)])]
    all_to_all x0 -> x1, blocking collectives: none -> 13.9 us  [body(): came = lax.all_to_all(slots, 'along', 0, 0, tiled=True)]
    ppermute x6, starting transfers between devices: 33.4 us -> 24 us  [passed_along(): return lax.ppermute(x, axis, [(i, (i + by) % count) for i in range(count)])]
    all_to_all x2 -> x1, starting transfers between devices: 9.16 us -> 15 us  [body(): every = lax.all_to_all(whole, 'blk', 0, 0, tiled=True)]
    ppermute x6 -> x0, waiting for transfers between devices: 5.83 us -> none  [the longest x3 5.82 us: with_halo(): lax.ppermute(tail, axis, [(i, (i + 1) % count) for i in range(ends)])]
    unnamed x90 -> x28, local copies, waits for them, and re-layouts: 4.03 us -> 8.38 us
  transfers between devices with their start and end apart: 14 -> 7, of which waited for: 3 -> 0; matrix products, arithmetic and copies ran while one was open for 52% -> 0% of each run, Pallas kernels for 0% -> 32%
where the time goes in v1:
time: 101 us; the launch traced here: 100 us
  starting transfers between devices  39 us (39%)
  Pallas kernels  38.3 us (38%)
  blocking collectives  13.9 us (14%)
  local copies, waits for them, and re-layouts  8.38 us (8%)
    ppermute x6, starting transfers between devices, passed_along(): return lax.ppermute(x, axis, [(i, (i + by) % count) for i in range(count)])  24 us
    pallas_call x1, Pallas kernels, body(): call(near_cross_kernel, shaped(LD, 8, LEAF), [VMEM] * 3, near_scratch(2 *...  16.6 us
    all_to_all x1, starting transfers between devices, body(): every = lax.all_to_all(whole, 'blk', 0, 0, tiled=True)  15 us
    all_to_all x1, blocking collectives, body(): came = lax.all_to_all(slots, 'along', 0, 0, tiled=True)  13.9 us
    pallas_call x1, Pallas kernels, body(): call(near_own_kernel, shaped(LD, 8, LEAF), [VMEM], near_scratch(TALL, 3),...  11.2 us
    unnamed x28, local copies, waits for them, and re-layouts  8.38 us
    pallas_call x1, Pallas kernels, body(): call(far_kernel, shaped(RHS, LD, LEAF), [SMEM] + [VMEM] * 8, flops=2 * 10...  3.79 us
    pallas_call x1, Pallas kernels, body(): call(downward_kernel, shaped(RHS, LD, LEAF), [SMEM] * 2 + [VMEM] * 6, flo...  3.56 us
  transfers between devices with their start and end apart: 7, of which 0 were waited for; matrix products, arithmetic and copies ran while one was open for 0% of the time, Pallas kernels for 32%

profile of v1, /device:TPU:1, one launch (start us, length us, event | category | flops | bytes accessed | tf_op | source)
XLA Modules:
  0.0 100.0 jit_solution(8856751796353042319)
XLA Ops:
  0.0 0.1 pad_add_fusion.at_ref
  0.1 0.0 copy-start.1
  0.1 1.4 %copy-done.1 = f32[1,24,64,256]{3,2,1,0:T(8,128)S(1)} copy-done((f32[1,24,64,256]{3,2,1,0:T(8,128)S(1)}, f32[1,24,64,256]{3,2,1,0:T(8,128)}, u32[]{:S(2)}) %copy-start.1) | copy-done | bytes 1572888
  1.5 0.0 copy-start.5
  1.5 1.1 %copy-done.5 = f32[1,24,64,64]{3,2,1,0:T(8,128)S(1)} copy-done((f32[1,24,64,64]{3,2,1,0:T(8,128)S(1)}, f32[1,24,64,64]{3,2,1,0:T(8,128)}, u32[]{:S(2)}) %copy-start.5) | copy-done | bytes 393240
  2.6 0.0 copy-start.7
  2.6 0.9 copy-done.7
  3.5 0.0 copy-start.8
  3.5 0.9 copy-done.8
  4.4 0.0 copy-start.9
  4.4 0.8 copy-done.9
  5.1 0.0 copy-start.11
  5.1 0.7 copy-done.11
  5.9 1.8 %shard_map.100 = (f32[24,8,256]{2,1,0:T(8,128)S(1)}, f32[8,8,384]{2,1,0:T(8,128)S(1)}) custom-call(s32[2]{0:T(128)S(1)} %pad_add_fusion.at_ref, f32[3,24,256]{2,1,0:T(8,128)S(1)} %bitcast.20, f32[3,24,256]{2,1,0:T(8,128)S(1)} %bitcast.21, f32[24,256]{1,0:T(8,128)S(1)} %bitcast.24, f32[24,64,256]{2,1,0:T(8,128)S(1)} %bitcast.14, f32[24,64,64]{2,1,0:T(8,128)S(1)} %bitcast.18, ...), custom_call_target="tpu_custom_call" | custom-call | flops 1000000000 | bytes 1048576 | tf_op jit(solution)/shard_map/pallas_call | solution.py:311
  7.7 13.9 %all_to_all.10.came_ref = f32[8,8,384]{2,1,0:T(8,128)S(1)} all-to-all(f32[8,8,384]{2,1,0:T(8,128)S(1)} %get-tuple-element.12), channel_id=1, replica_groups=mesh['blk'=64,'along'=8] {'along'}, dimensions={0} | all-to-all | bytes 196608 | tf_op jit(solution)/shard_map/all_to_all | solution.py:314
  21.7 1.3 %shard_map.101 = (f32[26,8,256]{2,1,0:T(8,128)S(1)}, f32[64,2,128]{2,1,0:T(2,128)}) custom-call(s32[2]{0:T(128)S(1)} %pad_add_fusion.at_ref, f32[8,8,384]{2,1,0:T(8,128)S(1)} %all_to_all.10.came_ref, f32[24,8,256]{2,1,0:T(8,128)S(1)} %get-tuple-element.13.wire_ref), custom_call_target="tpu_custom_call" | custom-call | flops 100000000 | bytes 1048576 | tf_op jit(solution)/shard_map/pallas_call | solution.py:318
  22.9 5.0 %collective-permute-start.1 = (f32[26,8,256]{2,1,0:T(8,128)S(1)}, f32[26,8,256]{2,1,0:T(8,128)S(1)}, u32[]{:S(2)}, u32[]{:S(2)}) collective-permute-start(f32[26,8,256]{2,1,0:T(8,128)S(1)} %get-tuple-element.15.tall_ref), channel_id=1, source_target_pairs={{0,504},{8,0},{16,8},{24,16},{32,24},{40,32},{48,40},{56,48},{64,5... | collective-permute-start | bytes 638984 | tf_op jit(solution)/shard_map/ppermute | solution.py:288
  28.0 2.4 %collective-permute-start = (f32[26,8,256]{2,1,0:T(8,128)S(1)}, f32[26,8,256]{2,1,0:T(8,128)S(1)}, u32[]{:S(2)}, u32[]{:S(2)}) collective-permute-start(f32[26,8,256]{2,1,0:T(8,128)S(1)} %get-tuple-element.15.tall_ref), channel_id=1, source_target_pairs={{0,8},{8,16},{16,24},{24,32},{32,40},{40,48},{48,56},{56,64},{64,7... | collective-permute-start | bytes 638984 | tf_op jit(solution)/shard_map/ppermute | solution.py:288
  30.4 11.2 %shard_map.103.own_ref = f32[24,8,256]{2,1,0:T(8,128)S(1)} custom-call(f32[24,8,256]{2,1,0:T(8,128)S(1)} %get-tuple-element.13.wire_ref), custom_call_target="tpu_custom_call" | custom-call | flops 8999999488 | bytes 1048576 | tf_op jit(solution)/shard_map/pallas_call | solution.py:315
  41.6 15.0 %all-to-all-start.1 = ((f32[64,2,128]{2,1,0:T(2,128)}), f32[64,2,128]{2,1,0:T(2,128)S(1)}, u32[]{:S(2)}, u32[]{:S(2)}) async-start(f32[64,2,128]{2,1,0:T(2,128)} %get-tuple-element.14), calls=%async_computation.1 | async-start | bytes 131072 | tf_op jit(solution)/shard_map/all_to_all | solution.py:323
  56.6 0.0 collective-permute-done.1.upper_ref
  56.6 0.0 collective-permute-done.lower_ref
  56.7 6.0 %collective-permute-start.3 = (f32[3,32,256]{2,1,0:T(8,128)S(1)}, f32[3,32,256]{2,1,0:T(8,128)S(1)}, u32[]{:S(2)}, u32[]{:S(2)}) collective-permute-start(f32[3,32,256]{2,1,0:T(8,128)S(1)} %get-tuple-element.16), channel_id=1, source_target_pairs={{0,488},{8,496},{16,504},{24,0},{32,8},{40,16},{48,24},{56,32},{64... | collective-permute-start | bytes 294920 | tf_op jit(solution)/shard_map/ppermute | solution.py:288
  62.7 1.9 %collective-permute-start.2 = (f32[3,32,256]{2,1,0:T(8,128)S(1)}, f32[3,32,256]{2,1,0:T(8,128)S(1)}, u32[]{:S(2)}, u32[]{:S(2)}) collective-permute-start(f32[3,32,256]{2,1,0:T(8,128)S(1)} %get-tuple-element.16), channel_id=1, source_target_pairs={{0,24},{8,32},{16,40},{24,48},{32,56},{40,64},{48,72},{56,80},{64,... | collective-permute-start | bytes 294920 | tf_op jit(solution)/shard_map/ppermute | solution.py:288
  64.6 4.2 %collective-permute-start.4 = (f32[2,32,256]{2,1,0:T(8,128)S(1)}, f32[2,32,256]{2,1,0:T(8,128)S(1)}, u32[]{:S(2)}, u32[]{:S(2)}) collective-permute-start(f32[2,32,256]{2,1,0:T(8,128)S(1)} %get-tuple-element.17), channel_id=1, source_target_pairs={{0,40},{8,48},{16,56},{24,64},{32,72},{40,80},{48,88},{56,96},{64,... | collective-permute-start | bytes 196616 | tf_op jit(solution)/shard_map/ppermute | solution.py:288
  68.8 0.0 copy-start.2
  68.8 0.0 copy-start.4
  68.9 0.0 copy-start.12
  68.9 4.5 %collective-permute-start.5 = (f32[2,32,256]{2,1,0:T(8,128)S(1)}, f32[2,32,256]{2,1,0:T(8,128)S(1)}, u32[]{:S(2)}, u32[]{:S(2)}) collective-permute-start(f32[2,32,256]{2,1,0:T(8,128)S(1)} %get-tuple-element.18), channel_id=1, source_target_pairs={{0,472},{8,480},{16,488},{24,496},{32,504},{40,0},{48,8},{56,16},{... | collective-permute-start | bytes 196616 | tf_op jit(solution)/shard_map/ppermute | solution.py:288
  73.3 16.6 %shard_map.104.cross_ref = f32[24,8,256]{2,1,0:T(8,128)S(1)} custom-call(f32[26,8,256]{2,1,0:T(8,128)S(1)} %get-tuple-element.15.tall_ref, f32[26,8,256]{2,1,0:T(8,128)S(1)} %collective-permute-done.lower_ref, f32[26,8,256]{2,1,0:T(8,128)S(1)} %collective-permute-done.1.upper_ref), custom_call_target="tpu_custom_call" | custom-call | flops 17999998976 | bytes 1048576 | tf_op jit(solution)/shard_map/pallas_call | solution.py:334
  89.9 0.0 collective-permute-done.4.far_below_ref
  89.9 0.0 collective-permute-done.5.far_above_ref
  89.9 0.0 collective-permute-done.3.above_ref
  89.9 0.0 collective-permute-done.2.below_ref
  89.9 0.0 copy-done.2
  90.0 0.0 copy-done.4
  90.0 0.0 copy-done.12
  90.0 0.0 copy-start
  90.0 0.0 copy-start.10
  90.0 0.0 copy-start.13
  90.0 3.8 %shard_map.105.part_ref = f32[3,24,256]{2,1,0:T(8,128)S(1)} custom-call(s32[1,30]{1,0:T(1,128)S(1)} %copy-done.12, f32[3,32,256]{2,1,0:T(8,128)S(1)} %collective-permute-done.2.below_ref, f32[3,32,256]{2,1,0:T(8,128)S(1)} %collective-permute-done.3.above_ref, f32[2,32,256]{2,1,0:T(8,128)S(1)} %collective-permute-done.4.far_below_ref, ...), custom_call_target="tpu_custom_call" | custom-call | flops 2000000000 | bytes 1048576 | tf_op jit(solution)/shard_map/pallas_call | solution.py:337
  93.8 0.0 all-to-all-done.1.every_ref
  93.8 0.0 copy-done
  93.8 0.0 copy-done.10
  93.8 0.0 copy-done.13
  93.8 0.0 copy-start.3
  93.9 1.4 %copy-done.3 = f32[1,24,64,256]{3,2,1,0:T(8,128)S(1)} copy-done((f32[1,24,64,256]{3,2,1,0:T(8,128)S(1)}, f32[1,24,64,256]{3,2,1,0:T(8,128)}, u32[]{:S(2)}) %copy-start.3) | copy-done | bytes 1572888
  95.3 0.0 copy-start.6
  95.3 1.1 %copy-done.6 = f32[1,24,64,64]{3,2,1,0:T(8,128)S(1)} copy-done((f32[1,24,64,64]{3,2,1,0:T(8,128)S(1)}, f32[1,24,64,64]{3,2,1,0:T(8,128)}, u32[]{:S(2)}) %copy-start.6) | copy-done | bytes 393240
  96.4 3.6 %shard_map.106 = f32[3,24,256]{2,1,0:T(8,128)} custom-call(s32[2]{0:T(128)S(1)} %pad_add_fusion.at_ref, s32[1,64]{1,0:T(1,128)S(1)} %copy-done.13, f32[64,2,128]{2,1,0:T(2,128)S(1)} %all-to-all-done.1.every_ref, f32[64,64,64]{2,1,0:T(8,128)S(1)} %bitcast.13, f32[64,64]{1,0:T(8,128)S(1)} %bitcast.23, f32[24,64,64]{2,1,0:T(8,128)S(1)} %bitcast.19, ...), custom_call_target="tpu_custom_call" | custom-call | flops 2000000000 | bytes 1048576 | tf_op jit(solution)/shard_map/pallas_call | solution.py:340
  (1 shorter events, 0.0 us)
Async XLA Ops:
  0.1 1.4 %copy-start.1 = (f32[1,24,64,256]{3,2,1,0:T(8,128)S(1)}, f32[1,24,64,256]{3,2,1,0:T(8,128)}, u32[]{:S(2)}) copy-start(f32[1,24,64,256]{3,2,1,0:T(8,128)} %param.13) | copy-start | bytes 4718596
  1.5 1.1 %copy-start.5 = (f32[1,24,64,64]{3,2,1,0:T(8,128)S(1)}, f32[1,24,64,64]{3,2,1,0:T(8,128)}, u32[]{:S(2)}) copy-start(f32[1,24,64,64]{3,2,1,0:T(8,128)} %param.14) | copy-start | bytes 1179652
  2.6 0.9 copy-start.7
  3.5 0.9 copy-start.8
  4.4 0.8 copy-start.9
  5.1 0.7 copy-start.11
  22.9 33.7 %collective-permute-start.1 = (f32[26,8,256]{2,1,0:T(8,128)S(1)}, f32[26,8,256]{2,1,0:T(8,128)S(1)}, u32[]{:S(2)}, u32[]{:S(2)}) collective-permute-start(f32[26,8,256]{2,1,0:T(8,128)S(1)} %get-tuple-element.15.tall_ref), channel_id=1, source_target_pairs={{0,504},{8,0},{16,8},{24,16},{32,24},{40,32},{48,40},{56,48},{64,5... | collective-permute-start | bytes 638984 | tf_op jit(solution)/shard_map/ppermute | solution.py:288
  28.0 28.7 %collective-permute-start = (f32[26,8,256]{2,1,0:T(8,128)S(1)}, f32[26,8,256]{2,1,0:T(8,128)S(1)}, u32[]{:S(2)}, u32[]{:S(2)}) collective-permute-start(f32[26,8,256]{2,1,0:T(8,128)S(1)} %get-tuple-element.15.tall_ref), channel_id=1, source_target_pairs={{0,8},{8,16},{16,24},{24,32},{32,40},{40,48},{48,56},{56,64},{64,7... | collective-permute-start | bytes 638984 | tf_op jit(solution)/shard_map/ppermute | solution.py:288
  41.6 52.2 %all-to-all-start.1 = ((f32[64,2,128]{2,1,0:T(2,128)}), f32[64,2,128]{2,1,0:T(2,128)S(1)}, u32[]{:S(2)}, u32[]{:S(2)}) async-start(f32[64,2,128]{2,1,0:T(2,128)} %get-tuple-element.14), calls=%async_computation.1 | async-start | bytes 131072 | tf_op jit(solution)/shard_map/all_to_all | solution.py:323
  56.7 33.2 %collective-permute-start.3 = (f32[3,32,256]{2,1,0:T(8,128)S(1)}, f32[3,32,256]{2,1,0:T(8,128)S(1)}, u32[]{:S(2)}, u32[]{:S(2)}) collective-permute-start(f32[3,32,256]{2,1,0:T(8,128)S(1)} %get-tuple-element.16), channel_id=1, source_target_pairs={{0,488},{8,496},{16,504},{24,0},{32,8},{40,16},{48,24},{56,32},{64... | collective-permute-start | bytes 294920 | tf_op jit(solution)/shard_map/ppermute | solution.py:288
  62.7 27.3 %collective-permute-start.2 = (f32[3,32,256]{2,1,0:T(8,128)S(1)}, f32[3,32,256]{2,1,0:T(8,128)S(1)}, u32[]{:S(2)}, u32[]{:S(2)}) collective-permute-start(f32[3,32,256]{2,1,0:T(8,128)S(1)} %get-tuple-element.16), channel_id=1, source_target_pairs={{0,24},{8,32},{16,40},{24,48},{32,56},{40,64},{48,72},{56,80},{64,... | collective-permute-start | bytes 294920 | tf_op jit(solution)/shard_map/ppermute | solution.py:288
  64.6 25.3 %collective-permute-start.4 = (f32[2,32,256]{2,1,0:T(8,128)S(1)}, f32[2,32,256]{2,1,0:T(8,128)S(1)}, u32[]{:S(2)}, u32[]{:S(2)}) collective-permute-start(f32[2,32,256]{2,1,0:T(8,128)S(1)} %get-tuple-element.17), channel_id=1, source_target_pairs={{0,40},{8,48},{16,56},{24,64},{32,72},{40,80},{48,88},{56,96},{64,... | collective-permute-start | bytes 196616 | tf_op jit(solution)/shard_map/ppermute | solution.py:288
  68.8 21.1 %copy-start.2 = (f32[1,24,64,256]{3,2,1,0:T(8,128)S(1)}, f32[1,24,64,256]{3,2,1,0:T(8,128)}, u32[]{:S(2)}) copy-start(f32[1,24,64,256]{3,2,1,0:T(8,128)} %param.13) | copy-start | bytes 4718596
  68.8 21.1 %copy-start.4 = (f32[1,30,64,64]{3,2,1,0:T(8,128)S(1)}, f32[1,30,64,64]{3,2,1,0:T(8,128)}, u32[]{:S(2)}) copy-start(f32[1,30,64,64]{3,2,1,0:T(8,128)} %param.16) | copy-start | bytes 1474564
  68.9 21.1 %copy-start.12 = (s32[1,30]{1,0:T(1,128)S(1)}, s32[1,30]{1,0:T(1,128)}, u32[]{:S(2)}) copy-start(s32[1,30]{1,0:T(1,128)} %mask_ref.1) | copy-start | bytes 364
  68.9 21.0 %collective-permute-start.5 = (f32[2,32,256]{2,1,0:T(8,128)S(1)}, f32[2,32,256]{2,1,0:T(8,128)S(1)}, u32[]{:S(2)}, u32[]{:S(2)}) collective-permute-start(f32[2,32,256]{2,1,0:T(8,128)S(1)} %get-tuple-element.18), channel_id=1, source_target_pairs={{0,472},{8,480},{16,488},{24,496},{32,504},{40,0},{48,8},{56,16},{... | collective-permute-start | bytes 196616 | tf_op jit(solution)/shard_map/ppermute | solution.py:288
  90.0 3.8 %copy-start = (f32[1,64,64,64]{3,2,1,0:T(8,128)S(1)}, f32[1,64,64,64]{3,2,1,0:T(8,128)}, u32[]{:S(2)}) copy-start(f32[1,64,64,64]{3,2,1,0:T(8,128)} %param.18) | copy-start | bytes 3145732
  90.0 3.8 %copy-start.10 = (f32[1,1,64,64]{3,2,1,0:T(8,128)S(1)}, f32[1,1,64,64]{3,2,1,0:T(8,128)}, u32[]{:S(2)}) copy-start(f32[1,1,64,64]{3,2,1,0:T(8,128)} %param.15) | copy-start | bytes 49156
  90.0 3.8 %copy-start.13 = (s32[1,64]{1,0:T(1,128)S(1)}, s32[1,64]{1,0:T(1,128)}, u32[]{:S(2)}) copy-start(s32[1,64]{1,0:T(1,128)} %admissible_ref.1) | copy-start | bytes 772
  93.8 1.4 %copy-start.3 = (f32[1,24,64,256]{3,2,1,0:T(8,128)S(1)}, f32[1,24,64,256]{3,2,1,0:T(8,128)}, u32[]{:S(2)}) copy-start(f32[1,24,64,256]{3,2,1,0:T(8,128)} %param.13) | copy-start | bytes 4718596
  95.3 1.1 %copy-start.6 = (f32[1,24,64,64]{3,2,1,0:T(8,128)S(1)}, f32[1,24,64,64]{3,2,1,0:T(8,128)}, u32[]{:S(2)}) copy-start(f32[1,24,64,64]{3,2,1,0:T(8,128)} %param.14) | copy-start | bytes 1179652

commit v2 on v1

--- a/solution.py
+++ b/solution.py
@@ -22,20 +22,26 @@
 BF16 = jnp.bfloat16
 EXACT = lax.Precision.HIGHEST
 VMEM = pl.BlockSpec(memory_space=pltpu.VMEM)
+HBM = pl.BlockSpec(memory_space=pltpu.HBM)
 SMEM = pl.BlockSpec(memory_space=pltpu.SMEM)
 BY_LAST = (((1,), (1,)), ((), ()))
 MIB = 2**20
-
-
-def call(kernel, outs, ins, scratch=(), flops=0, vmem=48):
+FULL = 60 * MIB + 128 * 1024
+OWN_TURN = 3
+CROSS_TURN = 2
+UP_PARTS = 4
+UP_LEAVES = LD // UP_PARTS
+
+
+def call(kernel, outs, ins, scratch=(), flops=0, bytes=1 << 20, vmem=16 * MIB):
     return pl.pallas_call(
         kernel,
         out_shape=outs,
         in_specs=ins,
         out_specs=jax.tree.map(lambda _: VMEM, outs),
         scratch_shapes=list(scratch),
-        compiler_params=pltpu.CompilerParams(vmem_limit_bytes=vmem * MIB),
-        cost_estimate=pl.CostEstimate(flops=flops, bytes_accessed=1 << 20, transcendentals=0),
+        compiler_params=pltpu.CompilerParams(vmem_limit_bytes=vmem),
+        cost_estimate=pl.CostEstimate(flops=flops, bytes_accessed=bytes, transcendentals=0),
     )
 
 
@@ -48,17 +54,45 @@
     return high, x - high
 
 
-def upward_kernel(at_ref, values_ref, offsets_ref, stiffness_ref, basis_ref, transfer_ref, slab_ref, wire_ref, slots_ref):
+def upward_kernel(
+    at_ref, values_hbm, offsets_hbm, stiffness_hbm, basis_hbm, transfer_hbm, slab_hbm, wire_ref, slots_ref,
+    values_ref, offsets_ref, stiffness_ref, basis_ref, transfer_ref, slab_ref, sems,
+):
     lane = lax.broadcasted_iota(jnp.int32, (RANK, 128), 1)
+    small = [
+        pltpu.make_async_copy(source, target, sems.at[n])
+        for n, (source, target) in enumerate(
+            ((values_hbm, values_ref), (offsets_hbm, offsets_ref), (stiffness_hbm, stiffness_ref), (slab_hbm, slab_ref))
+        )
+    ]
+    large = []
+    for part in range(UP_PARTS):
+        piece = pl.ds(part * UP_LEAVES, UP_LEAVES)
+        large.append(
+            [
+                pltpu.make_async_copy(source.at[piece], target.at[piece], sems.at[4 + 2 * part + n])
+                for n, (source, target) in enumerate(((basis_hbm, basis_ref), (transfer_hbm, transfer_ref)))
+            ]
+        )
+    for copy in small + [copy for pair in large for copy in pair]:
+        copy.start()
+    for copy in small:
+        copy.wait()
+
+    def record(l, _):
+        row = pl.ds(l, 1)
+        for r in range(3):
+            wire_ref[l, r : r + 1, :] = offsets_ref[r, row, :] - 0.5
+            wire_ref[l, 4 + r : 5 + r, :] = values_ref[r, row, :]
+        wire_ref[l, 3:4, :] = stiffness_ref[row, :]
+        return 0
+
+    lax.fori_loop(0, LD, record, 0, unroll=4)
 
     def leaf(l, carry):
         sums, columns = carry
         row = pl.ds(l, 1)
         new_sums = []
-        for r in range(3):
-            wire_ref[l, r : r + 1, :] = offsets_ref[r, row, :] - 0.5
-            wire_ref[l, 4 + r : 5 + r, :] = values_ref[r, row, :]
-        wire_ref[l, 3:4, :] = stiffness_ref[row, :]
         basis = basis_ref[l]
         transfer = transfer_ref[l]
         for r in range(3):
@@ -68,9 +102,12 @@
         return tuple(new_sums), columns
 
     nothing = jnp.zeros((RANK, RANK), F32)
-    sums, columns = lax.fori_loop(
-        0, LD, leaf, ((nothing,) * 3, jnp.zeros((RANK, 128), F32)), unroll=4
-    )
+    carry = ((nothing,) * 3, jnp.zeros((RANK, 128), F32))
+    for part in range(UP_PARTS):
+        for copy in large[part]:
+            copy.wait()
+        carry = lax.fori_loop(part * UP_LEAVES, (part + 1) * UP_LEAVES, leaf, carry, unroll=UP_LEAVES)
+    sums, columns = carry
     rows = jnp.transpose(columns, (1, 0))
     coefs = jnp.concatenate(
         [rows[:LD], rows[ROWS : ROWS + LD], rows[2 * ROWS : 2 * ROWS + LD], jnp.zeros((LD, RANK), F32)], 1
@@ -155,21 +192,23 @@
 
     lax.fori_loop(0, LD, prepare, 0, unroll=12)
 
-    def leaf(l, _):
-        here = wire_ref[l]
-        target = target_points(here)
-        for step in (-1, 0, 1):
-            pair_kernel(target, points_ref, l + 1 + step, pairs_ref, step + 1)
-        total = jnp.zeros((8, LEAF), F32)
-        for step in (-1, 0, 1):
-            total = total + pair_sum(here, loads_ref, l + 1 + step, pairs_ref, step + 1, 0, step)
-        near_ref[l] = total
+    def turn(g, _):
+        leaves = [g * OWN_TURN + n for n in range(OWN_TURN)]
+        places = [(n, step) for n in range(OWN_TURN) for step in (-1, 0, 1)]
+        targets = [target_points(wire_ref[l]) for l in leaves]
+        for place, (n, step) in enumerate(places):
+            pair_kernel(targets[n], points_ref, leaves[n] + 1 + step, pairs_ref, place)
+        totals = [jnp.zeros((8, LEAF), F32)] * OWN_TURN
+        for place, (n, step) in enumerate(places):
+            totals[n] += pair_sum(wire_ref[leaves[n]], loads_ref, leaves[n] + 1 + step, pairs_ref, place, 0, step)
+        for n in range(OWN_TURN):
+            near_ref[leaves[n]] = totals[n]
         return 0
 
-    lax.fori_loop(0, LD, leaf, 0)
-
-
-def near_cross_kernel(tall_ref, lower_ref, upper_ref, near_ref, points_ref, loads_ref, pairs_ref):
+    lax.fori_loop(0, LD // OWN_TURN, turn, 0)
+
+
+def near_cross_kernel(tall_ref, lower_ref, upper_ref, own_ref, near_ref, points_ref, loads_ref, pairs_ref):
     for around, came_ref, base in ((-1, lower_ref, 0), (1, upper_ref, TALL)):
 
         def prepare(l, _, around=around, came_ref=came_ref, base=base):
@@ -180,19 +219,26 @@
     source_side(tall_ref[0], 0, (-1,), 2 * TALL, points_ref, loads_ref)
     source_side(tall_ref[LD + 1], 0, (1,), 2 * TALL + 1, points_ref, loads_ref)
 
-    def leaf(l, _):
-        here = tall_ref[l + 1]
-        target = target_points(here)
-        sides = [(around, base, step) for around, base in ((-1, 0), (1, TALL)) for step in (-1, 0, 1)]
-        for place, (around, base, step) in enumerate(sides):
-            pair_kernel(target, points_ref, base + l + 1 + step, pairs_ref, place)
-        total = jnp.zeros((8, LEAF), F32)
-        for place, (around, base, step) in enumerate(sides):
-            total = total + pair_sum(here, loads_ref, base + l + 1 + step, pairs_ref, place, around, step)
-        near_ref[l] = total
+    def turn(g, _):
+        leaves = [g * CROSS_TURN + n for n in range(CROSS_TURN)]
+        places = [
+            (n, around, base, step)
+            for n in range(CROSS_TURN)
+            for around, base in ((-1, 0), (1, TALL))
+            for step in (-1, 0, 1)
+        ]
+        targets = [target_points(tall_ref[l + 1]) for l in leaves]
+        for place, (n, around, base, step) in enumerate(places):
+            pair_kernel(targets[n], points_ref, base + leaves[n] + 1 + step, pairs_ref, place)
+        totals = [jnp.zeros((8, LEAF), F32)] * CROSS_TURN
+        for place, (n, around, base, step) in enumerate(places):
+            slot = base + leaves[n] + 1 + step
+            totals[n] += pair_sum(tall_ref[leaves[n] + 1], loads_ref, slot, pairs_ref, place, around, step)
+        for n in range(CROSS_TURN):
+            near_ref[leaves[n]] = own_ref[leaves[n]] + totals[n]
         return 0
 
-    lax.fori_loop(0, LD, leaf, 0)
+    lax.fori_loop(0, LD // CROSS_TURN, turn, 0)
     for l, slot, step in ((0, 2 * TALL, -1), (LD - 1, 2 * TALL + 1, 1)):
         here = tall_ref[l + 1]
         pair_kernel(target_points(here), points_ref, slot, pairs_ref, 0)
@@ -219,7 +265,22 @@
             tail_ref[i - 1] = rows
 
 
-def far_kernel(mask_ref, below_ref, above_ref, far_below_ref, far_above_ref, coupling_ref, basis_ref, own_ref, cross_ref, part_ref):
+def exact_by_last(x, y):
+    return lax.dot_general(x, y, BY_LAST, precision=EXACT, preferred_element_type=F32)
+
+
+def three_by_last(x, y):
+    (xh, xl), (yh, yl) = halves(x), halves(y)
+    xh, xl, yh, yl = (z.astype(BF16) for z in (xh, xl, yh, yl))
+    high = lax.dot_general(xh, yh, BY_LAST, preferred_element_type=F32)
+    cross = lax.dot_general(xl, yh, BY_LAST, preferred_element_type=F32)
+    return high + (cross + lax.dot_general(xh, yl, BY_LAST, preferred_element_type=F32))
+
+
+def finish_kernel(
+    at_ref, mask_ref, admissible_ref, below_ref, above_ref, far_below_ref, far_above_ref, near_ref, every_ref,
+    slab_ref, coupling_ref, top_ref, transfer_ref, basis_ref, out_ref, far_ref,
+):
     held = {-4 + i: below_ref[i] for i in range(3)}
     held |= {2 + i: above_ref[i] for i in range(3)}
     held |= {-6 + i: far_below_ref[i] for i in range(2)}
@@ -232,24 +293,18 @@
         coupling = jnp.concatenate(
             [coupling_ref[3 * q + b] * mask_ref[0, 3 * q + b].astype(F32) for b in range(3)], 0
         )
-        total = total + lax.dot_general(stacked, coupling, BY_LAST, precision=EXACT, preferred_element_type=F32)
+        total = total + three_by_last(stacked, coupling)
     far = []
     for r in range(3):
         block = total[r * ROWS : (r + 1) * ROWS]
-        far.append(
-            block[0:LD, :RANK] + block[1 : LD + 1, RANK : 2 * RANK] + block[2 : LD + 2, 2 * RANK :]
-        )
-        far.append(jnp.zeros((ROWS - LD, RANK), F32))
+        rows = block[0:LD, :RANK] + block[1 : LD + 1, RANK : 2 * RANK] + block[2 : LD + 2, 2 * RANK :]
+        far.append(jnp.concatenate([rows, jnp.zeros((ROWS - LD, RANK), F32)], 0))
+    far.append(jnp.zeros((ROWS, RANK), F32))
     columns = jnp.transpose(jnp.concatenate(far, 0), (1, 0))
-    for l in range(LD):
-        basis = basis_ref[l]
-        for r in range(3):
-            at = r * ROWS + l
-            down = jnp.sum(basis * columns[:, at : at + 1], axis=0, keepdims=True)
-            part_ref[r, l : l + 1, :] = down + own_ref[l, 4 + r : 5 + r, :] + cross_ref[l, 4 + r : 5 + r, :]
-
-
-def downward_kernel(at_ref, admissible_ref, every_ref, top_ref, slab_ref, transfer_ref, basis_ref, part_ref, out_ref):
+    far_columns = [columns[:, r * ROWS : (r + 1) * ROWS] for r in range(3)]
+    for r in range(3):
+        far_ref[r] = jnp.concatenate([far_columns[r], jnp.zeros((RANK, RANK - ROWS), F32)], 1)
+
     here = at_ref[1]
     sectors = top_ref.shape[0]
 
@@ -263,24 +318,49 @@
         return tuple(s + coupling * row for s, row in zip(sums, rows))
 
     nothing = jnp.zeros((RANK, RANK), F32)
-    sums = lax.fori_loop(0, sectors, couple, (nothing,) * 3, unroll=8)
+    sums = lax.fori_loop(0, sectors, couple, (nothing,) * 3, unroll=16)
     lane = lax.broadcasted_iota(jnp.int32, (RANK, 128), 1)
     columns = jnp.zeros((RANK, 128), F32)
     for r in range(3):
         columns = jnp.where(lane == r, jnp.sum(sums[r], axis=1, keepdims=True), columns)
     local = jnp.transpose(columns, (1, 0))[:8]
-    slab = lax.dot_general(local, slab_ref[...], BY_LAST, precision=EXACT, preferred_element_type=F32)
+    slab = exact_by_last(local, slab_ref[...])
+
+    place = lax.broadcasted_iota(jnp.int32, (RANK, RANK), 1)
 
     def leaf(l, _):
         basis = basis_ref[l]
         transfer = transfer_ref[l]
+        near = near_ref[l]
         for r in range(3):
-            column = jnp.sum(transfer * slab[r : r + 1], axis=1, keepdims=True)
-            down = jnp.sum(basis * column, axis=0, keepdims=True)
-            out_ref[r, pl.ds(l, 1), :] = part_ref[r, pl.ds(l, 1), :] + down
+            terms = transfer * slab[r : r + 1] + jnp.where(place == l, far_ref[r], 0.0)
+            column = jnp.sum(terms, axis=1, keepdims=True)
+            out_ref[r, pl.ds(l, 1), :] = jnp.sum(basis * column, axis=0, keepdims=True) + near[4 + r : 5 + r]
         return 0
 
-    lax.fori_loop(0, LD, leaf, 0, unroll=4)
+    lax.fori_loop(0, LD, leaf, 0, unroll=8)
+
+
+def upward(*args):
+    outs = (shaped(LD, 8, LEAF), shaped(8, 8, LEAF + 128))
+    scratch = [pltpu.VMEM(x.shape, F32) for x in args[1:]] + [pltpu.SemaphoreType.DMA((4 + 2 * UP_PARTS,))]
+    return call(upward_kernel, outs, [SMEM] + [HBM] * 6, scratch, flops=10**9, vmem=FULL)(*args)
+
+
+def near_own(wire):
+    scratch = near_scratch(TALL, 3 * OWN_TURN)
+    return call(near_own_kernel, shaped(LD, 8, LEAF), [VMEM], scratch, flops=9 * 10**9)(wire)
+
+
+def near_cross(*args):
+    scratch = near_scratch(2 * TALL + 2, 6 * CROSS_TURN)
+    return call(near_cross_kernel, shaped(LD, 8, LEAF), [VMEM] * 4, scratch, flops=18 * 10**9, bytes=10**8)(*args)
+
+
+def finish(*args):
+    return call(finish_kernel, shaped(RHS, LD, LEAF), [SMEM] * 3 + [VMEM] * 11, [pltpu.VMEM((3, RANK, RANK), F32)], flops=4 * 10**9)(
+        *args
+    )
 
 
 def passed_along(x, axis, by):
@@ -308,13 +388,10 @@
     transfer = transfer[0]
     slab = slab_transfer_matrices[0, 0]
 
-    wire, slots = call(
-        upward_kernel, (shaped(LD, 8, LEAF), shaped(8, 8, LEAF + 128)), [SMEM] + [VMEM] * 6, flops=10**9
-    )(at, values, offsets, stiffness[0], basis, transfer, slab)
+    wire, slots = upward(at, values, offsets, stiffness[0], basis, transfer, slab)
     came = lax.all_to_all(slots, "along", 0, 0, tiled=True)
-    own = call(
-        near_own_kernel, shaped(LD, 8, LEAF), [VMEM], near_scratch(TALL, 3), flops=9 * 10**9
-    )(wire)
+    own = near_own(wire)
+    came, own = lax.optimization_barrier((came, own))
     tall, whole = call(
         joined_kernel, (shaped(TALL, 8, LEAF), shaped(sectors, 2, 128)), [SMEM, VMEM, VMEM], flops=10**8
     )(at, came, wire)
@@ -331,14 +408,10 @@
     above = passed_along(window, "blk", -3)
     far_below = passed_along(head, "blk", 5)
     far_above = passed_along(tail, "blk", -5)
-    cross = call(
-        near_cross_kernel, shaped(LD, 8, LEAF), [VMEM] * 3, near_scratch(2 * TALL + 2, 6), flops=18 * 10**9
-    )(tall, lower, upper)
-    part = call(far_kernel, shaped(RHS, LD, LEAF), [SMEM] + [VMEM] * 8, flops=2 * 10**9)(
-        leaf_admissible_mask, below, above, far_below, far_above, leaf_coupling_matrices[0], basis, own, cross
-    )
-    out = call(downward_kernel, shaped(RHS, LD, LEAF), [SMEM] * 2 + [VMEM] * 6, flops=2 * 10**9)(
-        at, top_admissible, every, top_coupling[0], slab, transfer, basis, part
+    near = near_cross(tall, lower, upper, own)
+    out = finish(
+        at, leaf_admissible_mask, top_admissible, below, above, far_below, far_above, near, every,
+        slab, leaf_coupling_matrices[0], top_coupling[0], transfer, basis,
     )
     return out[:, None]
 

time: 101 us -> 85.8 us (0.85)
  the two profiles are of different devices: /device:TPU:1 before, /device:TPU:16 now
where the time goes in v2:
time: 85.8 us; the launch traced here: 85.2 us
  starting transfers between devices  46.7 us (54%)
  Pallas kernels  30.3 us (35%)
  local copies, waits for them, and re-layouts  7.24 us (8%)
    ppermute x6, starting transfers between devices, passed_along(): return lax.ppermute(x, axis, [(i, (i + by) % count) for i in range(count)])  29.3 us
    pallas_call x1, Pallas kernels, near_cross(): call(near_cross_kernel, shaped(LD, 8, LEAF), [VMEM] * 4, scratch, flops=1...  14.4 us
    all_to_all x1, starting transfers between devices, body(): came = lax.all_to_all(slots, 'along', 0, 0, tiled=True)  8.98 us
    all_to_all x1, starting transfers between devices, body(): every = lax.all_to_all(whole, 'blk', 0, 0, tiled=True)  8.47 us
    unnamed x28, local copies, waits for them, and re-layouts  7.24 us
    pallas_call x1, Pallas kernels, near_own(): call(near_own_kernel, shaped(LD, 8, LEAF), [VMEM], scratch, flops=9 * 10...  6.57 us
    pallas_call x1, Pallas kernels, finish(): call(finish_kernel, shaped(RHS, LD, LEAF), [SMEM] * 3 + [VMEM] * 11, [plt...  4.34 us
    pallas_call x1, Pallas kernels, upward(): call(upward_kernel, outs, [SMEM] + [HBM] * 6, scratch, flops=10 ** 9, vme...  3.75 us
  transfers between devices with their start and end apart: 8, of which 0 were waited for; matrix products, arithmetic and copies ran while one was open for 0% of the time, Pallas kernels for 25%

profile of v2, /device:TPU:16, one launch (start us, length us, event | category | flops | bytes accessed | tf_op | source)
XLA Modules:
  0.0 85.2 jit_solution(3907134247211294968)
XLA Ops:
  0.0 0.6 pad_add_fusion.at_ref
  0.6 3.7 %shard_map.100 = (f32[24,8,256]{2,1,0:T(8,128)}, f32[8,8,384]{2,1,0:T(8,128)}) custom-call(s32[2]{0:T(128)} %pad_add_fusion.at_ref, f32[3,24,256]{2,1,0:T(8,128)} %bitcast.21, f32[3,24,256]{2,1,0:T(8,128)} %bitcast.22, f32[24,256]{1,0:T(8,128)} %bitcast.23, f32[24,64,256]{2,1,0:T(8,128)} %bitcast.14, f32[24,64,64]{2,1,0:T(8,128)} %bitcast.17, f32[64,64]{1,0:T(8,128)} %bitcast.19), custom_call_target="tpu_custom_call" | custom-call | flops 1000000000 | bytes 1048576 | tf_op jit(solution)/shard_map/pallas_call | solution.py:347
  4.4 9.0 %all-to-all-start = ((f32[8,8,384]{2,1,0:T(8,128)}), f32[8,8,384]{2,1,0:T(8,128)S(1)}, u32[]{:S(2)}, u32[]{:S(2)}) async-start(f32[8,8,384]{2,1,0:T(8,128)} %get-tuple-element.14), calls=%async_computation | async-start | bytes 196608 | tf_op jit(solution)/shard_map/all_to_all | solution.py:392
  13.4 0.0 copy-start.8
  13.4 0.9 %copy-done.8 = f32[24,8,256]{2,1,0:T(8,128)S(1)} copy-done((f32[24,8,256]{2,1,0:T(8,128)S(1)}, f32[24,8,256]{2,1,0:T(8,128)}, u32[]{:S(2)}) %copy-start.8) | copy-done | bytes 196632
  14.3 0.0 copy-start.7
  14.3 0.0 copy-start.9
  14.3 6.6 %shard_map.101.own_ref = f32[24,8,256]{2,1,0:T(8,128)S(1)} custom-call(f32[24,8,256]{2,1,0:T(8,128)S(1)} %copy-done.8), custom_call_target="tpu_custom_call" | custom-call | flops 8999999488 | bytes 1048576 | tf_op jit(solution)/shard_map/pallas_call | solution.py:352
  20.9 0.0 copy-start.12
  20.9 0.0 all-to-all-done.came_ref
  20.9 0.0 copy-done.7
  20.9 0.0 copy-done.9
  20.9 1.3 %shard_map.102 = (f32[26,8,256]{2,1,0:T(8,128)S(1)}, f32[64,2,128]{2,1,0:T(2,128)}) custom-call(s32[2]{0:T(128)S(1)} %copy-done.7, f32[8,8,384]{2,1,0:T(8,128)S(1)} %all-to-all-done.came_ref, f32[24,8,256]{2,1,0:T(8,128)S(1)} %copy-done.9), custom_call_target="tpu_custom_call" | custom-call | flops 100000000 | bytes 1048576 | tf_op jit(solution)/shard_map/pallas_call | solution.py:395
  22.2 0.0 copy-done.12
  22.2 9.3 %collective-permute-start.1 = (f32[26,8,256]{2,1,0:T(8,128)S(1)}, f32[26,8,256]{2,1,0:T(8,128)S(1)}, u32[]{:S(2)}, u32[]{:S(2)}) collective-permute-start(f32[26,8,256]{2,1,0:T(8,128)S(1)} %get-tuple-element.17.tall_ref), channel_id=1, source_target_pairs={{0,504},{8,0},{16,8},{24,16},{32,24},{40,32},{48,40},{56,48},{64,5... | collective-permute-start | bytes 638984 | tf_op jit(solution)/shard_map/ppermute | solution.py:368
  31.5 1.9 %collective-permute-start = (f32[26,8,256]{2,1,0:T(8,128)S(1)}, f32[26,8,256]{2,1,0:T(8,128)S(1)}, u32[]{:S(2)}, u32[]{:S(2)}) collective-permute-start(f32[26,8,256]{2,1,0:T(8,128)S(1)} %get-tuple-element.17.tall_ref), channel_id=1, source_target_pairs={{0,8},{8,16},{16,24},{24,32},{32,40},{40,48},{48,56},{56,64},{64,7... | collective-permute-start | bytes 638984 | tf_op jit(solution)/shard_map/ppermute | solution.py:368
  33.4 8.5 %all-to-all-start.1 = ((f32[64,2,128]{2,1,0:T(2,128)}), f32[64,2,128]{2,1,0:T(2,128)S(1)}, u32[]{:S(2)}, u32[]{:S(2)}) async-start(f32[64,2,128]{2,1,0:T(2,128)} %get-tuple-element.22), calls=%async_computation.1 | async-start | bytes 131072 | tf_op jit(solution)/shard_map/all_to_all | solution.py:400
  41.9 0.0 collective-permute-done.1.upper_ref
  41.9 0.0 collective-permute-done.lower_ref
  42.0 6.5 %collective-permute-start.3 = (f32[3,32,256]{2,1,0:T(8,128)S(1)}, f32[3,32,256]{2,1,0:T(8,128)S(1)}, u32[]{:S(2)}, u32[]{:S(2)}) collective-permute-start(f32[3,32,256]{2,1,0:T(8,128)S(1)} %get-tuple-element.18), channel_id=1, source_target_pairs={{0,488},{8,496},{16,504},{24,0},{32,8},{40,16},{48,24},{56,32},{64... | collective-permute-start | bytes 294920 | tf_op jit(solution)/shard_map/ppermute | solution.py:368
  48.5 1.9 %collective-permute-start.2 = (f32[3,32,256]{2,1,0:T(8,128)S(1)}, f32[3,32,256]{2,1,0:T(8,128)S(1)}, u32[]{:S(2)}, u32[]{:S(2)}) collective-permute-start(f32[3,32,256]{2,1,0:T(8,128)S(1)} %get-tuple-element.18), channel_id=1, source_target_pairs={{0,24},{8,32},{16,40},{24,48},{32,56},{40,64},{48,72},{56,80},{64,... | collective-permute-start | bytes 294920 | tf_op jit(solution)/shard_map/ppermute | solution.py:368
  50.4 3.4 %collective-permute-start.4 = (f32[2,32,256]{2,1,0:T(8,128)S(1)}, f32[2,32,256]{2,1,0:T(8,128)S(1)}, u32[]{:S(2)}, u32[]{:S(2)}) collective-permute-start(f32[2,32,256]{2,1,0:T(8,128)S(1)} %get-tuple-element.19), channel_id=1, source_target_pairs={{0,40},{8,48},{16,56},{24,64},{32,72},{40,80},{48,88},{56,96},{64,... | collective-permute-start | bytes 196616 | tf_op jit(solution)/shard_map/ppermute | solution.py:368
  53.8 0.0 copy-start
  53.8 0.0 copy-start.4
  53.8 0.0 copy-start.5
  53.8 0.0 copy-start.6
  53.9 6.2 %collective-permute-start.5 = (f32[2,32,256]{2,1,0:T(8,128)S(1)}, f32[2,32,256]{2,1,0:T(8,128)S(1)}, u32[]{:S(2)}, u32[]{:S(2)}) collective-permute-start(f32[2,32,256]{2,1,0:T(8,128)S(1)} %get-tuple-element.20), channel_id=1, source_target_pairs={{0,472},{8,480},{16,488},{24,496},{32,504},{40,0},{48,8},{56,16},{... | collective-permute-start | bytes 196616 | tf_op jit(solution)/shard_map/ppermute | solution.py:368
  60.1 0.0 copy-start.13
  60.1 0.9 %copy-done.13 = f32[24,8,256]{2,1,0:T(8,128)S(1)} copy-done((f32[24,8,256]{2,1,0:T(8,128)S(1)}, f32[24,8,256]{2,1,0:T(8,128)}, u32[]{:S(2)}) %copy-start.13) | copy-done | bytes 196632
  61.0 14.4 %shard_map.104.near_ref = f32[24,8,256]{2,1,0:T(8,128)S(1)} custom-call(f32[26,8,256]{2,1,0:T(8,128)S(1)} %get-tuple-element.17.tall_ref, f32[26,8,256]{2,1,0:T(8,128)S(1)} %collective-permute-done.lower_ref, f32[26,8,256]{2,1,0:T(8,128)S(1)} %collective-permute-done.1.upper_ref, f32[24,8,256]{2,1,0:T(8,128)S(1)} %copy-done.13), custom_call_target="tpu_custom_call" | custom-call | flops 17999998976 | bytes 100000000 | tf_op jit(solution)/shard_map/pallas_call | solution.py:357
  75.4 0.0 copy-start.10
  75.4 0.7 copy-done.10
  76.1 0.0 all-to-all-done.1.every_ref
  76.1 0.0 collective-permute-done.4.far_below_ref
  76.1 0.0 collective-permute-done.5.far_above_ref
  76.1 0.0 collective-permute-done.3.above_ref
  76.1 0.0 collective-permute-done.2.below_ref
  76.1 0.0 copy-done
  76.2 0.0 copy-done.4
  76.2 0.0 copy-done.5
  76.2 0.0 copy-done.6
  76.2 0.0 copy-start.1
  76.2 1.4 %copy-done.1 = f32[1,24,64,256]{3,2,1,0:T(8,128)S(1)} copy-done((f32[1,24,64,256]{3,2,1,0:T(8,128)S(1)}, f32[1,24,64,256]{3,2,1,0:T(8,128)}, u32[]{:S(2)}) %copy-start.1) | copy-done | bytes 1572888
  77.6 0.0 copy-start.2
  77.6 1.2 %copy-done.2 = f32[1,30,64,64]{3,2,1,0:T(8,128)S(1)} copy-done((f32[1,30,64,64]{3,2,1,0:T(8,128)S(1)}, f32[1,30,64,64]{3,2,1,0:T(8,128)}, u32[]{:S(2)}) %copy-start.2) | copy-done | bytes 491544
  78.8 0.0 copy-start.3
  78.8 1.1 %copy-done.3 = f32[1,24,64,64]{3,2,1,0:T(8,128)S(1)} copy-done((f32[1,24,64,64]{3,2,1,0:T(8,128)S(1)}, f32[1,24,64,64]{3,2,1,0:T(8,128)}, u32[]{:S(2)}) %copy-start.3) | copy-done | bytes 393240
  79.9 0.0 copy-start.11
  79.9 0.9 %copy-done.11 = f32[24,8,256]{2,1,0:T(8,128)S(1)} copy-done((f32[24,8,256]{2,1,0:T(8,128)S(1)}, f32[24,8,256]{2,1,0:T(8,128)}, u32[]{:S(2)}) %copy-start.11) | copy-done | bytes 196632
  80.9 4.3 %shard_map.105 = f32[3,24,256]{2,1,0:T(8,128)} custom-call(s32[2]{0:T(128)S(1)} %copy-done.7, s32[1,30]{1,0:T(1,128)S(1)} %copy-done.5, s32[1,64]{1,0:T(1,128)S(1)} %copy-done.6, f32[3,32,256]{2,1,0:T(8,128)S(1)} %collective-permute-done.2.below_ref, f32[3,32,256]{2,1,0:T(8,128)S(1)} %collective-permute-done.3.above_ref, ...), custom_call_target="tpu_custom_call" | custom-call | flops 4000000000 | bytes 1048576 | tf_op jit(solution)/shard_map/pallas_call | solution.py:361
  (1 shorter events, 0.0 us)
Async XLA Ops:
  4.4 16.5 %all-to-all-start = ((f32[8,8,384]{2,1,0:T(8,128)}), f32[8,8,384]{2,1,0:T(8,128)S(1)}, u32[]{:S(2)}, u32[]{:S(2)}) async-start(f32[8,8,384]{2,1,0:T(8,128)} %get-tuple-element.14), calls=%async_computation | async-start | bytes 196608 | tf_op jit(solution)/shard_map/all_to_all | solution.py:392
  13.4 0.9 %copy-start.8 = (f32[24,8,256]{2,1,0:T(8,128)S(1)}, f32[24,8,256]{2,1,0:T(8,128)}, u32[]{:S(2)}) copy-start(f32[24,8,256]{2,1,0:T(8,128)} %get-tuple-element.15.wire_ref) | copy-start | bytes 589828
  14.3 6.6 %copy-start.7 = (s32[2]{0:T(128)S(1)}, s32[2]{0:T(128)}, u32[]{:S(2)}) copy-start(s32[2]{0:T(128)} %pad_add_fusion.at_ref) | copy-start | bytes 28
  14.3 6.6 %copy-start.9 = (f32[24,8,256]{2,1,0:T(8,128)S(1)}, f32[24,8,256]{2,1,0:T(8,128)}, u32[]{:S(2)}) copy-start(f32[24,8,256]{2,1,0:T(8,128)} %get-tuple-element.15.wire_ref) | copy-start | bytes 589828
  20.9 1.3 %copy-start.12 = (f32[24,8,256]{2,1,0:T(8,128)}, f32[24,8,256]{2,1,0:T(8,128)S(1)}, u32[]{:S(2)}) copy-start(f32[24,8,256]{2,1,0:T(8,128)S(1)} %shard_map.101.own_ref) | copy-start | bytes 589828
  22.2 19.7 %collective-permute-start.1 = (f32[26,8,256]{2,1,0:T(8,128)S(1)}, f32[26,8,256]{2,1,0:T(8,128)S(1)}, u32[]{:S(2)}, u32[]{:S(2)}) collective-permute-start(f32[26,8,256]{2,1,0:T(8,128)S(1)} %get-tuple-element.17.tall_ref), channel_id=1, source_target_pairs={{0,504},{8,0},{16,8},{24,16},{32,24},{40,32},{48,40},{56,48},{64,5... | collective-permute-start | bytes 638984 | tf_op jit(solution)/shard_map/ppermute | solution.py:368
  31.5 10.4 %collective-permute-start = (f32[26,8,256]{2,1,0:T(8,128)S(1)}, f32[26,8,256]{2,1,0:T(8,128)S(1)}, u32[]{:S(2)}, u32[]{:S(2)}) collective-permute-start(f32[26,8,256]{2,1,0:T(8,128)S(1)} %get-tuple-element.17.tall_ref), channel_id=1, source_target_pairs={{0,8},{8,16},{16,24},{24,32},{32,40},{40,48},{48,56},{56,64},{64,7... | collective-permute-start | bytes 638984 | tf_op jit(solution)/shard_map/ppermute | solution.py:368
  33.4 42.7 %all-to-all-start.1 = ((f32[64,2,128]{2,1,0:T(2,128)}), f32[64,2,128]{2,1,0:T(2,128)S(1)}, u32[]{:S(2)}, u32[]{:S(2)}) async-start(f32[64,2,128]{2,1,0:T(2,128)} %get-tuple-element.22), calls=%async_computation.1 | async-start | bytes 131072 | tf_op jit(solution)/shard_map/all_to_all | solution.py:400
  42.0 34.2 %collective-permute-start.3 = (f32[3,32,256]{2,1,0:T(8,128)S(1)}, f32[3,32,256]{2,1,0:T(8,128)S(1)}, u32[]{:S(2)}, u32[]{:S(2)}) collective-permute-start(f32[3,32,256]{2,1,0:T(8,128)S(1)} %get-tuple-element.18), channel_id=1, source_target_pairs={{0,488},{8,496},{16,504},{24,0},{32,8},{40,16},{48,24},{56,32},{64... | collective-permute-start | bytes 294920 | tf_op jit(solution)/shard_map/ppermute | solution.py:368
  48.5 27.6 %collective-permute-start.2 = (f32[3,32,256]{2,1,0:T(8,128)S(1)}, f32[3,32,256]{2,1,0:T(8,128)S(1)}, u32[]{:S(2)}, u32[]{:S(2)}) collective-permute-start(f32[3,32,256]{2,1,0:T(8,128)S(1)} %get-tuple-element.18), channel_id=1, source_target_pairs={{0,24},{8,32},{16,40},{24,48},{32,56},{40,64},{48,72},{56,80},{64,... | collective-permute-start | bytes 294920 | tf_op jit(solution)/shard_map/ppermute | solution.py:368
  50.4 25.7 %collective-permute-start.4 = (f32[2,32,256]{2,1,0:T(8,128)S(1)}, f32[2,32,256]{2,1,0:T(8,128)S(1)}, u32[]{:S(2)}, u32[]{:S(2)}) collective-permute-start(f32[2,32,256]{2,1,0:T(8,128)S(1)} %get-tuple-element.19), channel_id=1, source_target_pairs={{0,40},{8,48},{16,56},{24,64},{32,72},{40,80},{48,88},{56,96},{64,... | collective-permute-start | bytes 196616 | tf_op jit(solution)/shard_map/ppermute | solution.py:368
  53.8 22.3 %copy-start = (f32[1,64,64,64]{3,2,1,0:T(8,128)S(1)}, f32[1,64,64,64]{3,2,1,0:T(8,128)}, u32[]{:S(2)}) copy-start(f32[1,64,64,64]{3,2,1,0:T(8,128)} %param.18) | copy-start | bytes 3145732
  53.8 22.3 %copy-start.4 = (f32[1,1,64,64]{3,2,1,0:T(8,128)S(1)}, f32[1,1,64,64]{3,2,1,0:T(8,128)}, u32[]{:S(2)}) copy-start(f32[1,1,64,64]{3,2,1,0:T(8,128)} %param.15) | copy-start | bytes 49156
  53.8 22.3 %copy-start.5 = (s32[1,30]{1,0:T(1,128)S(1)}, s32[1,30]{1,0:T(1,128)}, u32[]{:S(2)}) copy-start(s32[1,30]{1,0:T(1,128)} %mask_ref.1) | copy-start | bytes 364
  53.8 22.3 %copy-start.6 = (s32[1,64]{1,0:T(1,128)S(1)}, s32[1,64]{1,0:T(1,128)}, u32[]{:S(2)}) copy-start(s32[1,64]{1,0:T(1,128)} %admissible_ref.1) | copy-start | bytes 772
  53.9 22.3 %collective-permute-start.5 = (f32[2,32,256]{2,1,0:T(8,128)S(1)}, f32[2,32,256]{2,1,0:T(8,128)S(1)}, u32[]{:S(2)}, u32[]{:S(2)}) collective-permute-start(f32[2,32,256]{2,1,0:T(8,128)S(1)} %get-tuple-element.20), channel_id=1, source_target_pairs={{0,472},{8,480},{16,488},{24,496},{32,504},{40,0},{48,8},{56,16},{... | collective-permute-start | bytes 196616 | tf_op jit(solution)/shard_map/ppermute | solution.py:368
  60.1 0.9 %copy-start.13 = (f32[24,8,256]{2,1,0:T(8,128)S(1)}, f32[24,8,256]{2,1,0:T(8,128)}, u32[]{:S(2)}) copy-start(f32[24,8,256]{2,1,0:T(8,128)} %copy-done.12) | copy-start | bytes 589828
  75.4 0.7 copy-start.10
  76.2 1.4 %copy-start.1 = (f32[1,24,64,256]{3,2,1,0:T(8,128)S(1)}, f32[1,24,64,256]{3,2,1,0:T(8,128)}, u32[]{:S(2)}) copy-start(f32[1,24,64,256]{3,2,1,0:T(8,128)} %param.13) | copy-start | bytes 4718596
  77.6 1.2 %copy-start.2 = (f32[1,30,64,64]{3,2,1,0:T(8,128)S(1)}, f32[1,30,64,64]{3,2,1,0:T(8,128)}, u32[]{:S(2)}) copy-start(f32[1,30,64,64]{3,2,1,0:T(8,128)} %param.16) | copy-start | bytes 1474564
  78.8 1.1 %copy-start.3 = (f32[1,24,64,64]{3,2,1,0:T(8,128)S(1)}, f32[1,24,64,64]{3,2,1,0:T(8,128)}, u32[]{:S(2)}) copy-start(f32[1,24,64,64]{3,2,1,0:T(8,128)} %param.14) | copy-start | bytes 1179652
  79.9 0.9 %copy-start.11 = (f32[24,8,256]{2,1,0:T(8,128)S(1)}, f32[24,8,256]{2,1,0:T(8,128)}, u32[]{:S(2)}) copy-start(f32[24,8,256]{2,1,0:T(8,128)} %copy-done.10) | copy-start | bytes 589828

commit v3 on v2

--- a/solution.py
+++ b/solution.py
@@ -28,7 +28,7 @@
 MIB = 2**20
 FULL = 60 * MIB + 128 * 1024
 OWN_TURN = 3
-CROSS_TURN = 2
+GROUP = 8
 UP_PARTS = 4
 UP_LEAVES = LD // UP_PARTS
 
@@ -125,24 +125,29 @@
         slots_ref[j, :, LEAF:] = share
 
 
-def joined_kernel(at_ref, came_ref, wire_ref, tall_ref, whole_ref):
+def joined_kernel(at_ref, came_ref, wire_ref, tall_ref, rows_ref):
     here = at_ref[0]
     total = came_ref[0, :, LEAF:]
     for j in range(1, 8):
         total = total + came_ref[j, :, LEAF:]
-    packed = jnp.concatenate(
-        [
-            jnp.concatenate([total[0:1, :RANK], total[1:2, :RANK]], 1),
-            jnp.concatenate([total[2:3, :RANK], jnp.zeros((1, RANK), F32)], 1),
-        ],
-        0,
-    )
-    whole_ref[...] = jnp.broadcast_to(packed[None], whole_ref.shape)
     lower = came_ref[jnp.maximum(here - 1, 0), :, :LEAF]
     upper = came_ref[jnp.minimum(here + 1, 7), :, :LEAF]
     tall_ref[0] = jnp.where(here > 0, lower, 0.0)
     tall_ref[1 : LD + 1] = wire_ref[...]
     tall_ref[LD + 1] = jnp.where(here < 7, upper, 0.0)
+    share = jnp.concatenate([total[r : r + 1, :RANK] for r in range(3)] + [jnp.zeros((1, RANK), F32)], 1)
+    rows = jnp.concatenate(
+        [tall_ref[l, 7:8, :] for l in range(TALL)] + [share, jnp.zeros((ROWS - TALL - 1, LEAF), F32)], 0
+    )
+    for j in range(GROUP):
+        rows_ref[j] = rows
+
+
+def group_kernel(group_ref, low_ref, high_ref, shares_ref):
+    low_ref[...] = group_ref[GROUP - REACH :]
+    high_ref[...] = group_ref[:REACH]
+    shares = jnp.concatenate([group_ref[j, TALL : TALL + 1, :] for j in range(GROUP)], 0)
+    shares_ref[...] = jnp.broadcast_to(shares[None], shares_ref.shape)
 
 
 def source_side(leaf, around, steps, slot, points_ref, loads_ref):
@@ -208,41 +213,33 @@
     lax.fori_loop(0, LD // OWN_TURN, turn, 0)
 
 
-def near_cross_kernel(tall_ref, lower_ref, upper_ref, own_ref, near_ref, points_ref, loads_ref, pairs_ref):
-    for around, came_ref, base in ((-1, lower_ref, 0), (1, upper_ref, TALL)):
-
-        def prepare(l, _, around=around, came_ref=came_ref, base=base):
-            source_side(came_ref[l], around, (-1, 0, 1), base + l, points_ref, loads_ref)
-            return 0
-
-        lax.fori_loop(0, TALL, prepare, 0, unroll=13)
-    source_side(tall_ref[0], 0, (-1,), 2 * TALL, points_ref, loads_ref)
-    source_side(tall_ref[LD + 1], 0, (1,), 2 * TALL + 1, points_ref, loads_ref)
+def near_side_kernel(around, tall_ref, came_ref, before_ref, near_ref, points_ref, loads_ref, pairs_ref):
+    def prepare(l, _):
+        source_side(came_ref[l], around, (-1, 0, 1), l, points_ref, loads_ref)
+        return 0
+
+    lax.fori_loop(0, TALL, prepare, 0, unroll=13)
 
     def turn(g, _):
-        leaves = [g * CROSS_TURN + n for n in range(CROSS_TURN)]
-        places = [
-            (n, around, base, step)
-            for n in range(CROSS_TURN)
-            for around, base in ((-1, 0), (1, TALL))
-            for step in (-1, 0, 1)
-        ]
+        leaves = [g * OWN_TURN + n for n in range(OWN_TURN)]
+        places = [(n, step) for n in range(OWN_TURN) for step in (-1, 0, 1)]
         targets = [target_points(tall_ref[l + 1]) for l in leaves]
-        for place, (n, around, base, step) in enumerate(places):
-            pair_kernel(targets[n], points_ref, base + leaves[n] + 1 + step, pairs_ref, place)
-        totals = [jnp.zeros((8, LEAF), F32)] * CROSS_TURN
-        for place, (n, around, base, step) in enumerate(places):
-            slot = base + leaves[n] + 1 + step
+        for place, (n, step) in enumerate(places):
+            pair_kernel(targets[n], points_ref, leaves[n] + 1 + step, pairs_ref, place)
+        totals = [before_ref[l] for l in leaves]
+        for place, (n, step) in enumerate(places):
+            slot = leaves[n] + 1 + step
             totals[n] += pair_sum(tall_ref[leaves[n] + 1], loads_ref, slot, pairs_ref, place, around, step)
-        for n in range(CROSS_TURN):
-            near_ref[leaves[n]] = own_ref[leaves[n]] + totals[n]
-        return 0
-
-    lax.fori_loop(0, LD // CROSS_TURN, turn, 0)
-    for l, slot, step in ((0, 2 * TALL, -1), (LD - 1, 2 * TALL + 1, 1)):
-        here = tall_ref[l + 1]
-        pair_kernel(target_points(here), points_ref, slot, pairs_ref, 0)
-        near_ref[l] += pair_sum(here, loads_ref, slot, pairs_ref, 0, 0, step)
+        for n in range(OWN_TURN):
+            near_ref[leaves[n]] = totals[n]
+        return 0
+
+    lax.fori_loop(0, LD // OWN_TURN, turn, 0)
+    end, l, step = ((0, 0, -1), None, (LD + 1, LD - 1, 1))[around + 1]
+    here = tall_ref[l + 1]
+    source_side(tall_ref[end], 0, (step,), TALL, points_ref, loads_ref)
+    pair_kernel(target_points(here), points_ref, TALL, pairs_ref, 0)
+    near_ref[l] += pair_sum(here, loads_ref, TALL, pairs_ref, 0, 0, step)
 
 
 def near_scratch(leaves, places):
@@ -253,18 +250,6 @@
     ]
 
 
-def window_kernel(lower_ref, tall_ref, upper_ref, window_ref, head_ref, tail_ref):
-    for i, came_ref in enumerate((lower_ref, tall_ref, upper_ref)):
-        rows = jnp.concatenate(
-            [came_ref[l, 7:8, :] for l in range(TALL)] + [jnp.zeros((ROWS - TALL, LEAF), F32)], 0
-        )
-        window_ref[i] = rows
-        if i < 2:
-            head_ref[i] = rows
-        if i > 0:
-            tail_ref[i - 1] = rows
-
-
 def exact_by_last(x, y):
     return lax.dot_general(x, y, BY_LAST, precision=EXACT, preferred_element_type=F32)
 
@@ -278,17 +263,18 @@
 
 
 def finish_kernel(
-    at_ref, mask_ref, admissible_ref, below_ref, above_ref, far_below_ref, far_above_ref, near_ref, every_ref,
-    slab_ref, coupling_ref, top_ref, transfer_ref, basis_ref, out_ref, far_ref,
+    at_ref, mask_ref, admissible_ref, group_ref, below_ref, above_ref, near_ref, every_ref,
+    slab_ref, coupling_ref, top_ref, transfer_ref, basis_ref, out_ref, far_ref, ring_ref,
 ):
-    held = {-4 + i: below_ref[i] for i in range(3)}
-    held |= {2 + i: above_ref[i] for i in range(3)}
-    held |= {-6 + i: far_below_ref[i] for i in range(2)}
-    held |= {5 + i: far_above_ref[i] for i in range(2)}
+    ring_ref[:REACH] = below_ref[...]
+    ring_ref[REACH : REACH + GROUP] = group_ref[...]
+    ring_ref[REACH + GROUP :] = above_ref[...]
+    here = at_ref[1]
+    member = lax.rem(here, GROUP)
     total = jnp.zeros((3 * ROWS, 3 * RANK), F32)
     for q in range(2 * (REACH - 1)):
         around = q + 2 if q < REACH - 1 else 3 - q
-        rows = held[around]
+        rows = ring_ref[member + (REACH + around)]
         stacked = jnp.concatenate([rows[:, r * RANK : (r + 1) * RANK] for r in range(3)], 0)
         coupling = jnp.concatenate(
             [coupling_ref[3 * q + b] * mask_ref[0, 3 * q + b].astype(F32) for b in range(3)], 0
@@ -305,7 +291,6 @@
     for r in range(3):
         far_ref[r] = jnp.concatenate([far_columns[r], jnp.zeros((RANK, RANK - ROWS), F32)], 1)
 
-    here = at_ref[1]
     sectors = top_ref.shape[0]
 
     def couple(t, sums):
@@ -313,9 +298,8 @@
         distant = jnp.logical_and(apart > REACH, apart < sectors - REACH)
         allowed = jnp.where(distant, admissible_ref[0, t], 0).astype(F32)
         coupling = top_ref[t]
-        both = every_ref[t] * allowed
-        rows = (both[0:1, :RANK], both[0:1, RANK:], both[1:2, :RANK])
-        return tuple(s + coupling * row for s, row in zip(sums, rows))
+        row = every_ref[pl.ds(t, 1), :] * allowed
+        return tuple(s + coupling * row[:, r * RANK : (r + 1) * RANK] for r, s in enumerate(sums))
 
     nothing = jnp.zeros((RANK, RANK), F32)
     sums = lax.fori_loop(0, sectors, couple, (nothing,) * 3, unroll=16)
@@ -352,15 +336,16 @@
     return call(near_own_kernel, shaped(LD, 8, LEAF), [VMEM], scratch, flops=9 * 10**9)(wire)
 
 
-def near_cross(*args):
-    scratch = near_scratch(2 * TALL + 2, 6 * CROSS_TURN)
-    return call(near_cross_kernel, shaped(LD, 8, LEAF), [VMEM] * 4, scratch, flops=18 * 10**9, bytes=10**8)(*args)
+def near_side(around, *args):
+    kernel = functools.partial(near_side_kernel, around)
+    scratch = near_scratch(TALL + 1, 3 * OWN_TURN)
+    cost = 10**8 if around < 0 else 20 * 10**6
+    return call(kernel, shaped(LD, 8, LEAF), [VMEM] * 3, scratch, flops=90 * cost, bytes=cost)(*args)
 
 
 def finish(*args):
-    return call(finish_kernel, shaped(RHS, LD, LEAF), [SMEM] * 3 + [VMEM] * 11, [pltpu.VMEM((3, RANK, RANK), F32)], flops=4 * 10**9)(
-        *args
-    )
+    scratch = [pltpu.VMEM((3, RANK, RANK), F32), pltpu.VMEM((GROUP + 2 * REACH, ROWS, LEAF), F32)]
+    return call(finish_kernel, shaped(RHS, LD, LEAF), [SMEM] * 3 + [VMEM] * 10, scratch, flops=4 * 10**9)(*args)
 
 
 def passed_along(x, axis, by):
@@ -392,25 +377,28 @@
     came = lax.all_to_all(slots, "along", 0, 0, tiled=True)
     own = near_own(wire)
     came, own = lax.optimization_barrier((came, own))
-    tall, whole = call(
-        joined_kernel, (shaped(TALL, 8, LEAF), shaped(sectors, 2, 128)), [SMEM, VMEM, VMEM], flops=10**8
+    tall, rows = call(
+        joined_kernel, (shaped(TALL, 8, LEAF), shaped(GROUP, ROWS, LEAF)), [SMEM, VMEM, VMEM], flops=10**8
     )(at, came, wire)
+    beside = [[g * GROUP + j for j in range(GROUP)] for g in range(sectors // GROUP)]
+    across = [[g * GROUP + j for g in range(sectors // GROUP)] for j in range(GROUP)]
+    group = lax.all_to_all(rows, "blk", 0, 0, tiled=True, axis_index_groups=beside)
     lower = passed_along(tall, "blk", 1)
     upper = passed_along(tall, "blk", -1)
-    every = lax.all_to_all(whole, "blk", 0, 0, tiled=True)
-    window, head, tail = call(
-        window_kernel,
-        (shaped(3, ROWS, LEAF), shaped(2, ROWS, LEAF), shaped(2, ROWS, LEAF)),
-        [VMEM] * 3,
+    low, high, shares = call(
+        group_kernel,
+        (shaped(REACH, ROWS, LEAF), shaped(REACH, ROWS, LEAF), shaped(sectors // GROUP, GROUP, LEAF)),
+        [VMEM],
         flops=10**8,
-    )(lower, tall, upper)
-    below = passed_along(window, "blk", 3)
-    above = passed_along(window, "blk", -3)
-    far_below = passed_along(head, "blk", 5)
-    far_above = passed_along(tail, "blk", -5)
-    near = near_cross(tall, lower, upper, own)
+    )(group)
+    below = passed_along(low, "blk", GROUP)
+    above = passed_along(high, "blk", -GROUP)
+    every = lax.all_to_all(shares, "blk", 0, 0, tiled=True, axis_index_groups=across)
+    near = near_side(-1, tall, lower, own)
+    every, upper, near = lax.optimization_barrier((every, upper, near))
+    near = near_side(1, tall, upper, near)
     out = finish(
-        at, leaf_admissible_mask, top_admissible, below, above, far_below, far_above, near, every,
+        at, leaf_admissible_mask, top_admissible, group, below, above, near, every.reshape(sectors, LEAF),
         slab, leaf_coupling_matrices[0], top_coupling[0], transfer, basis,
     )
     return out[:, None]

time: 85.8 us -> 87.2 us (1.016)
  the two profiles are of different devices: /device:TPU:16 before, /device:TPU:1 now
where the time goes in v3:
time: 87.2 us; the launch traced here: 86.6 us
  starting transfers between devices  42.5 us (49%)
  Pallas kernels  34.1 us (39%)
  waiting for transfers between devices  6.51 us (7%)
  local copies, waits for them, and re-layouts  2.73 us (3%)
    pallas_call x2, Pallas kernels, near_side(): call(kernel, shaped(LD, 8, LEAF), [VMEM] * 3, scratch, flops=90 * cost, b...  16.7 us
    ppermute x4, starting transfers between devices, passed_along(): return lax.ppermute(x, axis, [(i, (i + by) % count) for i in range(count)])  15.5 us
    all_to_all x1, starting transfers between devices, body(): lax.all_to_all(shares, 'blk', 0, 0, tiled=True, axis_index_groups=across)  12.4 us
    all_to_all x1, starting transfers between devices, body(): came = lax.all_to_all(slots, 'along', 0, 0, tiled=True)  7.49 us
    all_to_all x1, starting transfers between devices, body(): lax.all_to_all(rows, 'blk', 0, 0, tiled=True, axis_index_groups=beside)  7.1 us
    pallas_call x1, Pallas kernels, near_own(): call(near_own_kernel, shaped(LD, 8, LEAF), [VMEM], scratch, flops=9 * 10...  6.59 us
    pallas_call x1, Pallas kernels, finish(): call(finish_kernel, shaped(RHS, LD, LEAF), [SMEM] * 3 + [VMEM] * 10, scra...  4.96 us
    pallas_call x1, Pallas kernels, upward(): call(upward_kernel, outs, [SMEM] + [HBM] * 6, scratch, flops=10 ** 9, vme...  3.71 us
  transfers between devices with their start and end apart: 7, of which 2 were waited for; matrix products, arithmetic and copies ran while one was open for 0% of the time, Pallas kernels for 28%

profile of v3, /device:TPU:1, one launch (start us, length us, event | category | flops | bytes accessed | tf_op | source)
XLA Modules:
  0.0 86.6 jit_solution(11796702438837197198)
XLA Ops:
  0.0 0.6 pad_add_fusion.at_ref
  0.6 3.7 %shard_map.100 = (f32[24,8,256]{2,1,0:T(8,128)}, f32[8,8,384]{2,1,0:T(8,128)}) custom-call(s32[2]{0:T(128)} %pad_add_fusion.at_ref, f32[3,24,256]{2,1,0:T(8,128)} %bitcast.23, f32[3,24,256]{2,1,0:T(8,128)} %bitcast.24, f32[24,256]{1,0:T(8,128)} %bitcast.25, f32[24,64,256]{2,1,0:T(8,128)} %bitcast.16, f32[24,64,64]{2,1,0:T(8,128)} %bitcast.19, f32[64,64]{1,0:T(8,128)} %bitcast.21), custom_call_target="tpu_custom_call" | custom-call | flops 1000000000 | bytes 1048576 | tf_op jit(solution)/shard_map/pallas_call | solution.py:331
  4.3 7.5 %all-to-all-start = ((f32[8,8,384]{2,1,0:T(8,128)}), f32[8,8,384]{2,1,0:T(8,128)S(1)}, u32[]{:S(2)}, u32[]{:S(2)}) async-start(f32[8,8,384]{2,1,0:T(8,128)} %get-tuple-element.17), calls=%async_computation | async-start | bytes 196608 | tf_op jit(solution)/shard_map/all_to_all | solution.py:377
  11.8 0.0 copy-start.8
  11.8 0.9 %copy-done.8 = f32[24,8,256]{2,1,0:T(8,128)S(1)} copy-done((f32[24,8,256]{2,1,0:T(8,128)S(1)}, f32[24,8,256]{2,1,0:T(8,128)}, u32[]{:S(2)}) %copy-start.8) | copy-done | bytes 196632
  12.7 0.0 copy-start.7
  12.7 0.0 copy-start.9
  12.7 6.6 %shard_map.101.before_ref = f32[24,8,256]{2,1,0:T(8,128)S(1)} custom-call(f32[24,8,256]{2,1,0:T(8,128)S(1)} %copy-done.8), custom_call_target="tpu_custom_call" | custom-call | flops 8999999488 | bytes 1048576 | tf_op jit(solution)/shard_map/pallas_call | solution.py:336
  19.3 0.0 all-to-all-done.came_ref
  19.3 0.0 copy-done.7
  19.4 0.0 copy-done.9
  19.4 1.4 %shard_map.102 = (f32[26,8,256]{2,1,0:T(8,128)}, f32[8,32,256]{2,1,0:T(8,128)}) custom-call(s32[2]{0:T(128)S(1)} %copy-done.7, f32[8,8,384]{2,1,0:T(8,128)S(1)} %all-to-all-done.came_ref, f32[24,8,256]{2,1,0:T(8,128)S(1)} %copy-done.9), custom_call_target="tpu_custom_call" | custom-call | flops 100000000 | bytes 1048576 | tf_op jit(solution)/shard_map/pallas_call | solution.py:380
  20.7 7.1 %all-to-all-start.1 = ((f32[8,32,256]{2,1,0:T(8,128)}), f32[8,32,256]{2,1,0:T(8,128)S(1)}, u32[]{:S(2)}, u32[]{:S(2)}) async-start(f32[8,32,256]{2,1,0:T(8,128)} %get-tuple-element.20), calls=%async_computation.1 | async-start | bytes 524288 | tf_op jit(solution)/shard_map/all_to_all | solution.py:385
  27.8 3.5 %collective-permute-start.3 = (f32[26,8,256]{2,1,0:T(8,128)}, f32[26,8,256]{2,1,0:T(8,128)S(1)}, u32[]{:S(2)}, u32[]{:S(2)}) collective-permute-start(f32[26,8,256]{2,1,0:T(8,128)} %get-tuple-element.23.tall_ref), channel_id=1, source_target_pairs={{0,8},{8,16},{16,24},{24,32},{32,40},{40,48},{48,56},{56,64},{64,7... | collective-permute-start | bytes 638984 | tf_op jit(solution)/shard_map/ppermute | solution.py:353
  31.4 1.9 %collective-permute-start.2 = (f32[26,8,256]{2,1,0:T(8,128)}, f32[26,8,256]{2,1,0:T(8,128)}, u32[]{:S(2)}, u32[]{:S(2)}) collective-permute-start(f32[26,8,256]{2,1,0:T(8,128)} %get-tuple-element.23.tall_ref), channel_id=1, source_target_pairs={{0,504},{8,0},{16,8},{24,16},{32,24},{40,32},{48,40},{56,48},{64,5... | collective-permute-start | bytes 638984 | tf_op jit(solution)/shard_map/ppermute | solution.py:353
  33.3 3.3 %all-to-all-done.1.group_ref = f32[8,32,256]{2,1,0:T(8,128)S(1)} async-done(((f32[8,32,256]{2,1,0:T(8,128)}), f32[8,32,256]{2,1,0:T(8,128)S(1)}, u32[]{:S(2)}, u32[]{:S(2)}) %all-to-all-start.1) | async-done | bytes 262176 | tf_op jit(solution)/shard_map/all_to_all | solution.py:385
  36.7 0.8 shard_map.103
  37.5 12.4 %all-to-all-start.2 = ((f32[8,8,256]{2,1,0:T(8,128)}), f32[8,8,256]{2,1,0:T(8,128)S(1)}, u32[]{:S(2)}, u32[]{:S(2)}) async-start(f32[8,8,256]{2,1,0:T(8,128)} %get-tuple-element.24), calls=%async_computation.2 | async-start | bytes 131072 | tf_op jit(solution)/shard_map/all_to_all | solution.py:396
  49.8 7.3 %collective-permute-start = (f32[6,32,256]{2,1,0:T(8,128)}, f32[6,32,256]{2,1,0:T(8,128)}, u32[]{:S(2)}, u32[]{:S(2)}) collective-permute-start(f32[6,32,256]{2,1,0:T(8,128)} %get-tuple-element.21), channel_id=1, source_target_pairs={{0,64},{8,72},{16,80},{24,88},{32,96},{40,104},{48,112},{56,120},{... | collective-permute-start | bytes 589832 | tf_op jit(solution)/shard_map/ppermute | solution.py:353
  57.1 2.8 %collective-permute-start.1 = (f32[6,32,256]{2,1,0:T(8,128)}, f32[6,32,256]{2,1,0:T(8,128)}, u32[]{:S(2)}, u32[]{:S(2)}) collective-permute-start(f32[6,32,256]{2,1,0:T(8,128)} %get-tuple-element.22), channel_id=1, source_target_pairs={{0,448},{8,456},{16,464},{24,472},{32,480},{40,488},{48,496},{56,5... | collective-permute-start | bytes 589832 | tf_op jit(solution)/shard_map/ppermute | solution.py:353
  59.9 0.0 collective-permute-done.3.came_ref
  59.9 8.2 %shard_map.104.before_ref = f32[24,8,256]{2,1,0:T(8,128)S(1)} custom-call(f32[26,8,256]{2,1,0:T(8,128)} %get-tuple-element.23.tall_ref, f32[26,8,256]{2,1,0:T(8,128)S(1)} %collective-permute-done.3.came_ref, f32[24,8,256]{2,1,0:T(8,128)S(1)} %shard_map.101.before_ref), custom_call_target="tpu_custom_call" | custom-call | flops 8999999488 | bytes 100000000 | tf_op jit(solution)/shard_map/pallas_call | solution.py:343
  68.1 0.0 copy-start.10
  68.1 0.7 copy-done.10
  68.8 0.0 copy-start
  68.8 0.0 copy-start.2
  68.8 0.0 copy-start.4
  68.8 0.0 copy-start.5
  68.8 0.0 copy-start.6
  68.9 0.0 collective-permute-done.2.came_ref
  68.9 0.0 all-to-all-done.2
  68.9 0.0 copy-start.11
  68.9 1.1 %copy-done.11 = f32[24,8,256]{2,1,0:T(8,128)S(1)} copy-done((f32[24,8,256]{2,1,0:T(8,128)S(1)}, f32[24,8,256]{2,1,0:T(8,128)}, u32[]{:S(2)}) %copy-start.11) | copy-done | bytes 196632
  70.0 0.0 copy-start.1
  70.0 0.0 copy-start.3
  70.0 8.5 %shard_map.105.near_ref = f32[24,8,256]{2,1,0:T(8,128)S(1)} custom-call(f32[26,8,256]{2,1,0:T(8,128)} %get-tuple-element.23.tall_ref, f32[26,8,256]{2,1,0:T(8,128)} %collective-permute-done.2.came_ref, f32[24,8,256]{2,1,0:T(8,128)S(1)} %copy-done.11), custom_call_target="tpu_custom_call" | custom-call | flops 1800000000 | bytes 20000000 | tf_op jit(solution)/shard_map/pallas_call | solution.py:343
  78.4 0.0 collective-permute-done.below_ref
  78.4 3.1 %collective-permute-done.1.above_ref = f32[6,32,256]{2,1,0:T(8,128)} collective-permute-done((f32[6,32,256]{2,1,0:T(8,128)}, f32[6,32,256]{2,1,0:T(8,128)}, u32[]{:S(2)}, u32[]{:S(2)}) %collective-permute-start.1) | collective-permute-done | bytes 196640 | tf_op jit(solution)/shard_map/ppermute | solution.py:353
  81.6 0.0 copy-done
  81.6 0.0 copy-done.2
  81.6 0.0 copy-done.4
  81.6 0.0 copy-done.5
  81.6 0.0 copy-done.6
  81.6 0.0 copy-done.1
  81.6 0.0 copy-done.3
  81.6 5.0 %shard_map.106 = f32[3,24,256]{2,1,0:T(8,128)} custom-call(s32[2]{0:T(128)S(1)} %copy-done.7, s32[1,30]{1,0:T(1,128)S(1)} %copy-done.5, s32[1,64]{1,0:T(1,128)S(1)} %copy-done.6, f32[8,32,256]{2,1,0:T(8,128)S(1)} %all-to-all-done.1.group_ref, f32[6,32,256]{2,1,0:T(8,128)} %collective-permute-done.below_ref, f32[6,32,256]{2,1,0:T(8,128)} %collective-permute-done.1.above_ref, ...), custom_call_target="tpu_custom_call" | custom-call | flops 4000000000 | bytes 1048576 | tf_op jit(solution)/shard_map/pallas_call | solution.py:348
Async XLA Ops:
  4.3 15.0 %all-to-all-start = ((f32[8,8,384]{2,1,0:T(8,128)}), f32[8,8,384]{2,1,0:T(8,128)S(1)}, u32[]{:S(2)}, u32[]{:S(2)}) async-start(f32[8,8,384]{2,1,0:T(8,128)} %get-tuple-element.17), calls=%async_computation | async-start | bytes 196608 | tf_op jit(solution)/shard_map/all_to_all | solution.py:377
  11.8 0.9 %copy-start.8 = (f32[24,8,256]{2,1,0:T(8,128)S(1)}, f32[24,8,256]{2,1,0:T(8,128)}, u32[]{:S(2)}) copy-start(f32[24,8,256]{2,1,0:T(8,128)} %get-tuple-element.18.wire_ref) | copy-start | bytes 589828
  12.7 6.6 %copy-start.7 = (s32[2]{0:T(128)S(1)}, s32[2]{0:T(128)}, u32[]{:S(2)}) copy-start(s32[2]{0:T(128)} %pad_add_fusion.at_ref) | copy-start | bytes 28
  12.7 6.6 %copy-start.9 = (f32[24,8,256]{2,1,0:T(8,128)S(1)}, f32[24,8,256]{2,1,0:T(8,128)}, u32[]{:S(2)}) copy-start(f32[24,8,256]{2,1,0:T(8,128)} %get-tuple-element.18.wire_ref) | copy-start | bytes 589828
  20.7 15.9 %all-to-all-start.1 = ((f32[8,32,256]{2,1,0:T(8,128)}), f32[8,32,256]{2,1,0:T(8,128)S(1)}, u32[]{:S(2)}, u32[]{:S(2)}) async-start(f32[8,32,256]{2,1,0:T(8,128)} %get-tuple-element.20), calls=%async_computation.1 | async-start | bytes 524288 | tf_op jit(solution)/shard_map/all_to_all | solution.py:385
  27.8 32.1 %collective-permute-start.3 = (f32[26,8,256]{2,1,0:T(8,128)}, f32[26,8,256]{2,1,0:T(8,128)S(1)}, u32[]{:S(2)}, u32[]{:S(2)}) collective-permute-start(f32[26,8,256]{2,1,0:T(8,128)} %get-tuple-element.23.tall_ref), channel_id=1, source_target_pairs={{0,8},{8,16},{16,24},{24,32},{32,40},{40,48},{48,56},{56,64},{64,7... | collective-permute-start | bytes 638984 | tf_op jit(solution)/shard_map/ppermute | solution.py:353
  31.4 37.5 %collective-permute-start.2 = (f32[26,8,256]{2,1,0:T(8,128)}, f32[26,8,256]{2,1,0:T(8,128)}, u32[]{:S(2)}, u32[]{:S(2)}) collective-permute-start(f32[26,8,256]{2,1,0:T(8,128)} %get-tuple-element.23.tall_ref), channel_id=1, source_target_pairs={{0,504},{8,0},{16,8},{24,16},{32,24},{40,32},{48,40},{56,48},{64,5... | collective-permute-start | bytes 638984 | tf_op jit(solution)/shard_map/ppermute | solution.py:353
  37.5 31.4 %all-to-all-start.2 = ((f32[8,8,256]{2,1,0:T(8,128)}), f32[8,8,256]{2,1,0:T(8,128)S(1)}, u32[]{:S(2)}, u32[]{:S(2)}) async-start(f32[8,8,256]{2,1,0:T(8,128)} %get-tuple-element.24), calls=%async_computation.2 | async-start | bytes 131072 | tf_op jit(solution)/shard_map/all_to_all | solution.py:396
  49.8 28.6 %collective-permute-start = (f32[6,32,256]{2,1,0:T(8,128)}, f32[6,32,256]{2,1,0:T(8,128)}, u32[]{:S(2)}, u32[]{:S(2)}) collective-permute-start(f32[6,32,256]{2,1,0:T(8,128)} %get-tuple-element.21), channel_id=1, source_target_pairs={{0,64},{8,72},{16,80},{24,88},{32,96},{40,104},{48,112},{56,120},{... | collective-permute-start | bytes 589832 | tf_op jit(solution)/shard_map/ppermute | solution.py:353
  57.1 24.5 %collective-permute-start.1 = (f32[6,32,256]{2,1,0:T(8,128)}, f32[6,32,256]{2,1,0:T(8,128)}, u32[]{:S(2)}, u32[]{:S(2)}) collective-permute-start(f32[6,32,256]{2,1,0:T(8,128)} %get-tuple-element.22), channel_id=1, source_target_pairs={{0,448},{8,456},{16,464},{24,472},{32,480},{40,488},{48,496},{56,5... | collective-permute-start | bytes 589832 | tf_op jit(solution)/shard_map/ppermute | solution.py:353
  68.1 0.7 copy-start.10
  68.8 12.7 %copy-start = (f32[1,64,64,64]{3,2,1,0:T(8,128)S(1)}, f32[1,64,64,64]{3,2,1,0:T(8,128)}, u32[]{:S(2)}) copy-start(f32[1,64,64,64]{3,2,1,0:T(8,128)} %param.18) | copy-start | bytes 3145732
  68.8 12.7 %copy-start.2 = (f32[1,30,64,64]{3,2,1,0:T(8,128)S(1)}, f32[1,30,64,64]{3,2,1,0:T(8,128)}, u32[]{:S(2)}) copy-start(f32[1,30,64,64]{3,2,1,0:T(8,128)} %param.16) | copy-start | bytes 1474564
  68.8 12.7 %copy-start.4 = (f32[1,1,64,64]{3,2,1,0:T(8,128)S(1)}, f32[1,1,64,64]{3,2,1,0:T(8,128)}, u32[]{:S(2)}) copy-start(f32[1,1,64,64]{3,2,1,0:T(8,128)} %param.15) | copy-start | bytes 49156
  68.8 12.7 %copy-start.5 = (s32[1,30]{1,0:T(1,128)S(1)}, s32[1,30]{1,0:T(1,128)}, u32[]{:S(2)}) copy-start(s32[1,30]{1,0:T(1,128)} %mask_ref.1) | copy-start | bytes 364
  68.8 12.7 %copy-start.6 = (s32[1,64]{1,0:T(1,128)S(1)}, s32[1,64]{1,0:T(1,128)}, u32[]{:S(2)}) copy-start(s32[1,64]{1,0:T(1,128)} %admissible_ref.1) | copy-start | bytes 772
  68.9 1.1 %copy-start.11 = (f32[24,8,256]{2,1,0:T(8,128)S(1)}, f32[24,8,256]{2,1,0:T(8,128)}, u32[]{:S(2)}) copy-start(f32[24,8,256]{2,1,0:T(8,128)} %copy-done.10) | copy-start | bytes 589828
  70.0 11.6 %copy-start.1 = (f32[1,24,64,256]{3,2,1,0:T(8,128)S(1)}, f32[1,24,64,256]{3,2,1,0:T(8,128)}, u32[]{:S(2)}) copy-start(f32[1,24,64,256]{3,2,1,0:T(8,128)} %param.13) | copy-start | bytes 4718596
  70.0 11.7 %copy-start.3 = (f32[1,24,64,64]{3,2,1,0:T(8,128)S(1)}, f32[1,24,64,64]{3,2,1,0:T(8,128)}, u32[]{:S(2)}) copy-start(f32[1,24,64,64]{3,2,1,0:T(8,128)} %param.14) | copy-start | bytes 1179652

commit v4 on v2

--- a/solution.py
+++ b/solution.py
@@ -15,6 +15,7 @@
 LD = 24
 TALL = LD + 2
 ROWS = 32
+PACKED = 40
 SHARPNESS = 2.0
 KERNEL_SCALE = 0.125
 LOG2E = math.log2(math.e)
@@ -208,7 +209,7 @@
     lax.fori_loop(0, LD // OWN_TURN, turn, 0)
 
 
-def near_cross_kernel(tall_ref, lower_ref, upper_ref, own_ref, near_ref, points_ref, loads_ref, pairs_ref):
+def near_cross_kernel(tall_ref, lower_ref, upper_ref, near_ref, points_ref, loads_ref, pairs_ref):
     for around, came_ref, base in ((-1, lower_ref, 0), (1, upper_ref, TALL)):
 
         def prepare(l, _, around=around, came_ref=came_ref, base=base):
@@ -235,7 +236,7 @@
             slot = base + leaves[n] + 1 + step
             totals[n] += pair_sum(tall_ref[leaves[n] + 1], loads_ref, slot, pairs_ref, place, around, step)
         for n in range(CROSS_TURN):
-            near_ref[leaves[n]] = own_ref[leaves[n]] + totals[n]
+            near_ref[leaves[n]] = totals[n]
         return 0
 
     lax.fori_loop(0, LD // CROSS_TURN, turn, 0)
@@ -255,14 +256,15 @@
 
 def window_kernel(lower_ref, tall_ref, upper_ref, window_ref, head_ref, tail_ref):
     for i, came_ref in enumerate((lower_ref, tall_ref, upper_ref)):
-        rows = jnp.concatenate(
-            [came_ref[l, 7:8, :] for l in range(TALL)] + [jnp.zeros((ROWS - TALL, LEAF), F32)], 0
-        )
-        window_ref[i] = rows
+        rows = jnp.concatenate([came_ref[l, 7:8, :] for l in range(TALL)], 0)
+        third = rows[:, 2 * RANK : 3 * RANK]
+        third = jnp.concatenate([third[: TALL // 2], third[TALL // 2 :]], 1)
+        packed = jnp.concatenate([rows[:, : 2 * RANK], third, jnp.zeros((PACKED - TALL - TALL // 2, 128), F32)], 0)
+        window_ref[i] = packed
         if i < 2:
-            head_ref[i] = rows
+            head_ref[i] = packed
         if i > 0:
-            tail_ref[i - 1] = rows
+            tail_ref[i - 1] = packed
 
 
 def exact_by_last(x, y):
@@ -277,10 +279,18 @@
     return high + (cross + lax.dot_general(xh, yl, BY_LAST, preferred_element_type=F32))
 
 
-def finish_kernel(
-    at_ref, mask_ref, admissible_ref, below_ref, above_ref, far_below_ref, far_above_ref, near_ref, every_ref,
-    slab_ref, coupling_ref, top_ref, transfer_ref, basis_ref, out_ref, far_ref,
-):
+def finish_kernel(at_ref, mask_ref, admissible_ref, *refs):
+    count = (len(refs) - 3) // 2
+    held_in, out_ref, local = refs[:count], refs[count], refs[count + 1 : 2 * count + 1]
+    far_ref, sems = refs[2 * count + 1 :]
+    copies = [pltpu.make_async_copy(held_in[n], local[n], sems.at[n]) for n in range(count)]
+    for copy in copies:
+        copy.start()
+    (coupling_ref, below_ref, above_ref, far_below_ref, far_above_ref) = local[:5]
+    (top_ref, every_ref, slab_ref, transfer_ref, basis_ref, own_ref, cross_ref) = local[5:]
+
+    for copy in copies[:5]:
+        copy.wait()
     held = {-4 + i: below_ref[i] for i in range(3)}
     held |= {2 + i: above_ref[i] for i in range(3)}
     held |= {-6 + i: far_below_ref[i] for i in range(2)}
@@ -289,7 +299,11 @@
     for q in range(2 * (REACH - 1)):
         around = q + 2 if q < REACH - 1 else 3 - q
         rows = held[around]
-        stacked = jnp.concatenate([rows[:, r * RANK : (r + 1) * RANK] for r in range(3)], 0)
+        gap = jnp.zeros((ROWS - TALL, RANK), F32)
+        third = rows[TALL : TALL + TALL // 2]
+        stacked = jnp.concatenate(
+            [rows[:TALL, :RANK], gap, rows[:TALL, RANK:], gap, third[:, :RANK], third[:, RANK:], gap], 0
+        )
         coupling = jnp.concatenate(
             [coupling_ref[3 * q + b] * mask_ref[0, 3 * q + b].astype(F32) for b in range(3)], 0
         )
@@ -317,6 +331,8 @@
         rows = (both[0:1, :RANK], both[0:1, RANK:], both[1:2, :RANK])
         return tuple(s + coupling * row for s, row in zip(sums, rows))
 
+    for copy in copies[5:8]:
+        copy.wait()
     nothing = jnp.zeros((RANK, RANK), F32)
     sums = lax.fori_loop(0, sectors, couple, (nothing,) * 3, unroll=16)
     lane = lax.broadcasted_iota(jnp.int32, (RANK, 128), 1)
@@ -326,12 +342,14 @@
     local = jnp.transpose(columns, (1, 0))[:8]
     slab = exact_by_last(local, slab_ref[...])
 
+    for copy in copies[8:]:
+        copy.wait()
     place = lax.broadcasted_iota(jnp.int32, (RANK, RANK), 1)
 
     def leaf(l, _):
         basis = basis_ref[l]
         transfer = transfer_ref[l]
-        near = near_ref[l]
+        near = own_ref[l] + cross_ref[l]
         for r in range(3):
             terms = transfer * slab[r : r + 1] + jnp.where(place == l, far_ref[r], 0.0)
             column = jnp.sum(terms, axis=1, keepdims=True)
@@ -354,13 +372,15 @@
 
 def near_cross(*args):
     scratch = near_scratch(2 * TALL + 2, 6 * CROSS_TURN)
-    return call(near_cross_kernel, shaped(LD, 8, LEAF), [VMEM] * 4, scratch, flops=18 * 10**9, bytes=10**8)(*args)
+    return call(near_cross_kernel, shaped(LD, 8, LEAF), [VMEM] * 3, scratch, flops=18 * 10**9, bytes=10**8)(*args)
 
 
 def finish(*args):
-    return call(finish_kernel, shaped(RHS, LD, LEAF), [SMEM] * 3 + [VMEM] * 11, [pltpu.VMEM((3, RANK, RANK), F32)], flops=4 * 10**9)(
-        *args
-    )
+    held = args[3:]
+    scratch = [pltpu.VMEM(x.shape, F32) for x in held]
+    scratch += [pltpu.VMEM((3, RANK, RANK), F32), pltpu.SemaphoreType.DMA((len(held),))]
+    ins = [SMEM] * 3 + [HBM] * len(held)
+    return call(finish_kernel, shaped(RHS, LD, LEAF), ins, scratch, flops=4 * 10**9, vmem=FULL)(*args)
 
 
 def passed_along(x, axis, by):
@@ -400,7 +420,7 @@
     every = lax.all_to_all(whole, "blk", 0, 0, tiled=True)
     window, head, tail = call(
         window_kernel,
-        (shaped(3, ROWS, LEAF), shaped(2, ROWS, LEAF), shaped(2, ROWS, LEAF)),
+        (shaped(3, PACKED, 128), shaped(2, PACKED, 128), shaped(2, PACKED, 128)),
         [VMEM] * 3,
         flops=10**8,
     )(lower, tall, upper)
@@ -408,10 +428,10 @@
     above = passed_along(window, "blk", -3)
     far_below = passed_along(head, "blk", 5)
     far_above = passed_along(tail, "blk", -5)
-    near = near_cross(tall, lower, upper, own)
+    cross = near_cross(tall, lower, upper)
     out = finish(
-        at, leaf_admissible_mask, top_admissible, below, above, far_below, far_above, near, every,
-        slab, leaf_coupling_matrices[0], top_coupling[0], transfer, basis,
+        at, leaf_admissible_mask, top_admissible, leaf_coupling_matrices[0], below, above, far_below, far_above,
+        top_coupling[0], every, slab, transfer, basis, own, cross,
     )
     return out[:, None]
 

time: 85.8 us -> 82.5 us (0.962)
  the two profiles are of different devices: /device:TPU:16 before, /device:TPU:1 now
where the time goes in v4:
time: 82.5 us; the launch traced here: 80.9 us
  starting transfers between devices  45.4 us (55%)
  Pallas kernels  31.9 us (39%)
  local copies, waits for them, and re-layouts  2.94 us (4%)
    ppermute x6, starting transfers between devices, passed_along(): return lax.ppermute(x, axis, [(i, (i + by) % count) for i in range(count)])  23 us
    all_to_all x1, starting transfers between devices, body(): every = lax.all_to_all(whole, 'blk', 0, 0, tiled=True)  14.8 us
    pallas_call x1, Pallas kernels, near_cross(): call(near_cross_kernel, shaped(LD, 8, LEAF), [VMEM] * 3, scratch, flops=1...  14.4 us
    all_to_all x1, starting transfers between devices, body(): came = lax.all_to_all(slots, 'along', 0, 0, tiled=True)  7.49 us
    pallas_call x1, Pallas kernels, near_own(): call(near_own_kernel, shaped(LD, 8, LEAF), [VMEM], scratch, flops=9 * 10...  6.58 us
    pallas_call x1, Pallas kernels, finish(): call(finish_kernel, shaped(RHS, LD, LEAF), ins, scratch, flops=4 * 10 **...  5.82 us
    pallas_call x1, Pallas kernels, upward(): call(upward_kernel, outs, [SMEM] + [HBM] * 6, scratch, flops=10 ** 9, vme...  3.7 us
    unnamed x20, local copies, waits for them, and re-layouts  2.94 us
  transfers between devices with their start and end apart: 8, of which 0 were waited for; matrix products, arithmetic and copies ran while one was open for 0% of the time, Pallas kernels for 26%

profile of v4, /device:TPU:1, one launch (start us, length us, event | category | flops | bytes accessed | tf_op | source)
XLA Modules:
  0.0 80.9 jit_solution(13754403315740421693)
XLA Ops:
  0.0 0.6 pad_add_fusion.at_ref
  0.6 3.7 %shard_map.100 = (f32[24,8,256]{2,1,0:T(8,128)}, f32[8,8,384]{2,1,0:T(8,128)}) custom-call(s32[2]{0:T(128)} %pad_add_fusion.at_ref, f32[3,24,256]{2,1,0:T(8,128)} %bitcast.19, f32[3,24,256]{2,1,0:T(8,128)} %bitcast.20, f32[24,256]{1,0:T(8,128)} %bitcast.23, f32[24,64,256]{2,1,0:T(8,128)} %bitcast.14, f32[24,64,64]{2,1,0:T(8,128)} %bitcast.17, f32[64,64]{1,0:T(8,128)} %bitcast.21), custom_call_target="tpu_custom_call" | custom-call | flops 1000000000 | bytes 1048576 | tf_op jit(solution)/shard_map/pallas_call | solution.py:365
  4.3 7.5 %all-to-all-start = ((f32[8,8,384]{2,1,0:T(8,128)}), f32[8,8,384]{2,1,0:T(8,128)S(1)}, u32[]{:S(2)}, u32[]{:S(2)}) async-start(f32[8,8,384]{2,1,0:T(8,128)} %get-tuple-element.14), calls=%async_computation | async-start | bytes 196608 | tf_op jit(solution)/shard_map/all_to_all | solution.py:412
  11.8 0.0 copy-start.1
  11.8 0.9 %copy-done.1 = f32[24,8,256]{2,1,0:T(8,128)S(1)} copy-done((f32[24,8,256]{2,1,0:T(8,128)S(1)}, f32[24,8,256]{2,1,0:T(8,128)}, u32[]{:S(2)}) %copy-start.1) | copy-done | bytes 196632
  12.7 0.0 copy-start
  12.7 0.0 copy-start.2
  12.7 6.6 %shard_map.101.refs_10_ = f32[24,8,256]{2,1,0:T(8,128)S(1)} custom-call(f32[24,8,256]{2,1,0:T(8,128)S(1)} %copy-done.1), custom_call_target="tpu_custom_call" | custom-call | flops 8999999488 | bytes 1048576 | tf_op jit(solution)/shard_map/pallas_call | solution.py:370
  19.3 0.0 copy-start.3
  19.3 0.7 copy-done.3
  20.0 0.0 all-to-all-done.came_ref
  20.0 0.0 copy-done
  20.0 0.0 copy-done.2
  20.0 1.3 %shard_map.102 = (f32[26,8,256]{2,1,0:T(8,128)S(1)}, f32[64,2,128]{2,1,0:T(2,128)}) custom-call(s32[2]{0:T(128)S(1)} %copy-done, f32[8,8,384]{2,1,0:T(8,128)S(1)} %all-to-all-done.came_ref, f32[24,8,256]{2,1,0:T(8,128)S(1)} %copy-done.2), custom_call_target="tpu_custom_call" | custom-call | flops 100000000 | bytes 1048576 | tf_op jit(solution)/shard_map/pallas_call | solution.py:415
  21.3 4.7 %collective-permute-start.1 = (f32[26,8,256]{2,1,0:T(8,128)S(1)}, f32[26,8,256]{2,1,0:T(8,128)S(1)}, u32[]{:S(2)}, u32[]{:S(2)}) collective-permute-start(f32[26,8,256]{2,1,0:T(8,128)S(1)} %get-tuple-element.17.tall_ref), channel_id=1, source_target_pairs={{0,504},{8,0},{16,8},{24,16},{32,24},{40,32},{48,40},{56,48},{64,5... | collective-permute-start | bytes 638984 | tf_op jit(solution)/shard_map/ppermute | solution.py:388
  25.9 1.9 %collective-permute-start = (f32[26,8,256]{2,1,0:T(8,128)S(1)}, f32[26,8,256]{2,1,0:T(8,128)S(1)}, u32[]{:S(2)}, u32[]{:S(2)}) collective-permute-start(f32[26,8,256]{2,1,0:T(8,128)S(1)} %get-tuple-element.17.tall_ref), channel_id=1, source_target_pairs={{0,8},{8,16},{16,24},{24,32},{32,40},{40,48},{48,56},{56,64},{64,7... | collective-permute-start | bytes 638984 | tf_op jit(solution)/shard_map/ppermute | solution.py:388
  27.9 14.8 %all-to-all-start.1 = ((f32[64,2,128]{2,1,0:T(2,128)}), f32[64,2,128]{2,1,0:T(2,128)S(1)}, u32[]{:S(2)}, u32[]{:S(2)}) async-start(f32[64,2,128]{2,1,0:T(2,128)} %get-tuple-element.21), calls=%async_computation.1 | async-start | bytes 131072 | tf_op jit(solution)/shard_map/all_to_all | solution.py:420
  42.7 0.0 collective-permute-done.1.upper_ref
  42.7 0.0 collective-permute-done.lower_ref
  42.7 0.1 shard_map.103
  42.8 6.0 %collective-permute-start.3 = (f32[3,40,128]{2,1,0:T(8,128)S(1)}, f32[3,40,128]{2,1,0:T(8,128)S(1)}, u32[]{:S(2)}, u32[]{:S(2)}) collective-permute-start(f32[3,40,128]{2,1,0:T(8,128)S(1)} %get-tuple-element.18), channel_id=1, source_target_pairs={{0,488},{8,496},{16,504},{24,0},{32,8},{40,16},{48,24},{56,32},{64... | collective-permute-start | bytes 184328 | tf_op jit(solution)/shard_map/ppermute | solution.py:388
  48.8 1.9 %collective-permute-start.2 = (f32[3,40,128]{2,1,0:T(8,128)S(1)}, f32[3,40,128]{2,1,0:T(8,128)S(1)}, u32[]{:S(2)}, u32[]{:S(2)}) collective-permute-start(f32[3,40,128]{2,1,0:T(8,128)S(1)} %get-tuple-element.18), channel_id=1, source_target_pairs={{0,24},{8,32},{16,40},{24,48},{32,56},{40,64},{48,72},{56,80},{64,... | collective-permute-start | bytes 184328 | tf_op jit(solution)/shard_map/ppermute | solution.py:388
  50.7 4.2 %collective-permute-start.4 = (f32[2,40,128]{2,1,0:T(8,128)S(1)}, f32[2,40,128]{2,1,0:T(8,128)S(1)}, u32[]{:S(2)}, u32[]{:S(2)}) collective-permute-start(f32[2,40,128]{2,1,0:T(8,128)S(1)} %get-tuple-element.19), channel_id=1, source_target_pairs={{0,40},{8,48},{16,56},{24,64},{32,72},{40,80},{48,88},{56,96},{64,... | collective-permute-start | bytes 122888 | tf_op jit(solution)/shard_map/ppermute | solution.py:388
  55.0 4.3 %collective-permute-start.5 = (f32[2,40,128]{2,1,0:T(8,128)S(1)}, f32[2,40,128]{2,1,0:T(8,128)S(1)}, u32[]{:S(2)}, u32[]{:S(2)}) collective-permute-start(f32[2,40,128]{2,1,0:T(8,128)S(1)} %get-tuple-element.20), channel_id=1, source_target_pairs={{0,472},{8,480},{16,488},{24,496},{32,504},{40,0},{48,8},{56,16},{... | collective-permute-start | bytes 122888 | tf_op jit(solution)/shard_map/ppermute | solution.py:388
  59.3 14.4 %shard_map.104.refs_11_ = f32[24,8,256]{2,1,0:T(8,128)S(1)} custom-call(f32[26,8,256]{2,1,0:T(8,128)S(1)} %get-tuple-element.17.tall_ref, f32[26,8,256]{2,1,0:T(8,128)S(1)} %collective-permute-done.lower_ref, f32[26,8,256]{2,1,0:T(8,128)S(1)} %collective-permute-done.1.upper_ref), custom_call_target="tpu_custom_call" | custom-call | flops 17999998976 | bytes 100000000 | tf_op jit(solution)/shard_map/pallas_call | solution.py:375
  73.7 0.0 copy-start.4
  73.7 0.7 copy-done.4
  74.4 0.0 collective-permute-done.4.refs_3_
  74.4 0.0 copy-start.8
  74.4 0.0 collective-permute-done.5.refs_4_
  74.4 0.0 copy-start.9
  74.4 0.0 all-to-all-done.1.refs_6_
  74.4 0.0 copy-start.5
  74.4 0.0 collective-permute-done.3.refs_2_
  74.4 0.0 copy-start.6
  74.5 0.0 collective-permute-done.2.refs_1_
  74.5 0.0 copy-start.7
  74.5 0.5 copy-done.8
  75.0 0.0 copy-done.9
  75.0 0.0 copy-done.5
  75.0 0.0 copy-done.6
  75.1 0.0 copy-done.7
  75.1 5.8 %shard_map.105 = f32[3,24,256]{2,1,0:T(8,128)} custom-call(s32[2]{0:T(128)} %pad_add_fusion.at_ref, s32[1,30]{1,0:T(1,128)} %mask_ref.1, s32[1,64]{1,0:T(1,128)} %admissible_ref.1, f32[30,64,64]{2,1,0:T(8,128)} %bitcast.16, f32[3,40,128]{2,1,0:T(8,128)} %copy-done.7, f32[3,40,128]{2,1,0:T(8,128)} %copy-done.6, f32[2,40,128]{2,1,0:T(8,128)} %copy-done.8, ...), custom_call_target="tpu_custom_call" | custom-call | flops 4000000000 | bytes 1048576 | tf_op jit(solution)/shard_map/pallas_call | solution.py:383
Async XLA Ops:
  4.3 15.7 %all-to-all-start = ((f32[8,8,384]{2,1,0:T(8,128)}), f32[8,8,384]{2,1,0:T(8,128)S(1)}, u32[]{:S(2)}, u32[]{:S(2)}) async-start(f32[8,8,384]{2,1,0:T(8,128)} %get-tuple-element.14), calls=%async_computation | async-start | bytes 196608 | tf_op jit(solution)/shard_map/all_to_all | solution.py:412
  11.8 0.9 %copy-start.1 = (f32[24,8,256]{2,1,0:T(8,128)S(1)}, f32[24,8,256]{2,1,0:T(8,128)}, u32[]{:S(2)}) copy-start(f32[24,8,256]{2,1,0:T(8,128)} %get-tuple-element.15.wire_ref) | copy-start | bytes 589828
  12.7 7.3 %copy-start = (s32[2]{0:T(128)S(1)}, s32[2]{0:T(128)}, u32[]{:S(2)}) copy-start(s32[2]{0:T(128)} %pad_add_fusion.at_ref) | copy-start | bytes 28
  12.7 7.3 %copy-start.2 = (f32[24,8,256]{2,1,0:T(8,128)S(1)}, f32[24,8,256]{2,1,0:T(8,128)}, u32[]{:S(2)}) copy-start(f32[24,8,256]{2,1,0:T(8,128)} %get-tuple-element.15.wire_ref) | copy-start | bytes 589828
  19.3 0.7 copy-start.3
  21.3 21.5 %collective-permute-start.1 = (f32[26,8,256]{2,1,0:T(8,128)S(1)}, f32[26,8,256]{2,1,0:T(8,128)S(1)}, u32[]{:S(2)}, u32[]{:S(2)}) collective-permute-start(f32[26,8,256]{2,1,0:T(8,128)S(1)} %get-tuple-element.17.tall_ref), channel_id=1, source_target_pairs={{0,504},{8,0},{16,8},{24,16},{32,24},{40,32},{48,40},{56,48},{64,5... | collective-permute-start | bytes 638984 | tf_op jit(solution)/shard_map/ppermute | solution.py:388
  25.9 16.8 %collective-permute-start = (f32[26,8,256]{2,1,0:T(8,128)S(1)}, f32[26,8,256]{2,1,0:T(8,128)S(1)}, u32[]{:S(2)}, u32[]{:S(2)}) collective-permute-start(f32[26,8,256]{2,1,0:T(8,128)S(1)} %get-tuple-element.17.tall_ref), channel_id=1, source_target_pairs={{0,8},{8,16},{16,24},{24,32},{32,40},{40,48},{48,56},{56,64},{64,7... | collective-permute-start | bytes 638984 | tf_op jit(solution)/shard_map/ppermute | solution.py:388
  27.9 46.5 %all-to-all-start.1 = ((f32[64,2,128]{2,1,0:T(2,128)}), f32[64,2,128]{2,1,0:T(2,128)S(1)}, u32[]{:S(2)}, u32[]{:S(2)}) async-start(f32[64,2,128]{2,1,0:T(2,128)} %get-tuple-element.21), calls=%async_computation.1 | async-start | bytes 131072 | tf_op jit(solution)/shard_map/all_to_all | solution.py:420
  42.8 31.6 %collective-permute-start.3 = (f32[3,40,128]{2,1,0:T(8,128)S(1)}, f32[3,40,128]{2,1,0:T(8,128)S(1)}, u32[]{:S(2)}, u32[]{:S(2)}) collective-permute-start(f32[3,40,128]{2,1,0:T(8,128)S(1)} %get-tuple-element.18), channel_id=1, source_target_pairs={{0,488},{8,496},{16,504},{24,0},{32,8},{40,16},{48,24},{56,32},{64... | collective-permute-start | bytes 184328 | tf_op jit(solution)/shard_map/ppermute | solution.py:388
  48.8 25.7 %collective-permute-start.2 = (f32[3,40,128]{2,1,0:T(8,128)S(1)}, f32[3,40,128]{2,1,0:T(8,128)S(1)}, u32[]{:S(2)}, u32[]{:S(2)}) collective-permute-start(f32[3,40,128]{2,1,0:T(8,128)S(1)} %get-tuple-element.18), channel_id=1, source_target_pairs={{0,24},{8,32},{16,40},{24,48},{32,56},{40,64},{48,72},{56,80},{64,... | collective-permute-start | bytes 184328 | tf_op jit(solution)/shard_map/ppermute | solution.py:388
  50.7 23.7 %collective-permute-start.4 = (f32[2,40,128]{2,1,0:T(8,128)S(1)}, f32[2,40,128]{2,1,0:T(8,128)S(1)}, u32[]{:S(2)}, u32[]{:S(2)}) collective-permute-start(f32[2,40,128]{2,1,0:T(8,128)S(1)} %get-tuple-element.19), channel_id=1, source_target_pairs={{0,40},{8,48},{16,56},{24,64},{32,72},{40,80},{48,88},{56,96},{64,... | collective-permute-start | bytes 122888 | tf_op jit(solution)/shard_map/ppermute | solution.py:388
  55.0 19.4 %collective-permute-start.5 = (f32[2,40,128]{2,1,0:T(8,128)S(1)}, f32[2,40,128]{2,1,0:T(8,128)S(1)}, u32[]{:S(2)}, u32[]{:S(2)}) collective-permute-start(f32[2,40,128]{2,1,0:T(8,128)S(1)} %get-tuple-element.20), channel_id=1, source_target_pairs={{0,472},{8,480},{16,488},{24,496},{32,504},{40,0},{48,8},{56,16},{... | collective-permute-start | bytes 122888 | tf_op jit(solution)/shard_map/ppermute | solution.py:388
  73.7 0.7 copy-start.4
  74.4 0.6 copy-start.8
  74.4 0.6 copy-start.9
  74.4 0.6 copy-start.5
  74.4 0.6 copy-start.6
  74.5 0.6 copy-start.7

commit v5 on v3

--- a/solution.py
+++ b/solution.py
@@ -15,6 +15,7 @@
 LD = 24
 TALL = LD + 2
 ROWS = 32
+PACKED = 40
 SHARPNESS = 2.0
 KERNEL_SCALE = 0.125
 LOG2E = math.log2(math.e)
@@ -28,7 +29,6 @@
 MIB = 2**20
 FULL = 60 * MIB + 128 * 1024
 OWN_TURN = 3
-GROUP = 8
 UP_PARTS = 4
 UP_LEAVES = LD // UP_PARTS
 
@@ -125,29 +125,24 @@
         slots_ref[j, :, LEAF:] = share
 
 
-def joined_kernel(at_ref, came_ref, wire_ref, tall_ref, rows_ref):
+def joined_kernel(at_ref, came_ref, wire_ref, tall_ref, whole_ref):
     here = at_ref[0]
     total = came_ref[0, :, LEAF:]
     for j in range(1, 8):
         total = total + came_ref[j, :, LEAF:]
+    packed = jnp.concatenate(
+        [
+            jnp.concatenate([total[0:1, :RANK], total[1:2, :RANK]], 1),
+            jnp.concatenate([total[2:3, :RANK], jnp.zeros((1, RANK), F32)], 1),
+        ],
+        0,
+    )
+    whole_ref[...] = jnp.broadcast_to(packed[None], whole_ref.shape)
     lower = came_ref[jnp.maximum(here - 1, 0), :, :LEAF]
     upper = came_ref[jnp.minimum(here + 1, 7), :, :LEAF]
     tall_ref[0] = jnp.where(here > 0, lower, 0.0)
     tall_ref[1 : LD + 1] = wire_ref[...]
     tall_ref[LD + 1] = jnp.where(here < 7, upper, 0.0)
-    share = jnp.concatenate([total[r : r + 1, :RANK] for r in range(3)] + [jnp.zeros((1, RANK), F32)], 1)
-    rows = jnp.concatenate(
-        [tall_ref[l, 7:8, :] for l in range(TALL)] + [share, jnp.zeros((ROWS - TALL - 1, LEAF), F32)], 0
-    )
-    for j in range(GROUP):
-        rows_ref[j] = rows
-
-
-def group_kernel(group_ref, low_ref, high_ref, shares_ref):
-    low_ref[...] = group_ref[GROUP - REACH :]
-    high_ref[...] = group_ref[:REACH]
-    shares = jnp.concatenate([group_ref[j, TALL : TALL + 1, :] for j in range(GROUP)], 0)
-    shares_ref[...] = jnp.broadcast_to(shares[None], shares_ref.shape)
 
 
 def source_side(leaf, around, steps, slot, points_ref, loads_ref):
@@ -213,12 +208,17 @@
     lax.fori_loop(0, LD // OWN_TURN, turn, 0)
 
 
-def near_side_kernel(around, tall_ref, came_ref, before_ref, near_ref, points_ref, loads_ref, pairs_ref):
+def near_side_kernel(beyond, at_ref, tall_ref, came_ref, near_ref, points_ref, loads_ref, pairs_ref):
+    odd = lax.rem(at_ref[1], 2)
+    around = ((2 * odd - 1) if beyond else (1 - 2 * odd)).astype(F32)
+
     def prepare(l, _):
         source_side(came_ref[l], around, (-1, 0, 1), l, points_ref, loads_ref)
         return 0
 
     lax.fori_loop(0, TALL, prepare, 0, unroll=13)
+    end, end_leaf, end_step = (LD + 1, LD - 1, 1) if beyond else (0, 0, -1)
+    source_side(tall_ref[end], 0, (end_step,), TALL, points_ref, loads_ref)
 
     def turn(g, _):
         leaves = [g * OWN_TURN + n for n in range(OWN_TURN)]
@@ -226,7 +226,7 @@
         targets = [target_points(tall_ref[l + 1]) for l in leaves]
         for place, (n, step) in enumerate(places):
             pair_kernel(targets[n], points_ref, leaves[n] + 1 + step, pairs_ref, place)
-        totals = [before_ref[l] for l in leaves]
+        totals = [jnp.zeros((8, LEAF), F32)] * OWN_TURN
         for place, (n, step) in enumerate(places):
             slot = leaves[n] + 1 + step
             totals[n] += pair_sum(tall_ref[leaves[n] + 1], loads_ref, slot, pairs_ref, place, around, step)
@@ -235,11 +235,9 @@
         return 0
 
     lax.fori_loop(0, LD // OWN_TURN, turn, 0)
-    end, l, step = ((0, 0, -1), None, (LD + 1, LD - 1, 1))[around + 1]
-    here = tall_ref[l + 1]
-    source_side(tall_ref[end], 0, (step,), TALL, points_ref, loads_ref)
+    here = tall_ref[end_leaf + 1]
     pair_kernel(target_points(here), points_ref, TALL, pairs_ref, 0)
-    near_ref[l] += pair_sum(here, loads_ref, TALL, pairs_ref, 0, 0, step)
+    near_ref[end_leaf] += pair_sum(here, loads_ref, TALL, pairs_ref, 0, 0, end_step)
 
 
 def near_scratch(leaves, places):
@@ -250,6 +248,44 @@
     ]
 
 
+def packed(rows):
+    third = rows[:, 2 * RANK : 3 * RANK]
+    third = jnp.concatenate([third[: TALL // 2], third[TALL // 2 :]], 1)
+    return jnp.concatenate([rows[:, : 2 * RANK], third, jnp.zeros((PACKED - TALL - TALL // 2, 128), F32)], 0)
+
+
+def coefs_of(tall_ref):
+    return jnp.concatenate([tall_ref[l, 7:8, :] for l in range(TALL)], 0)
+
+
+def pair_records_kernel(tall_ref, partner_ref, records_ref):
+    records_ref[:TALL] = tall_ref[...]
+    rows = jnp.concatenate([coefs_of(partner_ref), jnp.zeros((ROWS - TALL, LEAF), F32)], 0)
+    for n in range(ROWS // 8):
+        records_ref[TALL + n] = rows[8 * n : 8 * n + 8]
+
+
+def beside_kernel(at_ref, came_ref, beside_ref):
+    even = lax.rem(at_ref[1], 2) == 0
+    first = packed(coefs_of(came_ref))
+    second = packed(jnp.concatenate([came_ref[TALL + n] for n in range(ROWS // 8)], 0)[:TALL])
+    beside_ref[0] = jnp.where(even, second, first)
+    beside_ref[1] = jnp.where(even, first, second)
+
+
+def window_kernel(at_ref, tall_ref, partner_ref, beside_ref, other_ref, window_ref, onward_ref):
+    even = lax.rem(at_ref[1], 2) == 0
+    own, partner = packed(coefs_of(tall_ref)), packed(coefs_of(partner_ref))
+    beside, other = [beside_ref[n] for n in range(2)], [other_ref[n] for n in range(2)]
+    low = [jnp.where(even, beside[n], other[n]) for n in range(2)]
+    high = [jnp.where(even, other[n], beside[n]) for n in range(2)]
+    window = low + [jnp.where(even, own, partner), jnp.where(even, partner, own)] + high
+    for n in range(6):
+        window_ref[n] = window[n]
+    for n in range(4):
+        onward_ref[n] = jnp.where(even, window[n + 2], window[n])
+
+
 def exact_by_last(x, y):
     return lax.dot_general(x, y, BY_LAST, precision=EXACT, preferred_element_type=F32)
 
@@ -262,20 +298,29 @@
     return high + (cross + lax.dot_general(xh, yl, BY_LAST, preferred_element_type=F32))
 
 
-def finish_kernel(
-    at_ref, mask_ref, admissible_ref, group_ref, below_ref, above_ref, near_ref, every_ref,
-    slab_ref, coupling_ref, top_ref, transfer_ref, basis_ref, out_ref, far_ref, ring_ref,
-):
-    ring_ref[:REACH] = below_ref[...]
-    ring_ref[REACH : REACH + GROUP] = group_ref[...]
-    ring_ref[REACH + GROUP :] = above_ref[...]
+def finish_kernel(at_ref, mask_ref, admissible_ref, *refs):
+    count = len(refs) - 3
+    local, out_ref = refs[:count], refs[count]
+    far_ref, ring_ref = refs[count + 1 :]
+    coupling_ref, window_ref, onward_ref, back_ref = local[:4]
+    top_ref, every_ref, slab_ref, transfer_ref, basis_ref, own_ref, side_ref, beyond_ref = local[4:]
+
     here = at_ref[1]
-    member = lax.rem(here, GROUP)
+    odd = lax.rem(here, 2)
+    for n in range(4):
+        ring_ref[n] = jnp.where(odd == 0, onward_ref[n], back_ref[n])
+        ring_ref[n + 10] = jnp.where(odd == 0, back_ref[n], onward_ref[n])
+    for n in range(6):
+        ring_ref[n + 4] = window_ref[n]
     total = jnp.zeros((3 * ROWS, 3 * RANK), F32)
     for q in range(2 * (REACH - 1)):
         around = q + 2 if q < REACH - 1 else 3 - q
-        rows = ring_ref[member + (REACH + around)]
-        stacked = jnp.concatenate([rows[:, r * RANK : (r + 1) * RANK] for r in range(3)], 0)
+        rows = ring_ref[odd + (REACH + around)]
+        gap = jnp.zeros((ROWS - TALL, RANK), F32)
+        third = rows[TALL : TALL + TALL // 2]
+        stacked = jnp.concatenate(
+            [rows[:TALL, :RANK], gap, rows[:TALL, RANK:], gap, third[:, :RANK], third[:, RANK:], gap], 0
+        )
         coupling = jnp.concatenate(
             [coupling_ref[3 * q + b] * mask_ref[0, 3 * q + b].astype(F32) for b in range(3)], 0
         )
@@ -298,8 +343,9 @@
         distant = jnp.logical_and(apart > REACH, apart < sectors - REACH)
         allowed = jnp.where(distant, admissible_ref[0, t], 0).astype(F32)
         coupling = top_ref[t]
-        row = every_ref[pl.ds(t, 1), :] * allowed
-        return tuple(s + coupling * row[:, r * RANK : (r + 1) * RANK] for r, s in enumerate(sums))
+        both = every_ref[t] * allowed
+        rows = (both[0:1, :RANK], both[0:1, RANK:], both[1:2, :RANK])
+        return tuple(s + coupling * row for s, row in zip(sums, rows))
 
     nothing = jnp.zeros((RANK, RANK), F32)
     sums = lax.fori_loop(0, sectors, couple, (nothing,) * 3, unroll=16)
@@ -315,7 +361,7 @@
     def leaf(l, _):
         basis = basis_ref[l]
         transfer = transfer_ref[l]
-        near = near_ref[l]
+        near = own_ref[l] + side_ref[l] + beyond_ref[l]
         for r in range(3):
             terms = transfer * slab[r : r + 1] + jnp.where(place == l, far_ref[r], 0.0)
             column = jnp.sum(terms, axis=1, keepdims=True)
@@ -336,21 +382,16 @@
     return call(near_own_kernel, shaped(LD, 8, LEAF), [VMEM], scratch, flops=9 * 10**9)(wire)
 
 
-def near_side(around, *args):
-    kernel = functools.partial(near_side_kernel, around)
+def near_side(beyond, *args):
+    kernel = functools.partial(near_side_kernel, beyond)
     scratch = near_scratch(TALL + 1, 3 * OWN_TURN)
-    cost = 10**8 if around < 0 else 20 * 10**6
-    return call(kernel, shaped(LD, 8, LEAF), [VMEM] * 3, scratch, flops=90 * cost, bytes=cost)(*args)
+    return call(kernel, shaped(LD, 8, LEAF), [SMEM, VMEM, VMEM], scratch, flops=9 * 10**9, bytes=2 * 10**7)(*args)
 
 
 def finish(*args):
-    scratch = [pltpu.VMEM((3, RANK, RANK), F32), pltpu.VMEM((GROUP + 2 * REACH, ROWS, LEAF), F32)]
-    return call(finish_kernel, shaped(RHS, LD, LEAF), [SMEM] * 3 + [VMEM] * 10, scratch, flops=4 * 10**9)(*args)
-
-
-def passed_along(x, axis, by):
-    count = lax.axis_size(axis)
-    return lax.ppermute(x, axis, [(i, (i + by) % count) for i in range(count)])
+    scratch = [pltpu.VMEM((3, RANK, RANK), F32), pltpu.VMEM((14, PACKED, 128), F32)]
+    ins = [SMEM] * 3 + [VMEM] * (len(args) - 3)
+    return call(finish_kernel, shaped(RHS, LD, LEAF), ins, scratch, flops=4 * 10**9)(*args)
 
 
 def body(
@@ -377,29 +418,31 @@
     came = lax.all_to_all(slots, "along", 0, 0, tiled=True)
     own = near_own(wire)
     came, own = lax.optimization_barrier((came, own))
-    tall, rows = call(
-        joined_kernel, (shaped(TALL, 8, LEAF), shaped(GROUP, ROWS, LEAF)), [SMEM, VMEM, VMEM], flops=10**8
+    tall, whole = call(
+        joined_kernel, (shaped(TALL, 8, LEAF), shaped(sectors, 2, 128)), [SMEM, VMEM, VMEM], flops=10**8
     )(at, came, wire)
-    beside = [[g * GROUP + j for j in range(GROUP)] for g in range(sectors // GROUP)]
-    across = [[g * GROUP + j for g in range(sectors // GROUP)] for j in range(GROUP)]
-    group = lax.all_to_all(rows, "blk", 0, 0, tiled=True, axis_index_groups=beside)
-    lower = passed_along(tall, "blk", 1)
-    upper = passed_along(tall, "blk", -1)
-    low, high, shares = call(
-        group_kernel,
-        (shaped(REACH, ROWS, LEAF), shaped(REACH, ROWS, LEAF), shaped(sectors // GROUP, GROUP, LEAF)),
-        [VMEM],
-        flops=10**8,
-    )(group)
-    below = passed_along(low, "blk", GROUP)
-    above = passed_along(high, "blk", -GROUP)
-    every = lax.all_to_all(shares, "blk", 0, 0, tiled=True, axis_index_groups=across)
-    near = near_side(-1, tall, lower, own)
-    every, upper, near = lax.optimization_barrier((every, upper, near))
-    near = near_side(1, tall, upper, near)
+    flip = [(i, i ^ 1) for i in range(sectors)]
+    step_out = [(i, (i + 1 if i % 2 else i - 1) % sectors) for i in range(sectors)]
+    stride = [(i, (i + 3 if i % 2 else i - 3) % sectors) for i in range(sectors)]
+    partner = lax.ppermute(tall, "blk", flip)
+    records = call(pair_records_kernel, shaped(TALL + ROWS // 8, 8, LEAF), [VMEM] * 2)(tall, partner)
+    records, whole, partner = lax.optimization_barrier((records, whole, partner))
+    came = lax.ppermute(records, "blk", step_out)
+    side = near_side(False, at, tall, partner)
+    came, side = lax.optimization_barrier((came, side))
+    every = lax.all_to_all(whole, "blk", 0, 0, tiled=True)
+    beside = call(beside_kernel, shaped(2, PACKED, 128), [SMEM, VMEM])(at, came)
+    other = lax.ppermute(beside, "blk", flip)
+    window, onward = call(
+        window_kernel, (shaped(6, PACKED, 128), shaped(4, PACKED, 128)), [SMEM] + [VMEM] * 4
+    )(at, tall, partner, beside, other)
+    onward = lax.ppermute(onward, "blk", stride)
+    window, came, every = lax.optimization_barrier((window, came, every))
+    beyond = near_side(True, at, tall, came)
+    back = lax.ppermute(onward, "blk", flip)
     out = finish(
-        at, leaf_admissible_mask, top_admissible, group, below, above, near, every.reshape(sectors, LEAF),
-        slab, leaf_coupling_matrices[0], top_coupling[0], transfer, basis,
+        at, leaf_admissible_mask, top_admissible, leaf_coupling_matrices[0], window, onward, back,
+        top_coupling[0], every, slab, transfer, basis, own, side, beyond,
     )
     return out[:, None]
 

time: 87.2 us -> 82.7 us (0.948)
  starting transfers between devices: 42.5 us -> 40.6 us
  local copies, waits for them, and re-layouts: 2.73 us -> 0.98 us
  Pallas kernels: 34.1 us -> 32.9 us
    all_to_all x2 -> x1, starting transfers between devices: 19.5 us -> 14.4 us  [body(): every = lax.all_to_all(whole, 'blk', 0, 0, tiled=True)]
    ppermute x4 -> x5, waiting for transfers between devices: 3.15 us -> 6.95 us  [the longest x1 5.02 us: body(): onward = lax.ppermute(onward, 'blk', stride)]
    all_to_all x2 -> x1, waiting for transfers between devices: 3.35 us -> 0.01 us  [body(): every = lax.all_to_all(whole, 'blk', 0, 0, tiled=True)]
    ppermute x4 -> x5, starting transfers between devices: 15.5 us -> 18.7 us  [the longest x1 4.86 us: body(): partner = lax.ppermute(tall, 'blk', flip)]
    unnamed x24 -> x20, local copies, waits for them, and re-layouts: 2.73 us -> 0.98 us
    pallas_call x5 -> x7, Pallas kernels: 23.8 us -> 22.6 us  [the longest x2 15.7 us: near_side(): call(kernel, shaped(LD, 8, LEAF), [SMEM, VMEM, VMEM], scratch, flops=9 *...]
  transfers between devices with their start and end apart: 7 -> 7, of which waited for: 2 -> 3; matrix products, arithmetic and copies ran while one was open for 0% -> 0% of each run, Pallas kernels for 28% -> 29%
where the time goes in v5:
time: 82.7 us; the launch traced here: 82.3 us
  starting transfers between devices  40.6 us (49%)
  Pallas kernels  32.9 us (40%)
  waiting for transfers between devices  6.96 us (8%)
  local copies, waits for them, and re-layouts  0.98 us (1%)
    pallas_call x2, Pallas kernels, near_side(): call(kernel, shaped(LD, 8, LEAF), [SMEM, VMEM, VMEM], scratch, flops=9 *...  15.7 us
    all_to_all x1, starting transfers between devices, body(): every = lax.all_to_all(whole, 'blk', 0, 0, tiled=True)  14.4 us
    all_to_all x1, starting transfers between devices, body(): came = lax.all_to_all(slots, 'along', 0, 0, tiled=True)  7.49 us
    pallas_call x1, Pallas kernels, near_own(): call(near_own_kernel, shaped(LD, 8, LEAF), [VMEM], scratch, flops=9 * 10...  6.58 us
    ppermute x1, waiting for transfers between devices, body(): onward = lax.ppermute(onward, 'blk', stride)  5.02 us
    ppermute x1, starting transfers between devices, body(): partner = lax.ppermute(tall, 'blk', flip)  4.86 us
    ppermute x1, starting transfers between devices, body(): other = lax.ppermute(beside, 'blk', flip)  4.46 us
    pallas_call x1, Pallas kernels, finish(): call(finish_kernel, shaped(RHS, LD, LEAF), ins, scratch, flops=4 * 10 ** 9)  4.38 us
  transfers between devices with their start and end apart: 7, of which 3 were waited for; matrix products, arithmetic and copies ran while one was open for 0% of the time, Pallas kernels for 29%

profile of v5, /device:TPU:1, one launch (start us, length us, event | category | flops | bytes accessed | tf_op | source)
XLA Modules:
  0.0 82.3 jit_solution(9103755868065944245)
XLA Ops:
  0.0 0.6 pad_add_fusion.at_ref
  0.6 3.7 %shard_map.100 = (f32[24,8,256]{2,1,0:T(8,128)}, f32[8,8,384]{2,1,0:T(8,128)}) custom-call(s32[2]{0:T(128)} %pad_add_fusion.at_ref, f32[3,24,256]{2,1,0:T(8,128)} %bitcast.21, f32[3,24,256]{2,1,0:T(8,128)} %bitcast.22, f32[24,256]{1,0:T(8,128)} %bitcast.23, f32[24,64,256]{2,1,0:T(8,128)} %bitcast.14, f32[24,64,64]{2,1,0:T(8,128)} %bitcast.17, f32[64,64]{1,0:T(8,128)} %bitcast.19), custom_call_target="tpu_custom_call" | custom-call | flops 1000000000 | bytes 1048576 | tf_op jit(solution)/shard_map/pallas_call | solution.py:377
  4.3 7.5 %all-to-all-start = ((f32[8,8,384]{2,1,0:T(8,128)}), f32[8,8,384]{2,1,0:T(8,128)S(1)}, u32[]{:S(2)}, u32[]{:S(2)}) async-start(f32[8,8,384]{2,1,0:T(8,128)} %get-tuple-element.21), calls=%async_computation | async-start | bytes 196608 | tf_op jit(solution)/shard_map/all_to_all | solution.py:418
  11.8 0.0 copy-start.8
  11.8 0.9 %copy-done.8 = f32[24,8,256]{2,1,0:T(8,128)S(1)} copy-done((f32[24,8,256]{2,1,0:T(8,128)S(1)}, f32[24,8,256]{2,1,0:T(8,128)}, u32[]{:S(2)}) %copy-start.8) | copy-done | bytes 196632
  12.7 0.0 copy-start
  12.7 0.0 copy-start.9
  12.7 6.6 %shard_map.101.refs_9_ = f32[24,8,256]{2,1,0:T(8,128)S(1)} custom-call(f32[24,8,256]{2,1,0:T(8,128)S(1)} %copy-done.8), custom_call_target="tpu_custom_call" | custom-call | flops 8999999488 | bytes 1048576 | tf_op jit(solution)/shard_map/pallas_call | solution.py:382
  19.3 0.0 all-to-all-done.came_ref
  19.3 0.0 copy-done
  19.3 0.0 copy-done.9
  19.4 1.3 %shard_map.102 = (f32[26,8,256]{2,1,0:T(8,128)S(1)}, f32[64,2,128]{2,1,0:T(2,128)}) custom-call(s32[2]{0:T(128)S(1)} %copy-done, f32[8,8,384]{2,1,0:T(8,128)S(1)} %all-to-all-done.came_ref, f32[24,8,256]{2,1,0:T(8,128)S(1)} %copy-done.9), custom_call_target="tpu_custom_call" | custom-call | flops 100000000 | bytes 1048576 | tf_op jit(solution)/shard_map/pallas_call | solution.py:421
  20.6 4.9 %collective-permute-start = (f32[26,8,256]{2,1,0:T(8,128)S(1)}, f32[26,8,256]{2,1,0:T(8,128)S(1)}, u32[]{:S(2)}, u32[]{:S(2)}) collective-permute-start(f32[26,8,256]{2,1,0:T(8,128)S(1)} %get-tuple-element.24.tall_ref), channel_id=1, source_target_pairs={{0,8},{8,0},{16,24},{24,16},{32,40},{40,32},{48,56},{56,48},{64,72... | collective-permute-start | bytes 638984 | tf_op jit(solution)/shard_map/ppermute | solution.py:427
  25.5 1.1 %collective-permute-done.partner_ref.came_ref = f32[26,8,256]{2,1,0:T(8,128)S(1)} collective-permute-done((f32[26,8,256]{2,1,0:T(8,128)S(1)}, f32[26,8,256]{2,1,0:T(8,128)S(1)}, u32[]{:S(2)}, u32[]{:S(2)}) %collective-permute-start) | collective-permute-done | bytes 213024 | tf_op jit(solution)/shard_map/ppermute | solution.py:427
  26.6 14.4 %all-to-all-start.1 = ((f32[64,2,128]{2,1,0:T(2,128)}), f32[64,2,128]{2,1,0:T(2,128)S(1)}, u32[]{:S(2)}, u32[]{:S(2)}) async-start(f32[64,2,128]{2,1,0:T(2,128)} %get-tuple-element.30), calls=%async_computation.1 | async-start | bytes 131072 | tf_op jit(solution)/shard_map/all_to_all | solution.py:433
  41.0 3.5 %collective-permute-start.1 = (f32[30,8,256]{2,1,0:T(8,128)S(1)}, f32[30,8,256]{2,1,0:T(8,128)S(1)}, u32[]{:S(2)}, u32[]{:S(2)}) collective-permute-start(f32[30,8,256]{2,1,0:T(8,128)S(1)} %shard_map.103), channel_id=1, source_target_pairs={{0,504},{8,16},{16,8},{24,32},{32,24},{40,48},{48,40},{56,64},{64,... | collective-permute-start | bytes 737288 | tf_op jit(solution)/shard_map/ppermute | solution.py:430
  44.5 7.8 %shard_map.104.refs_10_ = f32[24,8,256]{2,1,0:T(8,128)S(1)} custom-call(s32[2]{0:T(128)S(1)} %copy-done, f32[26,8,256]{2,1,0:T(8,128)S(1)} %get-tuple-element.24.tall_ref, f32[26,8,256]{2,1,0:T(8,128)S(1)} %collective-permute-done.partner_ref.came_ref), custom_call_target="tpu_custom_call" | custom-call | flops 8999999488 | bytes 20000000 | tf_op jit(solution)/shard_map/pallas_call | solution.py:388
  52.4 0.0 collective-permute-done.1.came_ref
  52.4 0.6 shard_map.105.beside_ref
  53.0 4.5 %collective-permute-start.2 = (f32[2,40,128]{2,1,0:T(8,128)S(1)}, f32[2,40,128]{2,1,0:T(8,128)S(1)}, u32[]{:S(2)}, u32[]{:S(2)}) collective-permute-start(f32[2,40,128]{2,1,0:T(8,128)S(1)} %shard_map.105.beside_ref), channel_id=1, source_target_pairs={{0,8},{8,0},{16,24},{24,16},{32,40},{40,32},{48,56},{56,48},{64,72... | collective-permute-start | bytes 122888 | tf_op jit(solution)/shard_map/ppermute | solution.py:435
  57.5 0.8 %collective-permute-done.2.other_ref = f32[2,40,128]{2,1,0:T(8,128)S(1)} collective-permute-done((f32[2,40,128]{2,1,0:T(8,128)S(1)}, f32[2,40,128]{2,1,0:T(8,128)S(1)}, u32[]{:S(2)}, u32[]{:S(2)}) %collective-permute-start.2) | collective-permute-done | bytes 40992 | tf_op jit(solution)/shard_map/ppermute | solution.py:435
  58.4 0.6 shard_map.106
  59.0 1.9 %collective-permute-start.3 = (f32[4,40,128]{2,1,0:T(8,128)S(1)}, f32[4,40,128]{2,1,0:T(8,128)S(1)}, u32[]{:S(2)}, u32[]{:S(2)}) collective-permute-start(f32[4,40,128]{2,1,0:T(8,128)S(1)} %get-tuple-element.32), channel_id=1, source_target_pairs={{0,488},{8,32},{16,504},{24,48},{32,8},{40,64},{48,24},{56,80},{64... | collective-permute-start | bytes 245768 | tf_op jit(solution)/shard_map/ppermute | solution.py:439
  60.9 0.0 all-to-all-done.1.refs_5_
  60.9 0.0 copy-start.1
  60.9 0.0 copy-start.2
  60.9 0.0 copy-start.3
  61.0 0.0 copy-start.4
  61.0 0.0 copy-start.5
  61.0 0.0 copy-start.6
  61.0 0.0 copy-start.7
  61.0 5.0 %collective-permute-done.3.refs_2_ = f32[4,40,128]{2,1,0:T(8,128)S(1)} collective-permute-done((f32[4,40,128]{2,1,0:T(8,128)S(1)}, f32[4,40,128]{2,1,0:T(8,128)S(1)}, u32[]{:S(2)}, u32[]{:S(2)}) %collective-permute-start.3) | collective-permute-done | bytes 81952 | tf_op jit(solution)/shard_map/ppermute | solution.py:439
  66.0 4.0 %collective-permute-start.4 = (f32[4,40,128]{2,1,0:T(8,128)S(1)}, f32[4,40,128]{2,1,0:T(8,128)S(1)}, u32[]{:S(2)}, u32[]{:S(2)}) collective-permute-start(f32[4,40,128]{2,1,0:T(8,128)S(1)} %collective-permute-done.3.refs_2_), channel_id=1, source_target_pairs={{0,8},{8,0},{16,24},{24,16},{32,40},{40,32},{48,56},{56,48},{64,72... | collective-permute-start | bytes 245768 | tf_op jit(solution)/shard_map/ppermute | solution.py:442
  70.0 7.8 %shard_map.107.refs_11_ = f32[24,8,256]{2,1,0:T(8,128)S(1)} custom-call(s32[2]{0:T(128)S(1)} %copy-done, f32[26,8,256]{2,1,0:T(8,128)S(1)} %get-tuple-element.24.tall_ref, f32[30,8,256]{2,1,0:T(8,128)S(1)} %collective-permute-done.1.came_ref), custom_call_target="tpu_custom_call" | custom-call | flops 8999999488 | bytes 20000000 | tf_op jit(solution)/shard_map/pallas_call | solution.py:388
  77.8 0.0 collective-permute-done.4.refs_3_
  77.9 0.0 copy-done.1
  77.9 0.0 copy-done.2
  77.9 0.0 copy-done.3
  77.9 0.0 copy-done.4
  77.9 0.0 copy-done.5
  77.9 0.0 copy-done.6
  77.9 0.0 copy-done.7
  77.9 4.4 %shard_map.108 = f32[3,24,256]{2,1,0:T(8,128)} custom-call(s32[2]{0:T(128)S(1)} %copy-done, s32[1,30]{1,0:T(1,128)S(1)} %copy-done.6, s32[1,64]{1,0:T(1,128)S(1)} %copy-done.7, f32[30,64,64]{2,1,0:T(8,128)S(1)} %bitcast.16, f32[6,40,128]{2,1,0:T(8,128)S(1)} %get-tuple-element.31.refs_1_, f32[4,40,128]{2,1,0:T(8,128)S(1)} %collective-permute-done.3.refs_2_, ...), custom_call_target="tpu_custom_call" | custom-call | flops 4000000000 | bytes 1048576 | tf_op jit(solution)/shard_map/pallas_call | solution.py:394
  (1 shorter events, 0.0 us)
Async XLA Ops:
  4.3 15.0 %all-to-all-start = ((f32[8,8,384]{2,1,0:T(8,128)}), f32[8,8,384]{2,1,0:T(8,128)S(1)}, u32[]{:S(2)}, u32[]{:S(2)}) async-start(f32[8,8,384]{2,1,0:T(8,128)} %get-tuple-element.21), calls=%async_computation | async-start | bytes 196608 | tf_op jit(solution)/shard_map/all_to_all | solution.py:418
  11.8 0.9 %copy-start.8 = (f32[24,8,256]{2,1,0:T(8,128)S(1)}, f32[24,8,256]{2,1,0:T(8,128)}, u32[]{:S(2)}) copy-start(f32[24,8,256]{2,1,0:T(8,128)} %get-tuple-element.22.wire_ref) | copy-start | bytes 589828
  12.7 6.6 %copy-start = (s32[2]{0:T(128)S(1)}, s32[2]{0:T(128)}, u32[]{:S(2)}) copy-start(s32[2]{0:T(128)} %pad_add_fusion.at_ref) | copy-start | bytes 28
  12.7 6.6 %copy-start.9 = (f32[24,8,256]{2,1,0:T(8,128)S(1)}, f32[24,8,256]{2,1,0:T(8,128)}, u32[]{:S(2)}) copy-start(f32[24,8,256]{2,1,0:T(8,128)} %get-tuple-element.22.wire_ref) | copy-start | bytes 589828
  20.6 5.9 %collective-permute-start = (f32[26,8,256]{2,1,0:T(8,128)S(1)}, f32[26,8,256]{2,1,0:T(8,128)S(1)}, u32[]{:S(2)}, u32[]{:S(2)}) collective-permute-start(f32[26,8,256]{2,1,0:T(8,128)S(1)} %get-tuple-element.24.tall_ref), channel_id=1, source_target_pairs={{0,8},{8,0},{16,24},{24,16},{32,40},{40,32},{48,56},{56,48},{64,72... | collective-permute-start | bytes 638984 | tf_op jit(solution)/shard_map/ppermute | solution.py:427
  26.6 34.3 %all-to-all-start.1 = ((f32[64,2,128]{2,1,0:T(2,128)}), f32[64,2,128]{2,1,0:T(2,128)S(1)}, u32[]{:S(2)}, u32[]{:S(2)}) async-start(f32[64,2,128]{2,1,0:T(2,128)} %get-tuple-element.30), calls=%async_computation.1 | async-start | bytes 131072 | tf_op jit(solution)/shard_map/all_to_all | solution.py:433
  41.0 11.4 %collective-permute-start.1 = (f32[30,8,256]{2,1,0:T(8,128)S(1)}, f32[30,8,256]{2,1,0:T(8,128)S(1)}, u32[]{:S(2)}, u32[]{:S(2)}) collective-permute-start(f32[30,8,256]{2,1,0:T(8,128)S(1)} %shard_map.103), channel_id=1, source_target_pairs={{0,504},{8,16},{16,8},{24,32},{32,24},{40,48},{48,40},{56,64},{64,... | collective-permute-start | bytes 737288 | tf_op jit(solution)/shard_map/ppermute | solution.py:430
  53.0 5.3 %collective-permute-start.2 = (f32[2,40,128]{2,1,0:T(8,128)S(1)}, f32[2,40,128]{2,1,0:T(8,128)S(1)}, u32[]{:S(2)}, u32[]{:S(2)}) collective-permute-start(f32[2,40,128]{2,1,0:T(8,128)S(1)} %shard_map.105.beside_ref), channel_id=1, source_target_pairs={{0,8},{8,0},{16,24},{24,16},{32,40},{40,32},{48,56},{56,48},{64,72... | collective-permute-start | bytes 122888 | tf_op jit(solution)/shard_map/ppermute | solution.py:435
  59.0 7.0 %collective-permute-start.3 = (f32[4,40,128]{2,1,0:T(8,128)S(1)}, f32[4,40,128]{2,1,0:T(8,128)S(1)}, u32[]{:S(2)}, u32[]{:S(2)}) collective-permute-start(f32[4,40,128]{2,1,0:T(8,128)S(1)} %get-tuple-element.32), channel_id=1, source_target_pairs={{0,488},{8,32},{16,504},{24,48},{32,8},{40,64},{48,24},{56,80},{64... | collective-permute-start | bytes 245768 | tf_op jit(solution)/shard_map/ppermute | solution.py:439
  60.9 16.9 %copy-start.1 = (f32[1,64,64,64]{3,2,1,0:T(8,128)S(1)}, f32[1,64,64,64]{3,2,1,0:T(8,128)}, u32[]{:S(2)}) copy-start(f32[1,64,64,64]{3,2,1,0:T(8,128)} %param.18) | copy-start | bytes 3145732
  60.9 16.9 %copy-start.2 = (f32[1,24,64,256]{3,2,1,0:T(8,128)S(1)}, f32[1,24,64,256]{3,2,1,0:T(8,128)}, u32[]{:S(2)}) copy-start(f32[1,24,64,256]{3,2,1,0:T(8,128)} %param.13) | copy-start | bytes 4718596
  60.9 16.9 %copy-start.3 = (f32[1,30,64,64]{3,2,1,0:T(8,128)S(1)}, f32[1,30,64,64]{3,2,1,0:T(8,128)}, u32[]{:S(2)}) copy-start(f32[1,30,64,64]{3,2,1,0:T(8,128)} %param.16) | copy-start | bytes 1474564
  61.0 16.9 %copy-start.4 = (f32[1,24,64,64]{3,2,1,0:T(8,128)S(1)}, f32[1,24,64,64]{3,2,1,0:T(8,128)}, u32[]{:S(2)}) copy-start(f32[1,24,64,64]{3,2,1,0:T(8,128)} %param.14) | copy-start | bytes 1179652
  61.0 16.9 %copy-start.5 = (f32[1,1,64,64]{3,2,1,0:T(8,128)S(1)}, f32[1,1,64,64]{3,2,1,0:T(8,128)}, u32[]{:S(2)}) copy-start(f32[1,1,64,64]{3,2,1,0:T(8,128)} %param.15) | copy-start | bytes 49156
  61.0 16.9 %copy-start.6 = (s32[1,30]{1,0:T(1,128)S(1)}, s32[1,30]{1,0:T(1,128)}, u32[]{:S(2)}) copy-start(s32[1,30]{1,0:T(1,128)} %mask_ref.1) | copy-start | bytes 364
  61.0 16.9 %copy-start.7 = (s32[1,64]{1,0:T(1,128)S(1)}, s32[1,64]{1,0:T(1,128)}, u32[]{:S(2)}) copy-start(s32[1,64]{1,0:T(1,128)} %admissible_ref.1) | copy-start | bytes 772
  66.0 11.8 %collective-permute-start.4 = (f32[4,40,128]{2,1,0:T(8,128)S(1)}, f32[4,40,128]{2,1,0:T(8,128)S(1)}, u32[]{:S(2)}, u32[]{:S(2)}) collective-permute-start(f32[4,40,128]{2,1,0:T(8,128)S(1)} %collective-permute-done.3.refs_2_), channel_id=1, source_target_pairs={{0,8},{8,0},{16,24},{24,16},{32,40},{40,32},{48,56},{56,48},{64,72... | collective-permute-start | bytes 245768 | tf_op jit(solution)/shard_map/ppermute | solution.py:442

commit v6 on v5

--- a/solution.py
+++ b/solution.py
@@ -28,7 +28,8 @@
 BY_LAST = (((1,), (1,)), ((), ()))
 MIB = 2**20
 FULL = 60 * MIB + 128 * 1024
-OWN_TURN = 3
+TURN_OWN = 6
+TURN = 3
 UP_PARTS = 4
 UP_LEAVES = LD // UP_PARTS
 
@@ -125,24 +126,27 @@
         slots_ref[j, :, LEAF:] = share
 
 
-def joined_kernel(at_ref, came_ref, wire_ref, tall_ref, whole_ref):
+def tall_kernel(at_ref, came_ref, wire_ref, tall_ref):
     here = at_ref[0]
+    lower = came_ref[jnp.maximum(here - 1, 0), :, :LEAF]
+    upper = came_ref[jnp.minimum(here + 1, 7), :, :LEAF]
+    tall_ref[0] = jnp.where(here > 0, lower, 0.0)
+    tall_ref[1 : LD + 1] = wire_ref[...]
+    tall_ref[LD + 1] = jnp.where(here < 7, upper, 0.0)
+
+
+def whole_kernel(came_ref, whole_ref):
     total = came_ref[0, :, LEAF:]
     for j in range(1, 8):
         total = total + came_ref[j, :, LEAF:]
-    packed = jnp.concatenate(
+    both = jnp.concatenate(
         [
             jnp.concatenate([total[0:1, :RANK], total[1:2, :RANK]], 1),
             jnp.concatenate([total[2:3, :RANK], jnp.zeros((1, RANK), F32)], 1),
         ],
         0,
     )
-    whole_ref[...] = jnp.broadcast_to(packed[None], whole_ref.shape)
-    lower = came_ref[jnp.maximum(here - 1, 0), :, :LEAF]
-    upper = came_ref[jnp.minimum(here + 1, 7), :, :LEAF]
-    tall_ref[0] = jnp.where(here > 0, lower, 0.0)
-    tall_ref[1 : LD + 1] = wire_ref[...]
-    tall_ref[LD + 1] = jnp.where(here < 7, upper, 0.0)
+    whole_ref[...] = jnp.broadcast_to(both[None], whole_ref.shape)
 
 
 def source_side(leaf, around, steps, slot, points_ref, loads_ref):
@@ -193,19 +197,19 @@
     lax.fori_loop(0, LD, prepare, 0, unroll=12)
 
     def turn(g, _):
-        leaves = [g * OWN_TURN + n for n in range(OWN_TURN)]
-        places = [(n, step) for n in range(OWN_TURN) for step in (-1, 0, 1)]
+        leaves = [g * TURN_OWN + n for n in range(TURN_OWN)]
+        places = [(n, step) for n in range(TURN_OWN) for step in (-1, 0, 1)]
         targets = [target_points(wire_ref[l]) for l in leaves]
         for place, (n, step) in enumerate(places):
             pair_kernel(targets[n], points_ref, leaves[n] + 1 + step, pairs_ref, place)
-        totals = [jnp.zeros((8, LEAF), F32)] * OWN_TURN
+        totals = [jnp.zeros((8, LEAF), F32)] * TURN_OWN
         for place, (n, step) in enumerate(places):
             totals[n] += pair_sum(wire_ref[leaves[n]], loads_ref, leaves[n] + 1 + step, pairs_ref, place, 0, step)
-        for n in range(OWN_TURN):
+        for n in range(TURN_OWN):
             near_ref[leaves[n]] = totals[n]
         return 0
 
-    lax.fori_loop(0, LD // OWN_TURN, turn, 0)
+    lax.fori_loop(0, LD // TURN_OWN, turn, 0)
 
 
 def near_side_kernel(beyond, at_ref, tall_ref, came_ref, near_ref, points_ref, loads_ref, pairs_ref):
@@ -221,20 +225,20 @@
     source_side(tall_ref[end], 0, (end_step,), TALL, points_ref, loads_ref)
 
     def turn(g, _):
-        leaves = [g * OWN_TURN + n for n in range(OWN_TURN)]
-        places = [(n, step) for n in range(OWN_TURN) for step in (-1, 0, 1)]
+        leaves = [g * TURN + n for n in range(TURN)]
+        places = [(n, step) for n in range(TURN) for step in (-1, 0, 1)]
         targets = [target_points(tall_ref[l + 1]) for l in leaves]
         for place, (n, step) in enumerate(places):
             pair_kernel(targets[n], points_ref, leaves[n] + 1 + step, pairs_ref, place)
-        totals = [jnp.zeros((8, LEAF), F32)] * OWN_TURN
+        totals = [jnp.zeros((8, LEAF), F32)] * TURN
         for place, (n, step) in enumerate(places):
             slot = leaves[n] + 1 + step
             totals[n] += pair_sum(tall_ref[leaves[n] + 1], loads_ref, slot, pairs_ref, place, around, step)
-        for n in range(OWN_TURN):
+        for n in range(TURN):
             near_ref[leaves[n]] = totals[n]
         return 0
 
-    lax.fori_loop(0, LD // OWN_TURN, turn, 0)
+    lax.fori_loop(0, LD // TURN, turn, 0)
     here = tall_ref[end_leaf + 1]
     pair_kernel(target_points(here), points_ref, TALL, pairs_ref, 0)
     near_ref[end_leaf] += pair_sum(here, loads_ref, TALL, pairs_ref, 0, 0, end_step)
@@ -273,13 +277,19 @@
     beside_ref[1] = jnp.where(even, first, second)
 
 
-def window_kernel(at_ref, tall_ref, partner_ref, beside_ref, other_ref, window_ref, onward_ref):
+def chip_kernel(at_ref, tall_ref, partner_ref, chip_ref):
     even = lax.rem(at_ref[1], 2) == 0
     own, partner = packed(coefs_of(tall_ref)), packed(coefs_of(partner_ref))
-    beside, other = [beside_ref[n] for n in range(2)], [other_ref[n] for n in range(2)]
+    chip_ref[0] = jnp.where(even, own, partner)
+    chip_ref[1] = jnp.where(even, partner, own)
+
+
+def window_kernel(at_ref, chip_ref, beside_ref, other_ref, window_ref, onward_ref):
+    even = lax.rem(at_ref[1], 2) == 0
+    chip, beside, other = ([ref[n] for n in range(2)] for ref in (chip_ref, beside_ref, other_ref))
     low = [jnp.where(even, beside[n], other[n]) for n in range(2)]
     high = [jnp.where(even, other[n], beside[n]) for n in range(2)]
-    window = low + [jnp.where(even, own, partner), jnp.where(even, partner, own)] + high
+    window = low + chip + high
     for n in range(6):
         window_ref[n] = window[n]
     for n in range(4):
@@ -298,12 +308,36 @@
     return high + (cross + lax.dot_general(xh, yl, BY_LAST, preferred_element_type=F32))
 
 
-def finish_kernel(at_ref, mask_ref, admissible_ref, *refs):
+def top_kernel(at_ref, admissible_ref, every_ref, top_ref, slab_ref, down_ref):
+    here = at_ref[1]
+    sectors = top_ref.shape[0]
+
+    def couple(t, sums):
+        apart = lax.rem(t - here + sectors, sectors)
+        distant = jnp.logical_and(apart > REACH, apart < sectors - REACH)
+        allowed = jnp.where(distant, admissible_ref[0, t], 0).astype(F32)
+        coupling = top_ref[t]
+        both = every_ref[t] * allowed
+        rows = (both[0:1, :RANK], both[0:1, RANK:], both[1:2, :RANK])
+        return tuple(s + coupling * row for s, row in zip(sums, rows))
+
+    nothing = jnp.zeros((RANK, RANK), F32)
+    sums = lax.fori_loop(0, sectors, couple, (nothing,) * 3, unroll=16)
+    lane = lax.broadcasted_iota(jnp.int32, (RANK, 128), 1)
+    columns = jnp.zeros((RANK, 128), F32)
+    for r in range(3):
+        columns = jnp.where(lane == r, jnp.sum(sums[r], axis=1, keepdims=True), columns)
+    local = jnp.transpose(columns, (1, 0))[:8]
+    down_ref[...] = exact_by_last(local, slab_ref[...])
+
+
+def finish_kernel(at_ref, mask_ref, *refs):
     count = len(refs) - 3
     local, out_ref = refs[:count], refs[count]
     far_ref, ring_ref = refs[count + 1 :]
     coupling_ref, window_ref, onward_ref, back_ref = local[:4]
-    top_ref, every_ref, slab_ref, transfer_ref, basis_ref, own_ref, side_ref, beyond_ref = local[4:]
+    down_ref, transfer_ref, basis_ref, own_ref, side_ref, beyond_ref = local[4:]
+    slab = down_ref[...]
 
     here = at_ref[1]
     odd = lax.rem(here, 2)
@@ -336,26 +370,6 @@
     for r in range(3):
         far_ref[r] = jnp.concatenate([far_columns[r], jnp.zeros((RANK, RANK - ROWS), F32)], 1)
 
-    sectors = top_ref.shape[0]
-
-    def couple(t, sums):
-        apart = lax.rem(t - here + sectors, sectors)
-        distant = jnp.logical_and(apart > REACH, apart < sectors - REACH)
-        allowed = jnp.where(distant, admissible_ref[0, t], 0).astype(F32)
-        coupling = top_ref[t]
-        both = every_ref[t] * allowed
-        rows = (both[0:1, :RANK], both[0:1, RANK:], both[1:2, :RANK])
-        return tuple(s + coupling * row for s, row in zip(sums, rows))
-
-    nothing = jnp.zeros((RANK, RANK), F32)
-    sums = lax.fori_loop(0, sectors, couple, (nothing,) * 3, unroll=16)
-    lane = lax.broadcasted_iota(jnp.int32, (RANK, 128), 1)
-    columns = jnp.zeros((RANK, 128), F32)
-    for r in range(3):
-        columns = jnp.where(lane == r, jnp.sum(sums[r], axis=1, keepdims=True), columns)
-    local = jnp.transpose(columns, (1, 0))[:8]
-    slab = exact_by_last(local, slab_ref[...])
-
     place = lax.broadcasted_iota(jnp.int32, (RANK, RANK), 1)
 
     def leaf(l, _):
@@ -378,19 +392,19 @@
 
 
 def near_own(wire):
-    scratch = near_scratch(TALL, 3 * OWN_TURN)
+    scratch = near_scratch(TALL, 3 * TURN_OWN)
     return call(near_own_kernel, shaped(LD, 8, LEAF), [VMEM], scratch, flops=9 * 10**9)(wire)
 
 
 def near_side(beyond, *args):
     kernel = functools.partial(near_side_kernel, beyond)
-    scratch = near_scratch(TALL + 1, 3 * OWN_TURN)
+    scratch = near_scratch(TALL + 1, 3 * TURN)
     return call(kernel, shaped(LD, 8, LEAF), [SMEM, VMEM, VMEM], scratch, flops=9 * 10**9, bytes=2 * 10**7)(*args)
 
 
 def finish(*args):
     scratch = [pltpu.VMEM((3, RANK, RANK), F32), pltpu.VMEM((14, PACKED, 128), F32)]
-    ins = [SMEM] * 3 + [VMEM] * (len(args) - 3)
+    ins = [SMEM] * 2 + [VMEM] * (len(args) - 2)
     return call(finish_kernel, shaped(RHS, LD, LEAF), ins, scratch, flops=4 * 10**9)(*args)
 
 
@@ -418,31 +432,37 @@
     came = lax.all_to_all(slots, "along", 0, 0, tiled=True)
     own = near_own(wire)
     came, own = lax.optimization_barrier((came, own))
-    tall, whole = call(
-        joined_kernel, (shaped(TALL, 8, LEAF), shaped(sectors, 2, 128)), [SMEM, VMEM, VMEM], flops=10**8
-    )(at, came, wire)
+    tall = call(tall_kernel, shaped(TALL, 8, LEAF), [SMEM, VMEM, VMEM])(at, came, wire)
+    tall, came = lax.optimization_barrier((tall, came))
+    whole = call(whole_kernel, shaped(sectors, 2, 128), [VMEM])(came)
     flip = [(i, i ^ 1) for i in range(sectors)]
     step_out = [(i, (i + 1 if i % 2 else i - 1) % sectors) for i in range(sectors)]
     stride = [(i, (i + 3 if i % 2 else i - 3) % sectors) for i in range(sectors)]
     partner = lax.ppermute(tall, "blk", flip)
     records = call(pair_records_kernel, shaped(TALL + ROWS // 8, 8, LEAF), [VMEM] * 2)(tall, partner)
-    records, whole, partner = lax.optimization_barrier((records, whole, partner))
+    records, partner = lax.optimization_barrier((records, partner))
     came = lax.ppermute(records, "blk", step_out)
     side = near_side(False, at, tall, partner)
     came, side = lax.optimization_barrier((came, side))
     every = lax.all_to_all(whole, "blk", 0, 0, tiled=True)
     beside = call(beside_kernel, shaped(2, PACKED, 128), [SMEM, VMEM])(at, came)
     other = lax.ppermute(beside, "blk", flip)
+    partner, beside = lax.optimization_barrier((partner, beside))
+    chip = call(chip_kernel, shaped(2, PACKED, 128), [SMEM, VMEM, VMEM])(at, tall, partner)
     window, onward = call(
-        window_kernel, (shaped(6, PACKED, 128), shaped(4, PACKED, 128)), [SMEM] + [VMEM] * 4
-    )(at, tall, partner, beside, other)
+        window_kernel, (shaped(6, PACKED, 128), shaped(4, PACKED, 128)), [SMEM] + [VMEM] * 3
+    )(at, chip, beside, other)
     onward = lax.ppermute(onward, "blk", stride)
     window, came, every = lax.optimization_barrier((window, came, every))
     beyond = near_side(True, at, tall, came)
+    onward, beyond, every = lax.optimization_barrier((onward, beyond, every))
     back = lax.ppermute(onward, "blk", flip)
+    down = call(top_kernel, shaped(8, RANK), [SMEM] * 2 + [VMEM] * 3, flops=10**9)(
+        at, top_admissible, every, top_coupling[0], slab
+    )
     out = finish(
-        at, leaf_admissible_mask, top_admissible, leaf_coupling_matrices[0], window, onward, back,
-        top_coupling[0], every, slab, transfer, basis, own, side, beyond,
+        at, leaf_admissible_mask, leaf_coupling_matrices[0], window, onward, back, down,
+        transfer, basis, own, side, beyond,
     )
     return out[:, None]
 

time: 82.7 us -> 77.5 us (0.937)
  waiting for transfers between devices: 6.96 us -> 0.24 us
  starting transfers between devices: 40.6 us -> 41.6 us
    ppermute x1, waiting for transfers between devices: 5.02 us -> 0.01 us  [body(): onward = lax.ppermute(onward, 'blk', stride)]
    pallas_call x1 -> x4, Pallas kernels: 1.26 us -> 3.31 us  [the longest x1 1.4 us: body(): call(top_kernel, shaped(8, RANK), [SMEM] * 2 + [VMEM] * 3, flops=10 ** 9)]
    ppermute x1, waiting for transfers between devices: 1.07 us -> 0.01 us  [body(): partner = lax.ppermute(tall, 'blk', flip)]
    pallas_call x1, Pallas kernels: 4.38 us -> 3.42 us  [finish(): call(finish_kernel, shaped(RHS, LD, LEAF), ins, scratch, flops=4 * 10 ** 9)]
  transfers between devices with their start and end apart: 7 -> 7, of which waited for: 3 -> 1; matrix products, arithmetic and copies ran while one was open for 0% -> 0% of each run, Pallas kernels for 29% -> 33%
where the time goes in v6:
time: 77.5 us; the launch traced here: 77.1 us
  starting transfers between devices  41.6 us (54%)
  Pallas kernels  33.5 us (43%)
  local copies, waits for them, and re-layouts  0.98 us (1%)
    pallas_call x2, Pallas kernels, near_side(): call(kernel, shaped(LD, 8, LEAF), [SMEM, VMEM, VMEM], scratch, flops=9 *...  15.7 us
    all_to_all x1, starting transfers between devices, body(): every = lax.all_to_all(whole, 'blk', 0, 0, tiled=True)  14.1 us
    all_to_all x1, starting transfers between devices, body(): came = lax.all_to_all(slots, 'along', 0, 0, tiled=True)  7.49 us
    pallas_call x1, Pallas kernels, near_own(): call(near_own_kernel, shaped(LD, 8, LEAF), [VMEM], scratch, flops=9 * 10...  6.1 us
    ppermute x1, starting transfers between devices, body(): partner = lax.ppermute(tall, 'blk', flip)  5.35 us
    ppermute x1, starting transfers between devices, body(): back = lax.ppermute(onward, 'blk', flip)  4.59 us
    ppermute x1, starting transfers between devices, body(): other = lax.ppermute(beside, 'blk', flip)  4.48 us
    pallas_call x1, Pallas kernels, upward(): call(upward_kernel, outs, [SMEM] + [HBM] * 6, scratch, flops=10 ** 9, vme...  3.71 us
  transfers between devices with their start and end apart: 7, of which 1 were waited for; matrix products, arithmetic and copies ran while one was open for 0% of the time, Pallas kernels for 33%

profile of v6, /device:TPU:1, one launch (start us, length us, event | category | flops | bytes accessed | tf_op | source)
XLA Modules:
  0.0 77.1 jit_solution(261915918016859881)
XLA Ops:
  0.0 0.6 pad_add_fusion.at_ref
  0.6 3.7 %shard_map.100 = (f32[24,8,256]{2,1,0:T(8,128)}, f32[8,8,384]{2,1,0:T(8,128)}) custom-call(s32[2]{0:T(128)} %pad_add_fusion.at_ref, f32[3,24,256]{2,1,0:T(8,128)} %bitcast.21, f32[3,24,256]{2,1,0:T(8,128)} %bitcast.22, f32[24,256]{1,0:T(8,128)} %bitcast.23, f32[24,64,256]{2,1,0:T(8,128)} %bitcast.14, f32[24,64,64]{2,1,0:T(8,128)} %bitcast.17, f32[64,64]{1,0:T(8,128)} %bitcast.19), custom_call_target="tpu_custom_call" | custom-call | flops 1000000000 | bytes 1048576 | tf_op jit(solution)/shard_map/pallas_call | solution.py:391
  4.3 7.5 %all-to-all-start = ((f32[8,8,384]{2,1,0:T(8,128)}), f32[8,8,384]{2,1,0:T(8,128)S(1)}, u32[]{:S(2)}, u32[]{:S(2)}) async-start(f32[8,8,384]{2,1,0:T(8,128)} %get-tuple-element.25), calls=%async_computation | async-start | bytes 196608 | tf_op jit(solution)/shard_map/all_to_all | solution.py:432
  11.8 0.0 copy-start
  11.8 0.9 %copy-done = f32[24,8,256]{2,1,0:T(8,128)S(1)} copy-done((f32[24,8,256]{2,1,0:T(8,128)S(1)}, f32[24,8,256]{2,1,0:T(8,128)}, u32[]{:S(2)}) %copy-start) | copy-done | bytes 196632
  12.7 0.0 copy-start.1
  12.7 0.0 copy-start.2
  12.7 6.1 %shard_map.101.refs_7_ = f32[24,8,256]{2,1,0:T(8,128)S(1)} custom-call(f32[24,8,256]{2,1,0:T(8,128)S(1)} %copy-done), custom_call_target="tpu_custom_call" | custom-call | flops 8999999488 | bytes 1048576 | tf_op jit(solution)/shard_map/pallas_call | solution.py:396
  18.8 0.0 all-to-all-done.came_ref
  18.8 0.0 copy-done.1
  18.8 0.0 copy-done.2
  18.9 0.6 shard_map.102.tall_ref
  19.4 5.3 %collective-permute-start = (f32[26,8,256]{2,1,0:T(8,128)S(1)}, f32[26,8,256]{2,1,0:T(8,128)S(1)}, u32[]{:S(2)}, u32[]{:S(2)}) collective-permute-start(f32[26,8,256]{2,1,0:T(8,128)S(1)} %shard_map.102.tall_ref), channel_id=1, source_target_pairs={{0,8},{8,0},{16,24},{24,16},{32,40},{40,32},{48,56},{56,48},{64,72... | collective-permute-start | bytes 638984 | tf_op jit(solution)/shard_map/ppermute | solution.py:441
  24.8 0.7 shard_map.108
  25.5 14.1 %all-to-all-start.1 = ((f32[64,2,128]{2,1,0:T(2,128)}), f32[64,2,128]{2,1,0:T(2,128)S(1)}, u32[]{:S(2)}, u32[]{:S(2)}) async-start(f32[64,2,128]{2,1,0:T(2,128)} %shard_map.108), calls=%async_computation.1 | async-start | bytes 131072 | tf_op jit(solution)/shard_map/all_to_all | solution.py:447
  39.6 0.0 collective-permute-done.partner_ref.came_ref
  39.7 3.5 %collective-permute-start.1 = (f32[30,8,256]{2,1,0:T(8,128)S(1)}, f32[30,8,256]{2,1,0:T(8,128)S(1)}, u32[]{:S(2)}, u32[]{:S(2)}) collective-permute-start(f32[30,8,256]{2,1,0:T(8,128)S(1)} %shard_map.103), channel_id=1, source_target_pairs={{0,504},{8,16},{16,8},{24,32},{32,24},{40,48},{48,40},{56,64},{64,... | collective-permute-start | bytes 737288 | tf_op jit(solution)/shard_map/ppermute | solution.py:444
  43.2 7.8 %shard_map.104.refs_8_ = f32[24,8,256]{2,1,0:T(8,128)S(1)} custom-call(s32[2]{0:T(128)S(1)} %copy-done.2, f32[26,8,256]{2,1,0:T(8,128)S(1)} %shard_map.102.tall_ref, f32[26,8,256]{2,1,0:T(8,128)S(1)} %collective-permute-done.partner_ref.came_ref), custom_call_target="tpu_custom_call" | custom-call | flops 8999999488 | bytes 20000000 | tf_op jit(solution)/shard_map/pallas_call | solution.py:402
  51.1 0.0 collective-permute-done.1.came_ref
  51.1 0.6 shard_map.105.beside_ref
  51.7 4.5 %collective-permute-start.2 = (f32[2,40,128]{2,1,0:T(8,128)S(1)}, f32[2,40,128]{2,1,0:T(8,128)S(1)}, u32[]{:S(2)}, u32[]{:S(2)}) collective-permute-start(f32[2,40,128]{2,1,0:T(8,128)S(1)} %shard_map.105.beside_ref), channel_id=1, source_target_pairs={{0,8},{8,0},{16,24},{24,16},{32,40},{40,32},{48,56},{56,48},{64,72... | collective-permute-start | bytes 122888 | tf_op jit(solution)/shard_map/ppermute | solution.py:449
  56.2 0.6 shard_map.106.chip_ref
  56.8 0.2 collective-permute-done.2.other_ref
  57.1 0.6 shard_map.107
  57.6 0.0 all-to-all-done.1.every_ref
  57.6 0.0 copy-start.3
  57.6 0.0 copy-start.7
  57.7 0.0 copy-start.8
  57.7 2.1 %collective-permute-start.3 = (f32[4,40,128]{2,1,0:T(8,128)S(1)}, f32[4,40,128]{2,1,0:T(8,128)S(1)}, u32[]{:S(2)}, u32[]{:S(2)}) collective-permute-start(f32[4,40,128]{2,1,0:T(8,128)S(1)} %get-tuple-element.37), channel_id=1, source_target_pairs={{0,488},{8,32},{16,504},{24,48},{32,8},{40,64},{48,24},{56,80},{64... | collective-permute-start | bytes 245768 | tf_op jit(solution)/shard_map/ppermute | solution.py:455
  59.7 7.9 %shard_map.109.refs_9_ = f32[24,8,256]{2,1,0:T(8,128)S(1)} custom-call(s32[2]{0:T(128)S(1)} %copy-done.2, f32[26,8,256]{2,1,0:T(8,128)S(1)} %shard_map.102.tall_ref, f32[30,8,256]{2,1,0:T(8,128)S(1)} %collective-permute-done.1.came_ref), custom_call_target="tpu_custom_call" | custom-call | flops 8999999488 | bytes 20000000 | tf_op jit(solution)/shard_map/pallas_call | solution.py:402
  67.6 0.0 copy-start.4
  67.6 0.0 copy-start.5
  67.6 0.0 copy-start.6
  67.6 0.0 copy-start.9
  67.6 0.0 collective-permute-done.3.refs_2_
  67.6 4.6 %collective-permute-start.4 = (f32[4,40,128]{2,1,0:T(8,128)S(1)}, f32[4,40,128]{2,1,0:T(8,128)S(1)}, u32[]{:S(2)}, u32[]{:S(2)}) collective-permute-start(f32[4,40,128]{2,1,0:T(8,128)S(1)} %collective-permute-done.3.refs_2_), channel_id=1, source_target_pairs={{0,8},{8,0},{16,24},{24,16},{32,40},{40,32},{48,56},{56,48},{64,72... | collective-permute-start | bytes 245768 | tf_op jit(solution)/shard_map/ppermute | solution.py:459
  72.2 0.0 copy-done.3
  72.2 0.0 copy-done.7
  72.2 0.0 copy-done.8
  72.3 1.4 %shard_map.110.refs_4_ = f32[8,64]{1,0:T(8,128)S(1)} custom-call(s32[2]{0:T(128)S(1)} %copy-done.2, s32[1,64]{1,0:T(1,128)S(1)} %copy-done.8, f32[64,2,128]{2,1,0:T(2,128)S(1)} %all-to-all-done.1.every_ref, f32[64,64,64]{2,1,0:T(8,128)S(1)} %bitcast.13, f32[64,64]{1,0:T(8,128)S(1)} %bitcast.20), custom_call_target="tpu_custom_call" | custom-call | flops 1000000000 | bytes 1048576 | tf_op jit(solution)/shard_map/pallas_call | solution.py:460
  73.7 0.0 collective-permute-done.4.refs_3_
  73.7 0.0 copy-done.4
  73.7 0.0 copy-done.5
  73.7 0.0 copy-done.6
  73.7 0.0 copy-done.9
  73.7 3.4 %shard_map.111 = f32[3,24,256]{2,1,0:T(8,128)} custom-call(s32[2]{0:T(128)S(1)} %copy-done.2, s32[1,30]{1,0:T(1,128)S(1)} %copy-done.9, f32[30,64,64]{2,1,0:T(8,128)S(1)} %bitcast.16, f32[6,40,128]{2,1,0:T(8,128)S(1)} %get-tuple-element.36.refs_1_, f32[4,40,128]{2,1,0:T(8,128)S(1)} %collective-permute-done.3.refs_2_, ...), custom_call_target="tpu_custom_call" | custom-call | flops 4000000000 | bytes 1048576 | tf_op jit(solution)/shard_map/pallas_call | solution.py:408
  (1 shorter events, 0.0 us)
Async XLA Ops:
  4.3 14.5 %all-to-all-start = ((f32[8,8,384]{2,1,0:T(8,128)}), f32[8,8,384]{2,1,0:T(8,128)S(1)}, u32[]{:S(2)}, u32[]{:S(2)}) async-start(f32[8,8,384]{2,1,0:T(8,128)} %get-tuple-element.25), calls=%async_computation | async-start | bytes 196608 | tf_op jit(solution)/shard_map/all_to_all | solution.py:432
  11.8 0.9 %copy-start = (f32[24,8,256]{2,1,0:T(8,128)S(1)}, f32[24,8,256]{2,1,0:T(8,128)}, u32[]{:S(2)}) copy-start(f32[24,8,256]{2,1,0:T(8,128)} %get-tuple-element.26.wire_ref) | copy-start | bytes 589828
  12.7 6.1 %copy-start.1 = (f32[24,8,256]{2,1,0:T(8,128)S(1)}, f32[24,8,256]{2,1,0:T(8,128)}, u32[]{:S(2)}) copy-start(f32[24,8,256]{2,1,0:T(8,128)} %get-tuple-element.26.wire_ref) | copy-start | bytes 589828
  12.7 6.1 %copy-start.2 = (s32[2]{0:T(128)S(1)}, s32[2]{0:T(128)}, u32[]{:S(2)}) copy-start(s32[2]{0:T(128)} %pad_add_fusion.at_ref) | copy-start | bytes 28
  19.4 20.2 %collective-permute-start = (f32[26,8,256]{2,1,0:T(8,128)S(1)}, f32[26,8,256]{2,1,0:T(8,128)S(1)}, u32[]{:S(2)}, u32[]{:S(2)}) collective-permute-start(f32[26,8,256]{2,1,0:T(8,128)S(1)} %shard_map.102.tall_ref), channel_id=1, source_target_pairs={{0,8},{8,0},{16,24},{24,16},{32,40},{40,32},{48,56},{56,48},{64,72... | collective-permute-start | bytes 638984 | tf_op jit(solution)/shard_map/ppermute | solution.py:441
  25.5 32.1 %all-to-all-start.1 = ((f32[64,2,128]{2,1,0:T(2,128)}), f32[64,2,128]{2,1,0:T(2,128)S(1)}, u32[]{:S(2)}, u32[]{:S(2)}) async-start(f32[64,2,128]{2,1,0:T(2,128)} %shard_map.108), calls=%async_computation.1 | async-start | bytes 131072 | tf_op jit(solution)/shard_map/all_to_all | solution.py:447
  39.7 11.4 %collective-permute-start.1 = (f32[30,8,256]{2,1,0:T(8,128)S(1)}, f32[30,8,256]{2,1,0:T(8,128)S(1)}, u32[]{:S(2)}, u32[]{:S(2)}) collective-permute-start(f32[30,8,256]{2,1,0:T(8,128)S(1)} %shard_map.103), channel_id=1, source_target_pairs={{0,504},{8,16},{16,8},{24,32},{32,24},{40,48},{48,40},{56,64},{64,... | collective-permute-start | bytes 737288 | tf_op jit(solution)/shard_map/ppermute | solution.py:444
  51.7 5.3 %collective-permute-start.2 = (f32[2,40,128]{2,1,0:T(8,128)S(1)}, f32[2,40,128]{2,1,0:T(8,128)S(1)}, u32[]{:S(2)}, u32[]{:S(2)}) collective-permute-start(f32[2,40,128]{2,1,0:T(8,128)S(1)} %shard_map.105.beside_ref), channel_id=1, source_target_pairs={{0,8},{8,0},{16,24},{24,16},{32,40},{40,32},{48,56},{56,48},{64,72... | collective-permute-start | bytes 122888 | tf_op jit(solution)/shard_map/ppermute | solution.py:449
  57.6 14.6 %copy-start.3 = (f32[1,64,64,64]{3,2,1,0:T(8,128)S(1)}, f32[1,64,64,64]{3,2,1,0:T(8,128)}, u32[]{:S(2)}) copy-start(f32[1,64,64,64]{3,2,1,0:T(8,128)} %param.18) | copy-start | bytes 3145732
  57.6 14.6 %copy-start.7 = (f32[1,1,64,64]{3,2,1,0:T(8,128)S(1)}, f32[1,1,64,64]{3,2,1,0:T(8,128)}, u32[]{:S(2)}) copy-start(f32[1,1,64,64]{3,2,1,0:T(8,128)} %param.15) | copy-start | bytes 49156
  57.7 14.6 %copy-start.8 = (s32[1,64]{1,0:T(1,128)S(1)}, s32[1,64]{1,0:T(1,128)}, u32[]{:S(2)}) copy-start(s32[1,64]{1,0:T(1,128)} %admissible_ref.1) | copy-start | bytes 772
  57.7 10.0 %collective-permute-start.3 = (f32[4,40,128]{2,1,0:T(8,128)S(1)}, f32[4,40,128]{2,1,0:T(8,128)S(1)}, u32[]{:S(2)}, u32[]{:S(2)}) collective-permute-start(f32[4,40,128]{2,1,0:T(8,128)S(1)} %get-tuple-element.37), channel_id=1, source_target_pairs={{0,488},{8,32},{16,504},{24,48},{32,8},{40,64},{48,24},{56,80},{64... | collective-permute-start | bytes 245768 | tf_op jit(solution)/shard_map/ppermute | solution.py:455
  67.6 6.1 %copy-start.4 = (f32[1,24,64,256]{3,2,1,0:T(8,128)S(1)}, f32[1,24,64,256]{3,2,1,0:T(8,128)}, u32[]{:S(2)}) copy-start(f32[1,24,64,256]{3,2,1,0:T(8,128)} %param.13) | copy-start | bytes 4718596
  67.6 6.1 %copy-start.5 = (f32[1,30,64,64]{3,2,1,0:T(8,128)S(1)}, f32[1,30,64,64]{3,2,1,0:T(8,128)}, u32[]{:S(2)}) copy-start(f32[1,30,64,64]{3,2,1,0:T(8,128)} %param.16) | copy-start | bytes 1474564
  67.6 6.1 %copy-start.6 = (f32[1,24,64,64]{3,2,1,0:T(8,128)S(1)}, f32[1,24,64,64]{3,2,1,0:T(8,128)}, u32[]{:S(2)}) copy-start(f32[1,24,64,64]{3,2,1,0:T(8,128)} %param.14) | copy-start | bytes 1179652
  67.6 6.1 %copy-start.9 = (s32[1,30]{1,0:T(1,128)S(1)}, s32[1,30]{1,0:T(1,128)}, u32[]{:S(2)}) copy-start(s32[1,30]{1,0:T(1,128)} %mask_ref.1) | copy-start | bytes 364
  67.6 6.0 %collective-permute-start.4 = (f32[4,40,128]{2,1,0:T(8,128)S(1)}, f32[4,40,128]{2,1,0:T(8,128)S(1)}, u32[]{:S(2)}, u32[]{:S(2)}) collective-permute-start(f32[4,40,128]{2,1,0:T(8,128)S(1)} %collective-permute-done.3.refs_2_), channel_id=1, source_target_pairs={{0,8},{8,0},{16,24},{24,16},{32,40},{40,32},{48,56},{56,48},{64,72... | collective-permute-start | bytes 245768 | tf_op jit(solution)/shard_map/ppermute | solution.py:459

commit v7 on v6

--- a/solution.py
+++ b/solution.py
@@ -56,7 +56,7 @@
 
 
 def upward_kernel(
-    at_ref, values_hbm, offsets_hbm, stiffness_hbm, basis_hbm, transfer_hbm, slab_hbm, wire_ref, slots_ref,
+    values_hbm, offsets_hbm, stiffness_hbm, basis_hbm, transfer_hbm, slab_hbm, wire_ref, slots_ref,
     values_ref, offsets_ref, stiffness_ref, basis_ref, transfer_ref, slab_ref, sems,
 ):
     lane = lax.broadcasted_iota(jnp.int32, (RANK, 128), 1)
@@ -120,14 +120,14 @@
     )
     share = jnp.dot(slab_rows, slab_ref[...], precision=EXACT, preferred_element_type=F32)
     share = jnp.concatenate([share, jnp.zeros((8, 128 - RANK), F32)], 1)
-    here = at_ref[0]
+    here = lax.axis_index("along")
     for j in range(8):
         slots_ref[j, :, :LEAF] = jnp.where(j < here, wire_ref[0], wire_ref[LD - 1])
         slots_ref[j, :, LEAF:] = share
 
 
-def tall_kernel(at_ref, came_ref, wire_ref, tall_ref):
-    here = at_ref[0]
+def tall_kernel(came_ref, wire_ref, tall_ref):
+    here = lax.axis_index("along")
     lower = came_ref[jnp.maximum(here - 1, 0), :, :LEAF]
     upper = came_ref[jnp.minimum(here + 1, 7), :, :LEAF]
     tall_ref[0] = jnp.where(here > 0, lower, 0.0)
@@ -165,6 +165,16 @@
     return jnp.concatenate([high, low, high, low], 0).astype(BF16)
 
 
+def pair_kernels(target, points_ref, slot, pairs_ref, place):
+    points = points_ref[pl.ds(slot, 3)].reshape(3 * LEAF, 32)
+    pairs = jnp.exp2(jnp.dot(points, target, preferred_element_type=F32))
+    for step in range(3):
+        pair = pairs[step * LEAF : (step + 1) * LEAF]
+        high = pair.astype(BF16)
+        pairs_ref[place + step, 0] = high
+        pairs_ref[place + step, 1] = (pair - high.astype(F32)).astype(BF16)
+
+
 def pair_kernel(target, points_ref, slot, pairs_ref, place):
     power = jnp.dot(points_ref[slot], target, preferred_element_type=F32)
     pair = jnp.exp2(power)
@@ -200,8 +210,8 @@
         leaves = [g * TURN_OWN + n for n in range(TURN_OWN)]
         places = [(n, step) for n in range(TURN_OWN) for step in (-1, 0, 1)]
         targets = [target_points(wire_ref[l]) for l in leaves]
-        for place, (n, step) in enumerate(places):
-            pair_kernel(targets[n], points_ref, leaves[n] + 1 + step, pairs_ref, place)
+        for n in range(TURN_OWN):
+            pair_kernels(targets[n], points_ref, leaves[n], pairs_ref, 3 * n)
         totals = [jnp.zeros((8, LEAF), F32)] * TURN_OWN
         for place, (n, step) in enumerate(places):
             totals[n] += pair_sum(wire_ref[leaves[n]], loads_ref, leaves[n] + 1 + step, pairs_ref, place, 0, step)
@@ -212,8 +222,8 @@
     lax.fori_loop(0, LD // TURN_OWN, turn, 0)
 
 
-def near_side_kernel(beyond, at_ref, tall_ref, came_ref, near_ref, points_ref, loads_ref, pairs_ref):
-    odd = lax.rem(at_ref[1], 2)
+def near_side_kernel(beyond, tall_ref, came_ref, near_ref, points_ref, loads_ref, pairs_ref):
+    odd = lax.rem(lax.axis_index("blk"), 2)
     around = ((2 * odd - 1) if beyond else (1 - 2 * odd)).astype(F32)
 
     def prepare(l, _):
@@ -228,8 +238,8 @@
         leaves = [g * TURN + n for n in range(TURN)]
         places = [(n, step) for n in range(TURN) for step in (-1, 0, 1)]
         targets = [target_points(tall_ref[l + 1]) for l in leaves]
-        for place, (n, step) in enumerate(places):
-            pair_kernel(targets[n], points_ref, leaves[n] + 1 + step, pairs_ref, place)
+        for n in range(TURN):
+            pair_kernels(targets[n], points_ref, leaves[n], pairs_ref, 3 * n)
         totals = [jnp.zeros((8, LEAF), F32)] * TURN
         for place, (n, step) in enumerate(places):
             slot = leaves[n] + 1 + step
@@ -269,23 +279,23 @@
         records_ref[TALL + n] = rows[8 * n : 8 * n + 8]
 
 
-def beside_kernel(at_ref, came_ref, beside_ref):
-    even = lax.rem(at_ref[1], 2) == 0
+def beside_kernel(came_ref, beside_ref):
+    even = lax.rem(lax.axis_index("blk"), 2) == 0
     first = packed(coefs_of(came_ref))
     second = packed(jnp.concatenate([came_ref[TALL + n] for n in range(ROWS // 8)], 0)[:TALL])
     beside_ref[0] = jnp.where(even, second, first)
     beside_ref[1] = jnp.where(even, first, second)
 
 
-def chip_kernel(at_ref, tall_ref, partner_ref, chip_ref):
-    even = lax.rem(at_ref[1], 2) == 0
+def chip_kernel(tall_ref, partner_ref, chip_ref):
+    even = lax.rem(lax.axis_index("blk"), 2) == 0
     own, partner = packed(coefs_of(tall_ref)), packed(coefs_of(partner_ref))
     chip_ref[0] = jnp.where(even, own, partner)
     chip_ref[1] = jnp.where(even, partner, own)
 
 
-def window_kernel(at_ref, chip_ref, beside_ref, other_ref, window_ref, onward_ref):
-    even = lax.rem(at_ref[1], 2) == 0
+def window_kernel(chip_ref, beside_ref, other_ref, window_ref, onward_ref):
+    even = lax.rem(lax.axis_index("blk"), 2) == 0
     chip, beside, other = ([ref[n] for n in range(2)] for ref in (chip_ref, beside_ref, other_ref))
     low = [jnp.where(even, beside[n], other[n]) for n in range(2)]
     high = [jnp.where(even, other[n], beside[n]) for n in range(2)]
@@ -308,17 +318,19 @@
     return high + (cross + lax.dot_general(xh, yl, BY_LAST, preferred_element_type=F32))
 
 
-def top_kernel(at_ref, admissible_ref, every_ref, top_ref, slab_ref, down_ref):
-    here = at_ref[1]
+def top_kernel(admissible_ref, every_ref, top_ref, slab_ref, down_ref, first_ref, second_ref):
     sectors = top_ref.shape[0]
+    apart = lax.rem(lax.broadcasted_iota(jnp.int32, (8, sectors), 1) - lax.axis_index("blk") + sectors, sectors)
+    distant = jnp.logical_and(apart > REACH, apart < sectors - REACH)
+    allowed = jnp.where(distant, admissible_ref[...], 0).astype(F32)
+    allowed = jnp.transpose(jnp.concatenate([allowed, jnp.zeros((8, 128 - sectors), F32)], 1), (1, 0))[:sectors, :1]
+    first_ref[...] = every_ref[:, 0, :] * allowed
+    second_ref[...] = every_ref[:, 1, :] * allowed
 
     def couple(t, sums):
-        apart = lax.rem(t - here + sectors, sectors)
-        distant = jnp.logical_and(apart > REACH, apart < sectors - REACH)
-        allowed = jnp.where(distant, admissible_ref[0, t], 0).astype(F32)
         coupling = top_ref[t]
-        both = every_ref[t] * allowed
-        rows = (both[0:1, :RANK], both[0:1, RANK:], both[1:2, :RANK])
+        first, second = first_ref[pl.ds(t, 1), :], second_ref[pl.ds(t, 1), :]
+        rows = (first[:, :RANK], first[:, RANK:], second[:, :RANK])
         return tuple(s + coupling * row for s, row in zip(sums, rows))
 
     nothing = jnp.zeros((RANK, RANK), F32)
@@ -331,7 +343,7 @@
     down_ref[...] = exact_by_last(local, slab_ref[...])
 
 
-def finish_kernel(at_ref, mask_ref, *refs):
+def finish_kernel(mask_ref, *refs):
     count = len(refs) - 3
     local, out_ref = refs[:count], refs[count]
     far_ref, ring_ref = refs[count + 1 :]
@@ -339,13 +351,14 @@
     down_ref, transfer_ref, basis_ref, own_ref, side_ref, beyond_ref = local[4:]
     slab = down_ref[...]
 
-    here = at_ref[1]
+    here = lax.axis_index("blk")
     odd = lax.rem(here, 2)
     for n in range(4):
         ring_ref[n] = jnp.where(odd == 0, onward_ref[n], back_ref[n])
         ring_ref[n + 10] = jnp.where(odd == 0, back_ref[n], onward_ref[n])
     for n in range(6):
         ring_ref[n + 4] = window_ref[n]
+    mask = mask_ref[...].astype(F32)
     total = jnp.zeros((3 * ROWS, 3 * RANK), F32)
     for q in range(2 * (REACH - 1)):
         around = q + 2 if q < REACH - 1 else 3 - q
@@ -356,7 +369,7 @@
             [rows[:TALL, :RANK], gap, rows[:TALL, RANK:], gap, third[:, :RANK], third[:, RANK:], gap], 0
         )
         coupling = jnp.concatenate(
-            [coupling_ref[3 * q + b] * mask_ref[0, 3 * q + b].astype(F32) for b in range(3)], 0
+            [coupling_ref[3 * q + b] * mask[:, 3 * q + b : 3 * q + b + 1] for b in range(3)], 0
         )
         total = total + three_by_last(stacked, coupling)
     far = []
@@ -387,8 +400,8 @@
 
 def upward(*args):
     outs = (shaped(LD, 8, LEAF), shaped(8, 8, LEAF + 128))
-    scratch = [pltpu.VMEM(x.shape, F32) for x in args[1:]] + [pltpu.SemaphoreType.DMA((4 + 2 * UP_PARTS,))]
-    return call(upward_kernel, outs, [SMEM] + [HBM] * 6, scratch, flops=10**9, vmem=FULL)(*args)
+    scratch = [pltpu.VMEM(x.shape, F32) for x in args] + [pltpu.SemaphoreType.DMA((4 + 2 * UP_PARTS,))]
+    return call(upward_kernel, outs, [HBM] * 6, scratch, flops=10**9, vmem=FULL)(*args)
 
 
 def near_own(wire):
@@ -399,13 +412,18 @@
 def near_side(beyond, *args):
     kernel = functools.partial(near_side_kernel, beyond)
     scratch = near_scratch(TALL + 1, 3 * TURN)
-    return call(kernel, shaped(LD, 8, LEAF), [SMEM, VMEM, VMEM], scratch, flops=9 * 10**9, bytes=2 * 10**7)(*args)
+    return call(kernel, shaped(LD, 8, LEAF), [VMEM, VMEM], scratch, flops=9 * 10**9, bytes=2 * 10**7)(*args)
 
 
 def finish(*args):
     scratch = [pltpu.VMEM((3, RANK, RANK), F32), pltpu.VMEM((14, PACKED, 128), F32)]
-    ins = [SMEM] * 2 + [VMEM] * (len(args) - 2)
+    ins = [VMEM] * len(args)
     return call(finish_kernel, shaped(RHS, LD, LEAF), ins, scratch, flops=4 * 10**9)(*args)
+
+
+def top(*args):
+    scratch = [pltpu.VMEM((args[2].shape[0], 128), F32)] * 2
+    return call(top_kernel, shaped(8, RANK), [VMEM] * 4, scratch, flops=10**9)(*args)
 
 
 def body(
@@ -420,7 +438,6 @@
     top_coupling,
     top_admissible,
 ):
-    at = jnp.stack([lax.axis_index("along"), lax.axis_index("blk")]).astype(jnp.int32)
     sectors = lax.axis_size("blk")
     values = values[:, 0]
     offsets = offsets[:, 0]
@@ -428,11 +445,11 @@
     transfer = transfer[0]
     slab = slab_transfer_matrices[0, 0]
 
-    wire, slots = upward(at, values, offsets, stiffness[0], basis, transfer, slab)
+    wire, slots = upward(values, offsets, stiffness[0], basis, transfer, slab)
     came = lax.all_to_all(slots, "along", 0, 0, tiled=True)
     own = near_own(wire)
     came, own = lax.optimization_barrier((came, own))
-    tall = call(tall_kernel, shaped(TALL, 8, LEAF), [SMEM, VMEM, VMEM])(at, came, wire)
+    tall = call(tall_kernel, shaped(TALL, 8, LEAF), [VMEM, VMEM])(came, wire)
     tall, came = lax.optimization_barrier((tall, came))
     whole = call(whole_kernel, shaped(sectors, 2, 128), [VMEM])(came)
     flip = [(i, i ^ 1) for i in range(sectors)]
@@ -442,26 +459,26 @@
     records = call(pair_records_kernel, shaped(TALL + ROWS // 8, 8, LEAF), [VMEM] * 2)(tall, partner)
     records, partner = lax.optimization_barrier((records, partner))
     came = lax.ppermute(records, "blk", step_out)
-    side = near_side(False, at, tall, partner)
+    side = near_side(False, tall, partner)
     came, side = lax.optimization_barrier((came, side))
     every = lax.all_to_all(whole, "blk", 0, 0, tiled=True)
-    beside = call(beside_kernel, shaped(2, PACKED, 128), [SMEM, VMEM])(at, came)
+    beside = call(beside_kernel, shaped(2, PACKED, 128), [VMEM])(came)
     other = lax.ppermute(beside, "blk", flip)
     partner, beside = lax.optimization_barrier((partner, beside))
-    chip = call(chip_kernel, shaped(2, PACKED, 128), [SMEM, VMEM, VMEM])(at, tall, partner)
+    chip = call(chip_kernel, shaped(2, PACKED, 128), [VMEM, VMEM])(tall, partner)
     window, onward = call(
-        window_kernel, (shaped(6, PACKED, 128), shaped(4, PACKED, 128)), [SMEM] + [VMEM] * 3
-    )(at, chip, beside, other)
+        window_kernel, (shaped(6, PACKED, 128), shaped(4, PACKED, 128)), [VMEM] * 3
+    )(chip, beside, other)
     onward = lax.ppermute(onward, "blk", stride)
     window, came, every = lax.optimization_barrier((window, came, every))
-    beyond = near_side(True, at, tall, came)
+    beyond = near_side(True, tall, came)
     onward, beyond, every = lax.optimization_barrier((onward, beyond, every))
     back = lax.ppermute(onward, "blk", flip)
-    down = call(top_kernel, shaped(8, RANK), [SMEM] * 2 + [VMEM] * 3, flops=10**9)(
-        at, top_admissible, every, top_coupling[0], slab
+    down = top(
+        top_admissible, every, top_coupling[0], slab
     )
     out = finish(
-        at, leaf_admissible_mask, leaf_coupling_matrices[0], window, onward, back, down,
+        leaf_admissible_mask, leaf_coupling_matrices[0], window, onward, back, down,
         transfer, basis, own, side, beyond,
     )
     return out[:, None]

time: 77.5 us -> 71.9 us (0.928)
  Pallas kernels: 33.5 us -> 27.9 us
    pallas_call x8, Pallas kernels: 23.2 us -> 18.1 us  [the longest x2 13.9 us: near_side(): call(kernel, shaped(LD, 8, LEAF), [VMEM, VMEM], scratch, flops=9 * 10 **...]
  transfers between devices with their start and end apart: 7 -> 7, of which waited for: 1 -> 1; matrix products, arithmetic and copies ran while one was open for 0% -> 0% of each run, Pallas kernels for 33% -> 31%
where the time goes in v7:
time: 71.9 us; the launch traced here: 71.5 us
  starting transfers between devices  41.6 us (58%)
  Pallas kernels  27.9 us (39%)
  local copies, waits for them, and re-layouts  0.98 us (1%)
  waiting for transfers between devices  0.78 us (1%)
    all_to_all x1, starting transfers between devices, body(): every = lax.all_to_all(whole, 'blk', 0, 0, tiled=True)  14.1 us
    pallas_call x2, Pallas kernels, near_side(): call(kernel, shaped(LD, 8, LEAF), [VMEM, VMEM], scratch, flops=9 * 10 **...  13.9 us
    all_to_all x1, starting transfers between devices, body(): came = lax.all_to_all(slots, 'along', 0, 0, tiled=True)  7.49 us
    pallas_call x1, Pallas kernels, near_own(): call(near_own_kernel, shaped(LD, 8, LEAF), [VMEM], scratch, flops=9 * 10...  6.16 us
    ppermute x1, starting transfers between devices, body(): partner = lax.ppermute(tall, 'blk', flip)  5.29 us
    ppermute x1, starting transfers between devices, body(): back = lax.ppermute(onward, 'blk', flip)  4.6 us
    ppermute x1, starting transfers between devices, body(): other = lax.ppermute(beside, 'blk', flip)  4.47 us
    ppermute x1, starting transfers between devices, body(): came = lax.ppermute(records, 'blk', step_out)  3.54 us
  transfers between devices with their start and end apart: 7, of which 1 were waited for; matrix products, arithmetic and copies ran while one was open for 0% of the time, Pallas kernels for 31%

profile of v7, /device:TPU:1, one launch (start us, length us, event | category | flops | bytes accessed | tf_op | source)
XLA Modules:
  0.0 71.5 jit_solution(17005584646284775639)
XLA Ops:
  0.0 3.0 %shard_map.100 = (f32[24,8,256]{2,1,0:T(8,128)}, f32[8,8,384]{2,1,0:T(8,128)}) custom-call(f32[3,24,256]{2,1,0:T(8,128)} %bitcast.19, f32[3,24,256]{2,1,0:T(8,128)} %bitcast.20, f32[24,256]{1,0:T(8,128)} %bitcast.21, f32[24,64,256]{2,1,0:T(8,128)} %bitcast.12, f32[24,64,64]{2,1,0:T(8,128)} %bitcast.15, f32[64,64]{1,0:T(8,128)} %bitcast.17), custom_call_target="tpu_custom_call" | custom-call | flops 1000000000 | bytes 1048576 | tf_op jit(solution)/shard_map/pallas_call | solution.py:404
  3.1 7.5 %all-to-all-start = ((f32[8,8,384]{2,1,0:T(8,128)}), f32[8,8,384]{2,1,0:T(8,128)S(1)}, u32[]{:S(2)}, u32[]{:S(2)}) async-start(f32[8,8,384]{2,1,0:T(8,128)} %get-tuple-element.25), calls=%async_computation | async-start | bytes 196608 | tf_op jit(solution)/shard_map/all_to_all | solution.py:449
  10.5 0.0 copy-start
  10.6 0.9 %copy-done = f32[24,8,256]{2,1,0:T(8,128)S(1)} copy-done((f32[24,8,256]{2,1,0:T(8,128)S(1)}, f32[24,8,256]{2,1,0:T(8,128)}, u32[]{:S(2)}) %copy-start) | copy-done | bytes 196632
  11.5 0.0 copy-start.1
  11.5 6.2 %shard_map.101.refs_7_ = f32[24,8,256]{2,1,0:T(8,128)S(1)} custom-call(f32[24,8,256]{2,1,0:T(8,128)S(1)} %copy-done), custom_call_target="tpu_custom_call" | custom-call | flops 8999999488 | bytes 1048576 | tf_op jit(solution)/shard_map/pallas_call | solution.py:409
  17.6 0.0 all-to-all-done.came_ref
  17.6 0.0 copy-done.1
  17.7 5.3 %collective-permute-start = (f32[26,8,256]{2,1,0:T(8,128)S(1)}, f32[26,8,256]{2,1,0:T(8,128)S(1)}, u32[]{:S(2)}, u32[]{:S(2)}) collective-permute-start(f32[26,8,256]{2,1,0:T(8,128)S(1)} %shard_map.102.tall_ref), channel_id=1, source_target_pairs={{0,8},{8,0},{16,24},{24,16},{32,40},{40,32},{48,56},{56,48},{64,72... | collective-permute-start | bytes 638984 | tf_op jit(solution)/shard_map/ppermute | solution.py:458
  23.0 0.7 %shard_map.108 = f32[64,2,128]{2,1,0:T(2,128)} custom-call(f32[8,8,384]{2,1,0:T(8,128)S(1)} %all-to-all-done.came_ref), custom_call_target="tpu_custom_call" | custom-call | bytes 1048576 | tf_op jit(solution)/shard_map/pallas_call | solution.py:454
  23.7 14.1 %all-to-all-start.1 = ((f32[64,2,128]{2,1,0:T(2,128)}), f32[64,2,128]{2,1,0:T(2,128)S(1)}, u32[]{:S(2)}, u32[]{:S(2)}) async-start(f32[64,2,128]{2,1,0:T(2,128)} %shard_map.108), calls=%async_computation.1 | async-start | bytes 131072 | tf_op jit(solution)/shard_map/all_to_all | solution.py:464
  37.9 0.0 collective-permute-done.partner_ref.came_ref
  37.9 3.5 %collective-permute-start.1 = (f32[30,8,256]{2,1,0:T(8,128)S(1)}, f32[30,8,256]{2,1,0:T(8,128)S(1)}, u32[]{:S(2)}, u32[]{:S(2)}) collective-permute-start(f32[30,8,256]{2,1,0:T(8,128)S(1)} %shard_map.103), channel_id=1, source_target_pairs={{0,504},{8,16},{16,8},{24,32},{32,24},{40,48},{48,40},{56,64},{64,... | collective-permute-start | bytes 737288 | tf_op jit(solution)/shard_map/ppermute | solution.py:461
  41.5 6.9 %shard_map.104.refs_8_ = f32[24,8,256]{2,1,0:T(8,128)S(1)} custom-call(f32[26,8,256]{2,1,0:T(8,128)S(1)} %shard_map.102.tall_ref, f32[26,8,256]{2,1,0:T(8,128)S(1)} %collective-permute-done.partner_ref.came_ref), custom_call_target="tpu_custom_call" | custom-call | flops 8999999488 | bytes 20000000 | tf_op jit(solution)/shard_map/pallas_call | solution.py:415
  48.4 0.0 collective-permute-done.1.came_ref
  48.4 0.1 shard_map.105.beside_ref
  48.5 4.5 %collective-permute-start.2 = (f32[2,40,128]{2,1,0:T(8,128)S(1)}, f32[2,40,128]{2,1,0:T(8,128)S(1)}, u32[]{:S(2)}, u32[]{:S(2)}) collective-permute-start(f32[2,40,128]{2,1,0:T(8,128)S(1)} %shard_map.105.beside_ref), channel_id=1, source_target_pairs={{0,8},{8,0},{16,24},{24,16},{32,40},{40,32},{48,56},{56,48},{64,72... | collective-permute-start | bytes 122888 | tf_op jit(solution)/shard_map/ppermute | solution.py:466
  53.0 0.1 shard_map.106.chip_ref
  53.1 0.8 %collective-permute-done.2.other_ref = f32[2,40,128]{2,1,0:T(8,128)S(1)} collective-permute-done((f32[2,40,128]{2,1,0:T(8,128)S(1)}, f32[2,40,128]{2,1,0:T(8,128)S(1)}, u32[]{:S(2)}, u32[]{:S(2)}) %collective-permute-start.2) | collective-permute-done | bytes 40992 | tf_op jit(solution)/shard_map/ppermute | solution.py:466
  53.8 0.0 all-to-all-done.1.every_ref
  53.8 0.0 copy-start.2
  53.9 0.0 copy-start.6
  53.9 0.0 copy-start.7
  53.9 2.1 %collective-permute-start.3 = (f32[4,40,128]{2,1,0:T(8,128)S(1)}, f32[4,40,128]{2,1,0:T(8,128)S(1)}, u32[]{:S(2)}, u32[]{:S(2)}) collective-permute-start(f32[4,40,128]{2,1,0:T(8,128)S(1)} %get-tuple-element.37), channel_id=1, source_target_pairs={{0,488},{8,32},{16,504},{24,48},{32,8},{40,64},{48,24},{56,80},{64... | collective-permute-start | bytes 245768 | tf_op jit(solution)/shard_map/ppermute | solution.py:472
  55.9 6.9 %shard_map.109.refs_9_ = f32[24,8,256]{2,1,0:T(8,128)S(1)} custom-call(f32[26,8,256]{2,1,0:T(8,128)S(1)} %shard_map.102.tall_ref, f32[30,8,256]{2,1,0:T(8,128)S(1)} %collective-permute-done.1.came_ref), custom_call_target="tpu_custom_call" | custom-call | flops 8999999488 | bytes 20000000 | tf_op jit(solution)/shard_map/pallas_call | solution.py:415
  62.9 0.0 copy-start.3
  62.9 0.0 copy-start.4
  62.9 0.0 copy-start.5
  62.9 0.0 copy-start.8
  62.9 0.0 collective-permute-done.3.refs_2_
  62.9 4.6 %collective-permute-start.4 = (f32[4,40,128]{2,1,0:T(8,128)S(1)}, f32[4,40,128]{2,1,0:T(8,128)S(1)}, u32[]{:S(2)}, u32[]{:S(2)}) collective-permute-start(f32[4,40,128]{2,1,0:T(8,128)S(1)} %collective-permute-done.3.refs_2_), channel_id=1, source_target_pairs={{0,8},{8,0},{16,24},{24,16},{32,40},{40,32},{48,56},{56,48},{64,72... | collective-permute-start | bytes 245768 | tf_op jit(solution)/shard_map/ppermute | solution.py:476
  67.5 0.0 copy-done.2
  67.5 0.0 copy-done.6
  67.6 0.0 copy-done.7
  67.6 0.9 %shard_map.110.refs_4_ = f32[8,64]{1,0:T(8,128)S(1)} custom-call(s32[1,64]{1,0:T(1,128)S(1)} %copy-done.7, f32[64,2,128]{2,1,0:T(2,128)S(1)} %all-to-all-done.1.every_ref, f32[64,64,64]{2,1,0:T(8,128)S(1)} %bitcast.11, f32[64,64]{1,0:T(8,128)S(1)} %bitcast.18), custom_call_target="tpu_custom_call" | custom-call | flops 1000000000 | bytes 1048576 | tf_op jit(solution)/shard_map/pallas_call | solution.py:426
  68.5 0.0 collective-permute-done.4.refs_3_
  68.5 0.0 copy-done.3
  68.5 0.0 copy-done.4
  68.5 0.0 copy-done.5
  68.5 0.0 copy-done.8
  68.5 2.9 %shard_map.111 = f32[3,24,256]{2,1,0:T(8,128)} custom-call(s32[1,30]{1,0:T(1,128)S(1)} %copy-done.8, f32[30,64,64]{2,1,0:T(8,128)S(1)} %bitcast.14, f32[6,40,128]{2,1,0:T(8,128)S(1)} %get-tuple-element.36.refs_1_, f32[4,40,128]{2,1,0:T(8,128)S(1)} %collective-permute-done.3.refs_2_, f32[4,40,128]{2,1,0:T(8,128)S(1)} %collective-permute-done.4.refs_3_, ...), custom_call_target="tpu_custom_call" | custom-call | flops 4000000000 | bytes 1048576 | tf_op jit(solution)/shard_map/pallas_call | solution.py:421
  (3 shorter events, 0.1 us)
Async XLA Ops:
  3.1 14.6 %all-to-all-start = ((f32[8,8,384]{2,1,0:T(8,128)}), f32[8,8,384]{2,1,0:T(8,128)S(1)}, u32[]{:S(2)}, u32[]{:S(2)}) async-start(f32[8,8,384]{2,1,0:T(8,128)} %get-tuple-element.25), calls=%async_computation | async-start | bytes 196608 | tf_op jit(solution)/shard_map/all_to_all | solution.py:449
  10.5 0.9 %copy-start = (f32[24,8,256]{2,1,0:T(8,128)S(1)}, f32[24,8,256]{2,1,0:T(8,128)}, u32[]{:S(2)}) copy-start(f32[24,8,256]{2,1,0:T(8,128)} %get-tuple-element.26.wire_ref) | copy-start | bytes 589828
  11.5 6.2 %copy-start.1 = (f32[24,8,256]{2,1,0:T(8,128)S(1)}, f32[24,8,256]{2,1,0:T(8,128)}, u32[]{:S(2)}) copy-start(f32[24,8,256]{2,1,0:T(8,128)} %get-tuple-element.26.wire_ref) | copy-start | bytes 589828
  17.7 20.2 %collective-permute-start = (f32[26,8,256]{2,1,0:T(8,128)S(1)}, f32[26,8,256]{2,1,0:T(8,128)S(1)}, u32[]{:S(2)}, u32[]{:S(2)}) collective-permute-start(f32[26,8,256]{2,1,0:T(8,128)S(1)} %shard_map.102.tall_ref), channel_id=1, source_target_pairs={{0,8},{8,0},{16,24},{24,16},{32,40},{40,32},{48,56},{56,48},{64,72... | collective-permute-start | bytes 638984 | tf_op jit(solution)/shard_map/ppermute | solution.py:458
  23.7 30.1 %all-to-all-start.1 = ((f32[64,2,128]{2,1,0:T(2,128)}), f32[64,2,128]{2,1,0:T(2,128)S(1)}, u32[]{:S(2)}, u32[]{:S(2)}) async-start(f32[64,2,128]{2,1,0:T(2,128)} %shard_map.108), calls=%async_computation.1 | async-start | bytes 131072 | tf_op jit(solution)/shard_map/all_to_all | solution.py:464
  37.9 10.5 %collective-permute-start.1 = (f32[30,8,256]{2,1,0:T(8,128)S(1)}, f32[30,8,256]{2,1,0:T(8,128)S(1)}, u32[]{:S(2)}, u32[]{:S(2)}) collective-permute-start(f32[30,8,256]{2,1,0:T(8,128)S(1)} %shard_map.103), channel_id=1, source_target_pairs={{0,504},{8,16},{16,8},{24,32},{32,24},{40,48},{48,40},{56,64},{64,... | collective-permute-start | bytes 737288 | tf_op jit(solution)/shard_map/ppermute | solution.py:461
  48.5 5.3 %collective-permute-start.2 = (f32[2,40,128]{2,1,0:T(8,128)S(1)}, f32[2,40,128]{2,1,0:T(8,128)S(1)}, u32[]{:S(2)}, u32[]{:S(2)}) collective-permute-start(f32[2,40,128]{2,1,0:T(8,128)S(1)} %shard_map.105.beside_ref), channel_id=1, source_target_pairs={{0,8},{8,0},{16,24},{24,16},{32,40},{40,32},{48,56},{56,48},{64,72... | collective-permute-start | bytes 122888 | tf_op jit(solution)/shard_map/ppermute | solution.py:466
  53.8 13.7 %copy-start.2 = (f32[1,64,64,64]{3,2,1,0:T(8,128)S(1)}, f32[1,64,64,64]{3,2,1,0:T(8,128)}, u32[]{:S(2)}) copy-start(f32[1,64,64,64]{3,2,1,0:T(8,128)} %param.18) | copy-start | bytes 3145732
  53.9 13.7 %copy-start.6 = (f32[1,1,64,64]{3,2,1,0:T(8,128)S(1)}, f32[1,1,64,64]{3,2,1,0:T(8,128)}, u32[]{:S(2)}) copy-start(f32[1,1,64,64]{3,2,1,0:T(8,128)} %param.15) | copy-start | bytes 49156
  53.9 13.7 %copy-start.7 = (s32[1,64]{1,0:T(1,128)S(1)}, s32[1,64]{1,0:T(1,128)}, u32[]{:S(2)}) copy-start(s32[1,64]{1,0:T(1,128)} %admissible_ref.1) | copy-start | bytes 772
  53.9 9.0 %collective-permute-start.3 = (f32[4,40,128]{2,1,0:T(8,128)S(1)}, f32[4,40,128]{2,1,0:T(8,128)S(1)}, u32[]{:S(2)}, u32[]{:S(2)}) collective-permute-start(f32[4,40,128]{2,1,0:T(8,128)S(1)} %get-tuple-element.37), channel_id=1, source_target_pairs={{0,488},{8,32},{16,504},{24,48},{32,8},{40,64},{48,24},{56,80},{64... | collective-permute-start | bytes 245768 | tf_op jit(solution)/shard_map/ppermute | solution.py:472
  62.9 5.6 %copy-start.3 = (f32[1,24,64,256]{3,2,1,0:T(8,128)S(1)}, f32[1,24,64,256]{3,2,1,0:T(8,128)}, u32[]{:S(2)}) copy-start(f32[1,24,64,256]{3,2,1,0:T(8,128)} %param.13) | copy-start | bytes 4718596
  62.9 5.6 %copy-start.4 = (f32[1,30,64,64]{3,2,1,0:T(8,128)S(1)}, f32[1,30,64,64]{3,2,1,0:T(8,128)}, u32[]{:S(2)}) copy-start(f32[1,30,64,64]{3,2,1,0:T(8,128)} %param.16) | copy-start | bytes 1474564
  62.9 5.6 %copy-start.5 = (f32[1,24,64,64]{3,2,1,0:T(8,128)S(1)}, f32[1,24,64,64]{3,2,1,0:T(8,128)}, u32[]{:S(2)}) copy-start(f32[1,24,64,64]{3,2,1,0:T(8,128)} %param.14) | copy-start | bytes 1179652
  62.9 5.6 %copy-start.8 = (s32[1,30]{1,0:T(1,128)S(1)}, s32[1,30]{1,0:T(1,128)}, u32[]{:S(2)}) copy-start(s32[1,30]{1,0:T(1,128)} %mask_ref.1) | copy-start | bytes 364
  62.9 5.6 %collective-permute-start.4 = (f32[4,40,128]{2,1,0:T(8,128)S(1)}, f32[4,40,128]{2,1,0:T(8,128)S(1)}, u32[]{:S(2)}, u32[]{:S(2)}) collective-permute-start(f32[4,40,128]{2,1,0:T(8,128)S(1)} %collective-permute-done.3.refs_2_), channel_id=1, source_target_pairs={{0,8},{8,0},{16,24},{24,16},{32,40},{40,32},{48,56},{56,48},{64,72... | collective-permute-start | bytes 245768 | tf_op jit(solution)/shard_map/ppermute | solution.py:476

commit v8 on v7

--- a/solution.py
+++ b/solution.py
@@ -279,31 +279,23 @@
         records_ref[TALL + n] = rows[8 * n : 8 * n + 8]
 
 
-def beside_kernel(came_ref, beside_ref):
-    even = lax.rem(lax.axis_index("blk"), 2) == 0
+def is_even():
+    return lax.rem(lax.axis_index("blk"), 2) == 0
+
+
+def quad_kernel(tall_ref, partner_ref, came_ref, quad_ref):
+    own, partner = packed(coefs_of(tall_ref)), packed(coefs_of(partner_ref))
     first = packed(coefs_of(came_ref))
     second = packed(jnp.concatenate([came_ref[TALL + n] for n in range(ROWS // 8)], 0)[:TALL])
-    beside_ref[0] = jnp.where(even, second, first)
-    beside_ref[1] = jnp.where(even, first, second)
-
-
-def chip_kernel(tall_ref, partner_ref, chip_ref):
-    even = lax.rem(lax.axis_index("blk"), 2) == 0
-    own, partner = packed(coefs_of(tall_ref)), packed(coefs_of(partner_ref))
-    chip_ref[0] = jnp.where(even, own, partner)
-    chip_ref[1] = jnp.where(even, partner, own)
-
-
-def window_kernel(chip_ref, beside_ref, other_ref, window_ref, onward_ref):
-    even = lax.rem(lax.axis_index("blk"), 2) == 0
-    chip, beside, other = ([ref[n] for n in range(2)] for ref in (chip_ref, beside_ref, other_ref))
-    low = [jnp.where(even, beside[n], other[n]) for n in range(2)]
-    high = [jnp.where(even, other[n], beside[n]) for n in range(2)]
-    window = low + chip + high
+    for n, (if_even, if_odd) in enumerate(((second, partner), (first, own), (own, first), (partner, second))):
+        quad_ref[n] = jnp.where(is_even(), if_even, if_odd)
+
+
+def outer_kernel(quad_ref, onward_ref, outer_ref):
     for n in range(6):
-        window_ref[n] = window[n]
-    for n in range(4):
-        onward_ref[n] = jnp.where(even, window[n + 2], window[n])
+        if_even = onward_ref[n] if n < 4 else quad_ref[n - 4]
+        if_odd = quad_ref[n + 2] if n < 2 else onward_ref[n - 2]
+        outer_ref[n] = jnp.where(is_even(), if_even, if_odd)
 
 
 def exact_by_last(x, y):
@@ -347,17 +339,17 @@
     count = len(refs) - 3
     local, out_ref = refs[:count], refs[count]
     far_ref, ring_ref = refs[count + 1 :]
-    coupling_ref, window_ref, onward_ref, back_ref = local[:4]
+    coupling_ref, quad_ref, outer_ref, other_ref = local[:4]
     down_ref, transfer_ref, basis_ref, own_ref, side_ref, beyond_ref = local[4:]
     slab = down_ref[...]
 
     here = lax.axis_index("blk")
     odd = lax.rem(here, 2)
-    for n in range(4):
-        ring_ref[n] = jnp.where(odd == 0, onward_ref[n], back_ref[n])
-        ring_ref[n + 10] = jnp.where(odd == 0, back_ref[n], onward_ref[n])
     for n in range(6):
-        ring_ref[n + 4] = window_ref[n]
+        ring_ref[n] = jnp.where(odd == 0, outer_ref[n], other_ref[n])
+        ring_ref[n + 8] = jnp.where(odd == 0, other_ref[n], outer_ref[n])
+    for n in range(2):
+        ring_ref[n + 6] = jnp.where(odd == 0, quad_ref[n + 2], quad_ref[n])
     mask = mask_ref[...].astype(F32)
     total = jnp.zeros((3 * ROWS, 3 * RANK), F32)
     for q in range(2 * (REACH - 1)):
@@ -454,7 +446,7 @@
     whole = call(whole_kernel, shaped(sectors, 2, 128), [VMEM])(came)
     flip = [(i, i ^ 1) for i in range(sectors)]
     step_out = [(i, (i + 1 if i % 2 else i - 1) % sectors) for i in range(sectors)]
-    stride = [(i, (i + 3 if i % 2 else i - 3) % sectors) for i in range(sectors)]
+    stride = [(i, (i - 4 if i % 2 else i + 4) % sectors) for i in range(sectors)]
     partner = lax.ppermute(tall, "blk", flip)
     records = call(pair_records_kernel, shaped(TALL + ROWS // 8, 8, LEAF), [VMEM] * 2)(tall, partner)
     records, partner = lax.optimization_barrier((records, partner))
@@ -462,23 +454,18 @@
     side = near_side(False, tall, partner)
     came, side = lax.optimization_barrier((came, side))
     every = lax.all_to_all(whole, "blk", 0, 0, tiled=True)
-    beside = call(beside_kernel, shaped(2, PACKED, 128), [VMEM])(came)
-    other = lax.ppermute(beside, "blk", flip)
-    partner, beside = lax.optimization_barrier((partner, beside))
-    chip = call(chip_kernel, shaped(2, PACKED, 128), [VMEM, VMEM])(tall, partner)
-    window, onward = call(
-        window_kernel, (shaped(6, PACKED, 128), shaped(4, PACKED, 128)), [VMEM] * 3
-    )(chip, beside, other)
-    onward = lax.ppermute(onward, "blk", stride)
-    window, came, every = lax.optimization_barrier((window, came, every))
+    quad = call(quad_kernel, shaped(4, PACKED, 128), [VMEM] * 3)(tall, partner, came)
+    onward = lax.ppermute(quad, "blk", stride)
+    quad, came, every = lax.optimization_barrier((quad, came, every))
     beyond = near_side(True, tall, came)
     onward, beyond, every = lax.optimization_barrier((onward, beyond, every))
-    back = lax.ppermute(onward, "blk", flip)
+    outer = call(outer_kernel, shaped(6, PACKED, 128), [VMEM] * 2)(quad, onward)
+    other = lax.ppermute(outer, "blk", flip)
     down = top(
         top_admissible, every, top_coupling[0], slab
     )
     out = finish(
-        leaf_admissible_mask, leaf_coupling_matrices[0], window, onward, back, down,
+        leaf_admissible_mask, leaf_coupling_matrices[0], quad, outer, other, down,
         transfer, basis, own, side, beyond,
     )
     return out[:, None]

time: 71.9 us -> 68 us (0.946)
  starting transfers between devices: 41.6 us -> 38.3 us
    ppermute x3 -> x2, starting transfers between devices: 11.1 us -> 7.83 us  [the longest x1 5.64 us: body(): onward = lax.ppermute(quad, 'blk', stride)]
  transfers between devices with their start and end apart: 7 -> 6, of which waited for: 1 -> 1; matrix products, arithmetic and copies ran while one was open for 0% -> 0% of each run, Pallas kernels for 31% -> 32%
where the time goes in v8:
time: 68 us; the launch traced here: 67.7 us
  starting transfers between devices  38.3 us (56%)
  Pallas kernels  27.8 us (41%)
  local copies, waits for them, and re-layouts  0.97 us (1%)
    all_to_all x1, starting transfers between devices, body(): every = lax.all_to_all(whole, 'blk', 0, 0, tiled=True)  14.1 us
    pallas_call x2, Pallas kernels, near_side(): call(kernel, shaped(LD, 8, LEAF), [VMEM, VMEM], scratch, flops=9 * 10 **...  13.9 us
    all_to_all x1, starting transfers between devices, body(): came = lax.all_to_all(slots, 'along', 0, 0, tiled=True)  7.49 us
    pallas_call x1, Pallas kernels, near_own(): call(near_own_kernel, shaped(LD, 8, LEAF), [VMEM], scratch, flops=9 * 10...  6.16 us
    ppermute x1, starting transfers between devices, body(): onward = lax.ppermute(quad, 'blk', stride)  5.64 us
    ppermute x1, starting transfers between devices, body(): partner = lax.ppermute(tall, 'blk', flip)  5.29 us
    ppermute x1, starting transfers between devices, body(): came = lax.ppermute(records, 'blk', step_out)  3.54 us
    pallas_call x1, Pallas kernels, upward(): call(upward_kernel, outs, [HBM] * 6, scratch, flops=10 ** 9, vmem=FULL)  3.05 us
  transfers between devices with their start and end apart: 6, of which 1 were waited for; matrix products, arithmetic and copies ran while one was open for 0% of the time, Pallas kernels for 32%

profile of v8, /device:TPU:1, one launch (start us, length us, event | category | flops | bytes accessed | tf_op | source)
XLA Modules:
  0.0 67.7 jit_solution(6495197081203526048)
XLA Ops:
  0.0 3.0 %shard_map.100 = (f32[24,8,256]{2,1,0:T(8,128)}, f32[8,8,384]{2,1,0:T(8,128)}) custom-call(f32[3,24,256]{2,1,0:T(8,128)} %bitcast.19, f32[3,24,256]{2,1,0:T(8,128)} %bitcast.20, f32[24,256]{1,0:T(8,128)} %bitcast.21, f32[24,64,256]{2,1,0:T(8,128)} %bitcast.12, f32[24,64,64]{2,1,0:T(8,128)} %bitcast.15, f32[64,64]{1,0:T(8,128)} %bitcast.17), custom_call_target="tpu_custom_call" | custom-call | flops 1000000000 | bytes 1048576 | tf_op jit(solution)/shard_map/pallas_call | solution.py:396
  3.1 7.5 %all-to-all-start = ((f32[8,8,384]{2,1,0:T(8,128)}), f32[8,8,384]{2,1,0:T(8,128)S(1)}, u32[]{:S(2)}, u32[]{:S(2)}) async-start(f32[8,8,384]{2,1,0:T(8,128)} %get-tuple-element.21), calls=%async_computation | async-start | bytes 196608 | tf_op jit(solution)/shard_map/all_to_all | solution.py:441
  10.5 0.0 copy-start
  10.6 0.9 %copy-done = f32[24,8,256]{2,1,0:T(8,128)S(1)} copy-done((f32[24,8,256]{2,1,0:T(8,128)S(1)}, f32[24,8,256]{2,1,0:T(8,128)}, u32[]{:S(2)}) %copy-start) | copy-done | bytes 196632
  11.5 0.0 copy-start.1
  11.5 6.2 %shard_map.101.refs_7_ = f32[24,8,256]{2,1,0:T(8,128)S(1)} custom-call(f32[24,8,256]{2,1,0:T(8,128)S(1)} %copy-done), custom_call_target="tpu_custom_call" | custom-call | flops 8999999488 | bytes 1048576 | tf_op jit(solution)/shard_map/pallas_call | solution.py:401
  17.6 0.0 all-to-all-done.came_ref
  17.7 0.0 copy-done.1
  17.7 5.3 %collective-permute-start = (f32[26,8,256]{2,1,0:T(8,128)S(1)}, f32[26,8,256]{2,1,0:T(8,128)S(1)}, u32[]{:S(2)}, u32[]{:S(2)}) collective-permute-start(f32[26,8,256]{2,1,0:T(8,128)S(1)} %shard_map.102.tall_ref), channel_id=1, source_target_pairs={{0,8},{8,0},{16,24},{24,16},{32,40},{40,32},{48,56},{56,48},{64,72... | collective-permute-start | bytes 638984 | tf_op jit(solution)/shard_map/ppermute | solution.py:450
  23.0 0.7 %shard_map.106 = f32[64,2,128]{2,1,0:T(2,128)} custom-call(f32[8,8,384]{2,1,0:T(8,128)S(1)} %all-to-all-done.came_ref), custom_call_target="tpu_custom_call" | custom-call | bytes 1048576 | tf_op jit(solution)/shard_map/pallas_call | solution.py:446
  23.7 14.1 %all-to-all-start.1 = ((f32[64,2,128]{2,1,0:T(2,128)}), f32[64,2,128]{2,1,0:T(2,128)S(1)}, u32[]{:S(2)}, u32[]{:S(2)}) async-start(f32[64,2,128]{2,1,0:T(2,128)} %shard_map.106), calls=%async_computation.1 | async-start | bytes 131072 | tf_op jit(solution)/shard_map/all_to_all | solution.py:456
  37.9 0.0 collective-permute-done.partner_ref.came_ref
  37.9 3.5 %collective-permute-start.1 = (f32[30,8,256]{2,1,0:T(8,128)S(1)}, f32[30,8,256]{2,1,0:T(8,128)S(1)}, u32[]{:S(2)}, u32[]{:S(2)}) collective-permute-start(f32[30,8,256]{2,1,0:T(8,128)S(1)} %shard_map.103), channel_id=1, source_target_pairs={{0,504},{8,16},{16,8},{24,32},{32,24},{40,48},{48,40},{56,64},{64,... | collective-permute-start | bytes 737288 | tf_op jit(solution)/shard_map/ppermute | solution.py:453
  41.5 6.9 %shard_map.104.refs_8_ = f32[24,8,256]{2,1,0:T(8,128)S(1)} custom-call(f32[26,8,256]{2,1,0:T(8,128)S(1)} %shard_map.102.tall_ref, f32[26,8,256]{2,1,0:T(8,128)S(1)} %collective-permute-done.partner_ref.came_ref), custom_call_target="tpu_custom_call" | custom-call | flops 8999999488 | bytes 20000000 | tf_op jit(solution)/shard_map/pallas_call | solution.py:407
  48.4 0.0 collective-permute-done.1.came_ref
  48.4 0.1 shard_map.105.quad_ref.refs_1_
  48.5 0.0 copy-start.2
  48.5 0.0 copy-start.6
  48.5 0.0 copy-start.7
  48.5 5.6 %collective-permute-start.2 = (f32[4,40,128]{2,1,0:T(8,128)S(1)}, f32[4,40,128]{2,1,0:T(8,128)S(1)}, u32[]{:S(2)}, u32[]{:S(2)}) collective-permute-start(f32[4,40,128]{2,1,0:T(8,128)S(1)} %shard_map.105.quad_ref.refs_1_), channel_id=1, source_target_pairs={{0,32},{8,488},{16,48},{24,504},{32,64},{40,8},{48,80},{56,24},{64... | collective-permute-start | bytes 245768 | tf_op jit(solution)/shard_map/ppermute | solution.py:458
  54.2 0.0 all-to-all-done.1.every_ref
  54.2 6.9 %shard_map.107.refs_9_ = f32[24,8,256]{2,1,0:T(8,128)S(1)} custom-call(f32[26,8,256]{2,1,0:T(8,128)S(1)} %shard_map.102.tall_ref, f32[30,8,256]{2,1,0:T(8,128)S(1)} %collective-permute-done.1.came_ref), custom_call_target="tpu_custom_call" | custom-call | flops 8999999488 | bytes 20000000 | tf_op jit(solution)/shard_map/pallas_call | solution.py:407
  61.1 0.0 copy-start.3
  61.1 0.0 copy-start.4
  61.2 0.0 copy-start.5
  61.2 0.0 copy-start.8
  61.2 0.0 collective-permute-done.2.onward_ref
  61.2 2.2 %collective-permute-start.3 = (f32[6,40,128]{2,1,0:T(8,128)S(1)}, f32[6,40,128]{2,1,0:T(8,128)S(1)}, u32[]{:S(2)}, u32[]{:S(2)}) collective-permute-start(f32[6,40,128]{2,1,0:T(8,128)S(1)} %shard_map.108.refs_2_), channel_id=1, source_target_pairs={{0,8},{8,0},{16,24},{24,16},{32,40},{40,32},{48,56},{56,48},{64,72... | collective-permute-start | bytes 368648 | tf_op jit(solution)/shard_map/ppermute | solution.py:463
  63.4 0.0 copy-done.2
  63.4 0.0 copy-done.6
  63.4 0.0 copy-done.7
  63.4 0.9 %shard_map.109.refs_4_ = f32[8,64]{1,0:T(8,128)S(1)} custom-call(s32[1,64]{1,0:T(1,128)S(1)} %copy-done.7, f32[64,2,128]{2,1,0:T(2,128)S(1)} %all-to-all-done.1.every_ref, f32[64,64,64]{2,1,0:T(8,128)S(1)} %bitcast.11, f32[64,64]{1,0:T(8,128)S(1)} %bitcast.18), custom_call_target="tpu_custom_call" | custom-call | flops 1000000000 | bytes 1048576 | tf_op jit(solution)/shard_map/pallas_call | solution.py:418
  64.4 0.3 collective-permute-done.3.refs_3_
  64.7 0.0 copy-done.3
  64.7 0.0 copy-done.4
  64.7 0.0 copy-done.5
  64.7 0.0 copy-done.8
  64.7 2.9 %shard_map.110 = f32[3,24,256]{2,1,0:T(8,128)} custom-call(s32[1,30]{1,0:T(1,128)S(1)} %copy-done.8, f32[30,64,64]{2,1,0:T(8,128)S(1)} %bitcast.14, f32[4,40,128]{2,1,0:T(8,128)S(1)} %shard_map.105.quad_ref.refs_1_, f32[6,40,128]{2,1,0:T(8,128)S(1)} %shard_map.108.refs_2_, f32[6,40,128]{2,1,0:T(8,128)S(1)} %collective-permute-done.3.refs_3_, ...), custom_call_target="tpu_custom_call" | custom-call | flops 4000000000 | bytes 1048576 | tf_op jit(solution)/shard_map/pallas_call | solution.py:413
  (3 shorter events, 0.1 us)
Async XLA Ops:
  3.1 14.6 %all-to-all-start = ((f32[8,8,384]{2,1,0:T(8,128)}), f32[8,8,384]{2,1,0:T(8,128)S(1)}, u32[]{:S(2)}, u32[]{:S(2)}) async-start(f32[8,8,384]{2,1,0:T(8,128)} %get-tuple-element.21), calls=%async_computation | async-start | bytes 196608 | tf_op jit(solution)/shard_map/all_to_all | solution.py:441
  10.5 0.9 %copy-start = (f32[24,8,256]{2,1,0:T(8,128)S(1)}, f32[24,8,256]{2,1,0:T(8,128)}, u32[]{:S(2)}) copy-start(f32[24,8,256]{2,1,0:T(8,128)} %get-tuple-element.22.wire_ref) | copy-start | bytes 589828
  11.5 6.2 %copy-start.1 = (f32[24,8,256]{2,1,0:T(8,128)S(1)}, f32[24,8,256]{2,1,0:T(8,128)}, u32[]{:S(2)}) copy-start(f32[24,8,256]{2,1,0:T(8,128)} %get-tuple-element.22.wire_ref) | copy-start | bytes 589828
  17.7 20.2 %collective-permute-start = (f32[26,8,256]{2,1,0:T(8,128)S(1)}, f32[26,8,256]{2,1,0:T(8,128)S(1)}, u32[]{:S(2)}, u32[]{:S(2)}) collective-permute-start(f32[26,8,256]{2,1,0:T(8,128)S(1)} %shard_map.102.tall_ref), channel_id=1, source_target_pairs={{0,8},{8,0},{16,24},{24,16},{32,40},{40,32},{48,56},{56,48},{64,72... | collective-permute-start | bytes 638984 | tf_op jit(solution)/shard_map/ppermute | solution.py:450
  23.7 30.5 %all-to-all-start.1 = ((f32[64,2,128]{2,1,0:T(2,128)}), f32[64,2,128]{2,1,0:T(2,128)S(1)}, u32[]{:S(2)}, u32[]{:S(2)}) async-start(f32[64,2,128]{2,1,0:T(2,128)} %shard_map.106), calls=%async_computation.1 | async-start | bytes 131072 | tf_op jit(solution)/shard_map/all_to_all | solution.py:456
  37.9 10.5 %collective-permute-start.1 = (f32[30,8,256]{2,1,0:T(8,128)S(1)}, f32[30,8,256]{2,1,0:T(8,128)S(1)}, u32[]{:S(2)}, u32[]{:S(2)}) collective-permute-start(f32[30,8,256]{2,1,0:T(8,128)S(1)} %shard_map.103), channel_id=1, source_target_pairs={{0,504},{8,16},{16,8},{24,32},{32,24},{40,48},{48,40},{56,64},{64,... | collective-permute-start | bytes 737288 | tf_op jit(solution)/shard_map/ppermute | solution.py:453
  48.5 14.9 %copy-start.2 = (f32[1,64,64,64]{3,2,1,0:T(8,128)S(1)}, f32[1,64,64,64]{3,2,1,0:T(8,128)}, u32[]{:S(2)}) copy-start(f32[1,64,64,64]{3,2,1,0:T(8,128)} %param.18) | copy-start | bytes 3145732
  48.5 14.9 %copy-start.6 = (f32[1,1,64,64]{3,2,1,0:T(8,128)S(1)}, f32[1,1,64,64]{3,2,1,0:T(8,128)}, u32[]{:S(2)}) copy-start(f32[1,1,64,64]{3,2,1,0:T(8,128)} %param.15) | copy-start | bytes 49156
  48.5 14.9 %copy-start.7 = (s32[1,64]{1,0:T(1,128)S(1)}, s32[1,64]{1,0:T(1,128)}, u32[]{:S(2)}) copy-start(s32[1,64]{1,0:T(1,128)} %admissible_ref.1) | copy-start | bytes 772
  48.5 12.6 %collective-permute-start.2 = (f32[4,40,128]{2,1,0:T(8,128)S(1)}, f32[4,40,128]{2,1,0:T(8,128)S(1)}, u32[]{:S(2)}, u32[]{:S(2)}) collective-permute-start(f32[4,40,128]{2,1,0:T(8,128)S(1)} %shard_map.105.quad_ref.refs_1_), channel_id=1, source_target_pairs={{0,32},{8,488},{16,48},{24,504},{32,64},{40,8},{48,80},{56,24},{64... | collective-permute-start | bytes 245768 | tf_op jit(solution)/shard_map/ppermute | solution.py:458
  61.1 3.6 %copy-start.3 = (f32[1,24,64,256]{3,2,1,0:T(8,128)S(1)}, f32[1,24,64,256]{3,2,1,0:T(8,128)}, u32[]{:S(2)}) copy-start(f32[1,24,64,256]{3,2,1,0:T(8,128)} %param.13) | copy-start | bytes 4718596
  61.1 3.6 %copy-start.4 = (f32[1,30,64,64]{3,2,1,0:T(8,128)S(1)}, f32[1,30,64,64]{3,2,1,0:T(8,128)}, u32[]{:S(2)}) copy-start(f32[1,30,64,64]{3,2,1,0:T(8,128)} %param.16) | copy-start | bytes 1474564
  61.2 3.6 %copy-start.5 = (f32[1,24,64,64]{3,2,1,0:T(8,128)S(1)}, f32[1,24,64,64]{3,2,1,0:T(8,128)}, u32[]{:S(2)}) copy-start(f32[1,24,64,64]{3,2,1,0:T(8,128)} %param.14) | copy-start | bytes 1179652
  61.2 3.6 %copy-start.8 = (s32[1,30]{1,0:T(1,128)S(1)}, s32[1,30]{1,0:T(1,128)}, u32[]{:S(2)}) copy-start(s32[1,30]{1,0:T(1,128)} %mask_ref.1) | copy-start | bytes 364
  61.2 3.5 %collective-permute-start.3 = (f32[6,40,128]{2,1,0:T(8,128)S(1)}, f32[6,40,128]{2,1,0:T(8,128)S(1)}, u32[]{:S(2)}, u32[]{:S(2)}) collective-permute-start(f32[6,40,128]{2,1,0:T(8,128)S(1)} %shard_map.108.refs_2_), channel_id=1, source_target_pairs={{0,8},{8,0},{16,24},{24,16},{32,40},{40,32},{48,56},{56,48},{64,72... | collective-permute-start | bytes 368648 | tf_op jit(solution)/shard_map/ppermute | solution.py:463

commit v9 on v8

--- a/solution.py
+++ b/solution.py
@@ -30,6 +30,8 @@
 FULL = 60 * MIB + 128 * 1024
 TURN_OWN = 6
 TURN = 3
+EARLY = 18
+LATE = LD - EARLY
 UP_PARTS = 4
 UP_LEAVES = LD // UP_PARTS
 
@@ -196,15 +198,13 @@
 
 def near_own_kernel(wire_ref, near_ref, points_ref, loads_ref, pairs_ref):
     points_ref[0] = jnp.zeros((LEAF, 32), BF16)
-    points_ref[LD + 1] = jnp.zeros((LEAF, 32), BF16)
     loads_ref[0] = jnp.zeros((3, 16, LEAF), BF16)
-    loads_ref[LD + 1] = jnp.zeros((3, 16, LEAF), BF16)
 
     def prepare(l, _):
         source_side(wire_ref[l], 0, (-1, 0, 1), l + 1, points_ref, loads_ref)
         return 0
 
-    lax.fori_loop(0, LD, prepare, 0, unroll=12)
+    lax.fori_loop(0, EARLY + 1, prepare, 0, unroll=EARLY + 1)
 
     def turn(g, _):
         leaves = [g * TURN_OWN + n for n in range(TURN_OWN)]
@@ -219,7 +219,8 @@
             near_ref[leaves[n]] = totals[n]
         return 0
 
-    lax.fori_loop(0, LD // TURN_OWN, turn, 0)
+    lax.fori_loop(0, EARLY // TURN_OWN, turn, 0)
+    near_ref[EARLY:] = jnp.zeros((LD - EARLY, 8, LEAF), F32)
 
 
 def near_side_kernel(beyond, tall_ref, came_ref, near_ref, points_ref, loads_ref, pairs_ref):
@@ -231,27 +232,40 @@
         return 0
 
     lax.fori_loop(0, TALL, prepare, 0, unroll=13)
-    end, end_leaf, end_step = (LD + 1, LD - 1, 1) if beyond else (0, 0, -1)
-    source_side(tall_ref[end], 0, (end_step,), TALL, points_ref, loads_ref)
+
+    def add_leaves(leaves, slots, side):
+        count = len(leaves)
+        places = [(n, step) for n in range(count) for step in (-1, 0, 1)]
+        targets = [target_points(tall_ref[l + 1]) for l in leaves]
+        for n in range(count):
+            pair_kernels(targets[n], points_ref, slots[n], pairs_ref, 3 * n)
+        totals = [jnp.zeros((8, LEAF), F32)] * count
+        for place, (n, step) in enumerate(places):
+            slot = slots[n] + 1 + step
+            totals[n] += pair_sum(tall_ref[leaves[n] + 1], loads_ref, slot, pairs_ref, place, side, step)
+        return totals
 
     def turn(g, _):
         leaves = [g * TURN + n for n in range(TURN)]
-        places = [(n, step) for n in range(TURN) for step in (-1, 0, 1)]
-        targets = [target_points(tall_ref[l + 1]) for l in leaves]
-        for n in range(TURN):
-            pair_kernels(targets[n], points_ref, leaves[n], pairs_ref, 3 * n)
-        totals = [jnp.zeros((8, LEAF), F32)] * TURN
-        for place, (n, step) in enumerate(places):
-            slot = leaves[n] + 1 + step
-            totals[n] += pair_sum(tall_ref[leaves[n] + 1], loads_ref, slot, pairs_ref, place, around, step)
-        for n in range(TURN):
-            near_ref[leaves[n]] = totals[n]
+        for l, total in zip(leaves, add_leaves(leaves, leaves, around)):
+            near_ref[l] = total
         return 0
 
     lax.fori_loop(0, LD // TURN, turn, 0)
-    here = tall_ref[end_leaf + 1]
-    pair_kernel(target_points(here), points_ref, TALL, pairs_ref, 0)
-    near_ref[end_leaf] += pair_sum(here, loads_ref, TALL, pairs_ref, 0, 0, end_step)
+    if beyond:
+        return
+    for n in range(LATE + 2):
+        source_side(tall_ref[EARLY + n], 0, (-1, 0, 1), TALL + n, points_ref, loads_ref)
+    for first in range(0, LATE, TURN):
+        leaves = [EARLY + first + n for n in range(TURN)]
+        slots = [TALL + first + n for n in range(TURN)]
+        for l, total in zip(leaves, add_leaves(leaves, slots, 0)):
+            near_ref[l] += total
+    last = TALL + LATE + 2
+    source_side(tall_ref[0], 0, (-1,), last, points_ref, loads_ref)
+    here = tall_ref[1]
+    pair_kernel(target_points(here), points_ref, last, pairs_ref, 0)
+    near_ref[0] += pair_sum(here, loads_ref, last, pairs_ref, 0, 0, -1)
 
 
 def near_scratch(leaves, places):
@@ -403,7 +417,7 @@
 
 def near_side(beyond, *args):
     kernel = functools.partial(near_side_kernel, beyond)
-    scratch = near_scratch(TALL + 1, 3 * TURN)
+    scratch = near_scratch(TALL + LATE + 3, 3 * TURN)
     return call(kernel, shaped(LD, 8, LEAF), [VMEM, VMEM], scratch, flops=9 * 10**9, bytes=2 * 10**7)(*args)
 
 

time: 68 us -> 69.1 us (1.016)
  waiting for transfers between devices: 0.35 us -> 1.48 us
    pallas_call x1, Pallas kernels: 6.16 us -> 4.59 us  [near_own(): call(near_own_kernel, shaped(LD, 8, LEAF), [VMEM], scratch, flops=9 * 10...]
    all_to_all x1, waiting for transfers between devices: 0.01 us -> 1.14 us  [body(): came = lax.all_to_all(slots, 'along', 0, 0, tiled=True)]
    pallas_call x2, Pallas kernels: 13.9 us -> 14.9 us  [near_side(): call(kernel, shaped(LD, 8, LEAF), [VMEM, VMEM], scratch, flops=9 * 10 **...]
  transfers between devices with their start and end apart: 6 -> 6, of which waited for: 1 -> 2; matrix products, arithmetic and copies ran while one was open for 0% -> 0% of each run, Pallas kernels for 32% -> 31%
where the time goes in v9:
time: 69.1 us; the launch traced here: 68.7 us
  starting transfers between devices  38.7 us (56%)
  Pallas kernels  27.3 us (40%)
  waiting for transfers between devices  1.48 us (2%)
  local copies, waits for them, and re-layouts  0.97 us (1%)
    pallas_call x2, Pallas kernels, near_side(): call(kernel, shaped(LD, 8, LEAF), [VMEM, VMEM], scratch, flops=9 * 10 **...  14.9 us
    all_to_all x1, starting transfers between devices, body(): every = lax.all_to_all(whole, 'blk', 0, 0, tiled=True)  14.1 us
    all_to_all x1, starting transfers between devices, body(): came = lax.all_to_all(slots, 'along', 0, 0, tiled=True)  7.49 us
    ppermute x1, starting transfers between devices, body(): partner = lax.ppermute(tall, 'blk', flip)  5.75 us
    ppermute x1, starting transfers between devices, body(): onward = lax.ppermute(quad, 'blk', stride)  5.64 us
    pallas_call x1, Pallas kernels, near_own(): call(near_own_kernel, shaped(LD, 8, LEAF), [VMEM], scratch, flops=9 * 10...  4.59 us
    ppermute x1, starting transfers between devices, body(): came = lax.ppermute(records, 'blk', step_out)  3.54 us
    pallas_call x1, Pallas kernels, upward(): call(upward_kernel, outs, [HBM] * 6, scratch, flops=10 ** 9, vmem=FULL)  3.05 us
  transfers between devices with their start and end apart: 6, of which 2 were waited for; matrix products, arithmetic and copies ran while one was open for 0% of the time, Pallas kernels for 31%

profile of v9, /device:TPU:1, one launch (start us, length us, event | category | flops | bytes accessed | tf_op | source)
XLA Modules:
  0.0 68.7 jit_solution(186134679175251590)
XLA Ops:
  0.0 3.0 %shard_map.100 = (f32[24,8,256]{2,1,0:T(8,128)}, f32[8,8,384]{2,1,0:T(8,128)}) custom-call(f32[3,24,256]{2,1,0:T(8,128)} %bitcast.19, f32[3,24,256]{2,1,0:T(8,128)} %bitcast.20, f32[24,256]{1,0:T(8,128)} %bitcast.21, f32[24,64,256]{2,1,0:T(8,128)} %bitcast.12, f32[24,64,64]{2,1,0:T(8,128)} %bitcast.15, f32[64,64]{1,0:T(8,128)} %bitcast.17), custom_call_target="tpu_custom_call" | custom-call | flops 1000000000 | bytes 1048576 | tf_op jit(solution)/shard_map/pallas_call | solution.py:410
  3.1 7.5 %all-to-all-start = ((f32[8,8,384]{2,1,0:T(8,128)}), f32[8,8,384]{2,1,0:T(8,128)S(1)}, u32[]{:S(2)}, u32[]{:S(2)}) async-start(f32[8,8,384]{2,1,0:T(8,128)} %get-tuple-element.21), calls=%async_computation | async-start | bytes 196608 | tf_op jit(solution)/shard_map/all_to_all | solution.py:455
  10.5 0.0 copy-start
  10.6 0.9 %copy-done = f32[24,8,256]{2,1,0:T(8,128)S(1)} copy-done((f32[24,8,256]{2,1,0:T(8,128)S(1)}, f32[24,8,256]{2,1,0:T(8,128)}, u32[]{:S(2)}) %copy-start) | copy-done | bytes 196632
  11.5 0.0 copy-start.1
  11.5 4.6 %shard_map.101.refs_7_ = f32[24,8,256]{2,1,0:T(8,128)S(1)} custom-call(f32[24,8,256]{2,1,0:T(8,128)S(1)} %copy-done), custom_call_target="tpu_custom_call" | custom-call | flops 8999999488 | bytes 1048576 | tf_op jit(solution)/shard_map/pallas_call | solution.py:415
  16.1 1.1 %all-to-all-done.came_ref = f32[8,8,384]{2,1,0:T(8,128)S(1)} async-done(((f32[8,8,384]{2,1,0:T(8,128)}), f32[8,8,384]{2,1,0:T(8,128)S(1)}, u32[]{:S(2)}, u32[]{:S(2)}) %all-to-all-start) | async-done | bytes 98336 | tf_op jit(solution)/shard_map/all_to_all | solution.py:455
  17.2 0.0 copy-done.1
  17.2 5.7 %collective-permute-start = (f32[26,8,256]{2,1,0:T(8,128)S(1)}, f32[26,8,256]{2,1,0:T(8,128)S(1)}, u32[]{:S(2)}, u32[]{:S(2)}) collective-permute-start(f32[26,8,256]{2,1,0:T(8,128)S(1)} %shard_map.102.tall_ref), channel_id=1, source_target_pairs={{0,8},{8,0},{16,24},{24,16},{32,40},{40,32},{48,56},{56,48},{64,72... | collective-permute-start | bytes 638984 | tf_op jit(solution)/shard_map/ppermute | solution.py:464
  23.0 0.7 %shard_map.106 = f32[64,2,128]{2,1,0:T(2,128)} custom-call(f32[8,8,384]{2,1,0:T(8,128)S(1)} %all-to-all-done.came_ref), custom_call_target="tpu_custom_call" | custom-call | bytes 1048576 | tf_op jit(solution)/shard_map/pallas_call | solution.py:460
  23.7 14.1 %all-to-all-start.1 = ((f32[64,2,128]{2,1,0:T(2,128)}), f32[64,2,128]{2,1,0:T(2,128)S(1)}, u32[]{:S(2)}, u32[]{:S(2)}) async-start(f32[64,2,128]{2,1,0:T(2,128)} %shard_map.106), calls=%async_computation.1 | async-start | bytes 131072 | tf_op jit(solution)/shard_map/all_to_all | solution.py:470
  37.9 0.0 collective-permute-done.partner_ref.came_ref
  37.9 3.5 %collective-permute-start.1 = (f32[30,8,256]{2,1,0:T(8,128)S(1)}, f32[30,8,256]{2,1,0:T(8,128)S(1)}, u32[]{:S(2)}, u32[]{:S(2)}) collective-permute-start(f32[30,8,256]{2,1,0:T(8,128)S(1)} %shard_map.103), channel_id=1, source_target_pairs={{0,504},{8,16},{16,8},{24,32},{32,24},{40,48},{48,40},{56,64},{64,... | collective-permute-start | bytes 737288 | tf_op jit(solution)/shard_map/ppermute | solution.py:467
  41.5 8.4 %shard_map.104.refs_8_ = f32[24,8,256]{2,1,0:T(8,128)S(1)} custom-call(f32[26,8,256]{2,1,0:T(8,128)S(1)} %shard_map.102.tall_ref, f32[26,8,256]{2,1,0:T(8,128)S(1)} %collective-permute-done.partner_ref.came_ref), custom_call_target="tpu_custom_call" | custom-call | flops 8999999488 | bytes 20000000 | tf_op jit(solution)/shard_map/pallas_call | solution.py:421
  49.8 0.0 collective-permute-done.1.came_ref
  49.8 0.1 shard_map.105.quad_ref.refs_1_
  49.9 0.0 copy-start.2
  49.9 0.0 copy-start.6
  49.9 0.0 copy-start.7
  50.0 5.6 %collective-permute-start.2 = (f32[4,40,128]{2,1,0:T(8,128)S(1)}, f32[4,40,128]{2,1,0:T(8,128)S(1)}, u32[]{:S(2)}, u32[]{:S(2)}) collective-permute-start(f32[4,40,128]{2,1,0:T(8,128)S(1)} %shard_map.105.quad_ref.refs_1_), channel_id=1, source_target_pairs={{0,32},{8,488},{16,48},{24,504},{32,64},{40,8},{48,80},{56,24},{64... | collective-permute-start | bytes 245768 | tf_op jit(solution)/shard_map/ppermute | solution.py:472
  55.6 0.0 all-to-all-done.1.every_ref
  55.6 6.6 %shard_map.107.refs_9_ = f32[24,8,256]{2,1,0:T(8,128)S(1)} custom-call(f32[26,8,256]{2,1,0:T(8,128)S(1)} %shard_map.102.tall_ref, f32[30,8,256]{2,1,0:T(8,128)S(1)} %collective-permute-done.1.came_ref), custom_call_target="tpu_custom_call" | custom-call | flops 8999999488 | bytes 20000000 | tf_op jit(solution)/shard_map/pallas_call | solution.py:421
  62.2 0.0 copy-start.3
  62.2 0.0 copy-start.4
  62.2 0.0 copy-start.5
  62.2 0.0 copy-start.8
  62.2 0.0 collective-permute-done.2.onward_ref
  62.3 2.2 %collective-permute-start.3 = (f32[6,40,128]{2,1,0:T(8,128)S(1)}, f32[6,40,128]{2,1,0:T(8,128)S(1)}, u32[]{:S(2)}, u32[]{:S(2)}) collective-permute-start(f32[6,40,128]{2,1,0:T(8,128)S(1)} %shard_map.108.refs_2_), channel_id=1, source_target_pairs={{0,8},{8,0},{16,24},{24,16},{32,40},{40,32},{48,56},{56,48},{64,72... | collective-permute-start | bytes 368648 | tf_op jit(solution)/shard_map/ppermute | solution.py:477
  64.5 0.0 copy-done.2
  64.5 0.0 copy-done.6
  64.5 0.0 copy-done.7
  64.5 0.9 %shard_map.109.refs_4_ = f32[8,64]{1,0:T(8,128)S(1)} custom-call(s32[1,64]{1,0:T(1,128)S(1)} %copy-done.7, f32[64,2,128]{2,1,0:T(2,128)S(1)} %all-to-all-done.1.every_ref, f32[64,64,64]{2,1,0:T(8,128)S(1)} %bitcast.11, f32[64,64]{1,0:T(8,128)S(1)} %bitcast.18), custom_call_target="tpu_custom_call" | custom-call | flops 1000000000 | bytes 1048576 | tf_op jit(solution)/shard_map/pallas_call | solution.py:432
  65.4 0.3 collective-permute-done.3.refs_3_
  65.8 0.0 copy-done.3
  65.8 0.0 copy-done.4
  65.8 0.0 copy-done.5
  65.8 0.0 copy-done.8
  65.8 2.9 %shard_map.110 = f32[3,24,256]{2,1,0:T(8,128)} custom-call(s32[1,30]{1,0:T(1,128)S(1)} %copy-done.8, f32[30,64,64]{2,1,0:T(8,128)S(1)} %bitcast.14, f32[4,40,128]{2,1,0:T(8,128)S(1)} %shard_map.105.quad_ref.refs_1_, f32[6,40,128]{2,1,0:T(8,128)S(1)} %shard_map.108.refs_2_, f32[6,40,128]{2,1,0:T(8,128)S(1)} %collective-permute-done.3.refs_3_, ...), custom_call_target="tpu_custom_call" | custom-call | flops 4000000000 | bytes 1048576 | tf_op jit(solution)/shard_map/pallas_call | solution.py:427
  (3 shorter events, 0.1 us)
Async XLA Ops:
  3.1 14.2 %all-to-all-start = ((f32[8,8,384]{2,1,0:T(8,128)}), f32[8,8,384]{2,1,0:T(8,128)S(1)}, u32[]{:S(2)}, u32[]{:S(2)}) async-start(f32[8,8,384]{2,1,0:T(8,128)} %get-tuple-element.21), calls=%async_computation | async-start | bytes 196608 | tf_op jit(solution)/shard_map/all_to_all | solution.py:455
  10.5 0.9 %copy-start = (f32[24,8,256]{2,1,0:T(8,128)S(1)}, f32[24,8,256]{2,1,0:T(8,128)}, u32[]{:S(2)}) copy-start(f32[24,8,256]{2,1,0:T(8,128)} %get-tuple-element.22.wire_ref) | copy-start | bytes 589828
  11.5 5.7 %copy-start.1 = (f32[24,8,256]{2,1,0:T(8,128)S(1)}, f32[24,8,256]{2,1,0:T(8,128)}, u32[]{:S(2)}) copy-start(f32[24,8,256]{2,1,0:T(8,128)} %get-tuple-element.22.wire_ref) | copy-start | bytes 589828
  17.2 20.6 %collective-permute-start = (f32[26,8,256]{2,1,0:T(8,128)S(1)}, f32[26,8,256]{2,1,0:T(8,128)S(1)}, u32[]{:S(2)}, u32[]{:S(2)}) collective-permute-start(f32[26,8,256]{2,1,0:T(8,128)S(1)} %shard_map.102.tall_ref), channel_id=1, source_target_pairs={{0,8},{8,0},{16,24},{24,16},{32,40},{40,32},{48,56},{56,48},{64,72... | collective-permute-start | bytes 638984 | tf_op jit(solution)/shard_map/ppermute | solution.py:464
  23.7 31.9 %all-to-all-start.1 = ((f32[64,2,128]{2,1,0:T(2,128)}), f32[64,2,128]{2,1,0:T(2,128)S(1)}, u32[]{:S(2)}, u32[]{:S(2)}) async-start(f32[64,2,128]{2,1,0:T(2,128)} %shard_map.106), calls=%async_computation.1 | async-start | bytes 131072 | tf_op jit(solution)/shard_map/all_to_all | solution.py:470
  37.9 11.9 %collective-permute-start.1 = (f32[30,8,256]{2,1,0:T(8,128)S(1)}, f32[30,8,256]{2,1,0:T(8,128)S(1)}, u32[]{:S(2)}, u32[]{:S(2)}) collective-permute-start(f32[30,8,256]{2,1,0:T(8,128)S(1)} %shard_map.103), channel_id=1, source_target_pairs={{0,504},{8,16},{16,8},{24,32},{32,24},{40,48},{48,40},{56,64},{64,... | collective-permute-start | bytes 737288 | tf_op jit(solution)/shard_map/ppermute | solution.py:467
  49.9 14.6 %copy-start.2 = (f32[1,64,64,64]{3,2,1,0:T(8,128)S(1)}, f32[1,64,64,64]{3,2,1,0:T(8,128)}, u32[]{:S(2)}) copy-start(f32[1,64,64,64]{3,2,1,0:T(8,128)} %param.18) | copy-start | bytes 3145732
  49.9 14.6 %copy-start.6 = (f32[1,1,64,64]{3,2,1,0:T(8,128)S(1)}, f32[1,1,64,64]{3,2,1,0:T(8,128)}, u32[]{:S(2)}) copy-start(f32[1,1,64,64]{3,2,1,0:T(8,128)} %param.15) | copy-start | bytes 49156
  49.9 14.6 %copy-start.7 = (s32[1,64]{1,0:T(1,128)S(1)}, s32[1,64]{1,0:T(1,128)}, u32[]{:S(2)}) copy-start(s32[1,64]{1,0:T(1,128)} %admissible_ref.1) | copy-start | bytes 772
  50.0 12.3 %collective-permute-start.2 = (f32[4,40,128]{2,1,0:T(8,128)S(1)}, f32[4,40,128]{2,1,0:T(8,128)S(1)}, u32[]{:S(2)}, u32[]{:S(2)}) collective-permute-start(f32[4,40,128]{2,1,0:T(8,128)S(1)} %shard_map.105.quad_ref.refs_1_), channel_id=1, source_target_pairs={{0,32},{8,488},{16,48},{24,504},{32,64},{40,8},{48,80},{56,24},{64... | collective-permute-start | bytes 245768 | tf_op jit(solution)/shard_map/ppermute | solution.py:472
  62.2 3.6 %copy-start.3 = (f32[1,24,64,256]{3,2,1,0:T(8,128)S(1)}, f32[1,24,64,256]{3,2,1,0:T(8,128)}, u32[]{:S(2)}) copy-start(f32[1,24,64,256]{3,2,1,0:T(8,128)} %param.13) | copy-start | bytes 4718596
  62.2 3.6 %copy-start.4 = (f32[1,30,64,64]{3,2,1,0:T(8,128)S(1)}, f32[1,30,64,64]{3,2,1,0:T(8,128)}, u32[]{:S(2)}) copy-start(f32[1,30,64,64]{3,2,1,0:T(8,128)} %param.16) | copy-start | bytes 1474564
  62.2 3.6 %copy-start.5 = (f32[1,24,64,64]{3,2,1,0:T(8,128)S(1)}, f32[1,24,64,64]{3,2,1,0:T(8,128)}, u32[]{:S(2)}) copy-start(f32[1,24,64,64]{3,2,1,0:T(8,128)} %param.14) | copy-start | bytes 1179652
  62.2 3.6 %copy-start.8 = (s32[1,30]{1,0:T(1,128)S(1)}, s32[1,30]{1,0:T(1,128)}, u32[]{:S(2)}) copy-start(s32[1,30]{1,0:T(1,128)} %mask_ref.1) | copy-start | bytes 364
  62.3 3.5 %collective-permute-start.3 = (f32[6,40,128]{2,1,0:T(8,128)S(1)}, f32[6,40,128]{2,1,0:T(8,128)S(1)}, u32[]{:S(2)}, u32[]{:S(2)}) collective-permute-start(f32[6,40,128]{2,1,0:T(8,128)S(1)} %shard_map.108.refs_2_), channel_id=1, source_target_pairs={{0,8},{8,0},{16,24},{24,16},{32,40},{40,32},{48,56},{56,48},{64,72... | collective-permute-start | bytes 368648 | tf_op jit(solution)/shard_map/ppermute | solution.py:477
